TPU v7x, 256 devices: a whole 4x4x8 slice. The times are simulated.
256 devices in a mesh: member: 64 (over z, y, x_lo), tile: 4 (over x_hi, core).
Axes of the slice: x: 4 (x_hi: 2, x_lo: 2; x = x_hi * 2 + x_lo), y: 4, z: 8, core: 2. Of those that a mesh axis runs over, the one named last changes fastest.
Arguments:
- features: bfloat16 [64, 128, 32, 2048], P('member', None, 'tile')
- residual_state: float32 [64, 4, 32, 2048], P('member', None, 'tile'), may hold values from -6 to 6
- noise: float32 [64, 4, 32, 2048], P('member', None, 'tile'), may hold values from -6 to 6
- regression_mean: float32 [4, 32, 2048], P(None, 'tile', 'member'), may hold values from -6 to 6
- step_index: int32 [1], replicated, may hold values from 9 to 16
- conv_first: bfloat16 [9, 128, 128], replicated, may hold values from -0.1875 to 0.1875
- conv_second: bfloat16 [9, 128, 128], replicated, may hold values from -0.1875 to 0.1875
- head_weight: bfloat16 [4, 128], replicated, may hold values from -0.5 to 0.5
- spread_target: float32 [4], replicated, may hold values from 0.5 to 4
Outputs:
- ensemble_field: float32 [64, 4, 32, 2048], P('member', None, 'tile')
- next_state: float32 [64, 4, 32, 2048], P('member', None, 'tile')
All inputs are finite; a program needn't handle non-finite values.
Results may differ from a plain program's by a relative error of at most 0.0013.
Values may be sent and summed in bfloat16 or wider, within the bound.
No kernel may reach another device: no remote copies, remote signals or barrier semaphores. Data moves between devices by JAX's collectives and lax.ppermute only.
A program may use at most 128 MiB of HBM per device.

v0:
```python
import jax
import jax.numpy as jnp
from jax import lax
from jax.sharding import PartitionSpec as P

GROUPS = 32


def with_halo(cells, sides, width):
    for axis, dim in sides:
        count = lax.axis_size(axis)
        ends = count - 1
        head = lax.slice_in_dim(cells, 0, width, axis=dim)
        tail = lax.slice_in_dim(cells, cells.shape[dim] - width, cells.shape[dim], axis=dim)
        cells = jnp.concatenate(
            [
                lax.ppermute(tail, axis, [(i, (i + 1) % count) for i in range(ends)]),
                cells,
                lax.ppermute(head, axis, [((i + 1) % count, i) for i in range(ends)]),
            ],
            axis=dim,
        )
    return cells


def plan(step_index):
    steps = jnp.arange(18).astype(jnp.float32)
    upper = 800.0 ** (1.0 / 7.0)
    lower = 0.002 ** (1.0 / 7.0)
    sigmas = (upper + steps / 17.0 * (lower - upper)) ** 7
    places = jnp.arange(18)
    sigma = jnp.sum(jnp.where(places == step_index[0], sigmas, 0.0))
    sigma_next = jnp.sum(jnp.where(places == step_index[0] + 1, sigmas, 0.0))
    return (sigma, sigma_next)


def group_norm(block):
    height, width = (block.shape[1], block.shape[2])
    values = block.astype(jnp.float32).reshape(GROUPS, -1, height, width)
    count = values.shape[1] * height * width * lax.axis_size("tile")
    total = lax.psum(jnp.sum(values, axis=(1, 2, 3)), "tile")
    mean = total / count
    centred = values - mean[:, None, None, None]
    var = lax.psum(jnp.sum(centred * centred, axis=(1, 2, 3)), "tile") / count
    normed = centred * lax.rsqrt(var + 1e-05)[:, None, None, None]
    return jax.nn.silu(normed).astype(jnp.bfloat16).reshape(block.shape)


def convolve(activ, kernel):
    height, width = (activ.shape[1], activ.shape[2])
    bordered = with_halo(activ, (("tile", 1),), 1)
    padded = jnp.pad(bordered, ((0, 0), (0, 0), (1, 1)))
    stacked = jnp.concatenate(
        [padded[:, :, col_tap : col_tap + width] for col_tap in range(3)], axis=0
    )
    total = jnp.zeros((kernel.shape[1], height, width), jnp.float32)
    for row_tap in range(3):
        weight = jnp.concatenate([kernel[3 * row_tap + col_tap] for col_tap in range(3)], axis=1)
        window = stacked[:, row_tap : row_tap + height, :]
        total = total + jnp.einsum(
            "oc,chw->ohw", weight, window, preferred_element_type=jnp.float32
        )
    return total


def shards(
    features,
    residual_state,
    noise,
    regression_mean,
    step_index,
    conv_first,
    conv_second,
    head_weight,
    spread_target,
):
    sigma, sigma_next = plan(step_index)
    sigma_hat = 1.25 * sigma
    member_features = features[0]
    activ_first = group_norm(member_features)
    hidden_first = convolve(activ_first, conv_first).astype(jnp.bfloat16)
    activ_second = group_norm(hidden_first)
    block_out = (member_features.astype(jnp.float32) + convolve(activ_second, conv_second)).astype(
        jnp.bfloat16
    )
    network = jnp.einsum("oc,chw->ohw", head_weight, block_out, preferred_element_type=jnp.float32)
    state_hat = residual_state[0] + jnp.sqrt(sigma_hat * sigma_hat - sigma * sigma) * noise[0]
    c_skip = 0.25 / (sigma_hat * sigma_hat + 0.25)
    c_out = 0.5 * sigma_hat / jnp.sqrt(sigma_hat * sigma_hat + 0.25)
    denoised = c_skip * state_hat + c_out * network
    advanced = state_hat + (sigma_next - sigma_hat) / sigma_hat * (state_hat - denoised)
    members = features.shape[0] * lax.axis_size("member")
    target = spread_target[:, None, None]
    regional = lax.all_gather(regression_mean, "member", axis=2, tiled=True)
    first, second = lax.psum((advanced, advanced * advanced), "member")
    ens_mean = first / members
    ens_var = second / members - ens_mean * ens_mean
    factor = jnp.sqrt(1.0 + target / (ens_var + 1.0))
    field = regional + ens_mean + (advanced - ens_mean) * factor
    return (field[None], advanced[None])


def solution(mesh):
    return jax.shard_map(
        shards,
        mesh=mesh,
        in_specs=(
            P("member", None, "tile", None),
            P("member", None, "tile", None),
            P("member", None, "tile", None),
            P(None, "tile", "member"),
            P(),
            P(),
            P(),
            P(),
            P(),
        ),
        out_specs=(P("member", None, "tile", None), P("member", None, "tile", None)),
        check_vma=False,
    )
```

profile of v0, /device:TPU:4, one launch (start us, length us, event | category | flops | bytes accessed | tf_op | source)
XLA Modules:
  0.0 816.1 jit_solution(11904481483757699291)
XLA Ops:
  7.2 4.4 convert_reduce_fusion
  11.8 0.1 reduce_sum.69
  11.9 7.2 psum.42
  19.1 0.1 sub.50
  19.2 4.5 fusion.33
  23.7 0.1 reduce_sum.88
  23.8 0.1 reduce_sum.89
  23.9 8.9 %psum.43 = f32[32]{0:T(128)S(1)} all-reduce(f32[32]{0:T(128)S(1)} %reduce_sum.89), channel_id=1, replica_groups=mesh['member'=64,'tile'=4] {'tile'}, use_global_device_ids=true, to_apply=%region_7.8 | all-reduce | flops 32 | bytes 256 | tf_op jit(solution)/shard_map/psum | solution.py:44
  32.9 0.1 mul.131
  33.0 5.4 fusion.30
  38.5 1.9 collective-permute-start
  40.4 5.3 collective-permute-start.1
  45.8 4.7 collective-permute-done
  50.5 1.8 collective-permute-done.1
  52.3 7.2 fusion.38
  59.5 10.9 %fusion.93 = (bf16[128,10,2048]{2,0,1:T(8,128)(2,1)}, bf16[128,10,2048]{2,0,1:T(8,128)(2,1)}) fusion(bf16[128,10,2050]{2,0,1:T(8,128)(2,1)} %fusion.38), kind=kLoop, calls=%fused_computation.128 | loop fusion | bytes 20971520 | tf_op jit(solution)/shard_map/slice | solution.py:54
  70.4 8.0 pad_maximum_fusion
  78.4 5.2 fusion.8
  83.6 2.8 copy-done.1
  86.4 4.6 fusion.10
  91.0 12.9 %convert_reduce_fusion.1 = (f32[128]{0:T(128)S(1)}, bf16[128,8,2048]{2,0,1:T(8,128)(2,1)}) fusion(bf16[384,10,2048]{2,0,1:T(8,128)(2,1)} %copy-done.1, bf16[128,128]{1,0:T(8,128)(2,1)S(1)} %get-tuple-element.36, bf16[128,128]{1,0:T(8,128)(2,1)S(1)} %get-tuple-element.37, bf16[128,128]{1,0:T(8,128)(2,1)S(1)} %get-tuple-element.29, ...), kind=kOutput, calls=%fused_computation.23 | convolution fusion | flops 1621393280 | bytes 33653248 | tf_op jit(solution)/shard_map/oc,chw->ohw/dot_general | solution.py:60
  104.1 0.1 reduce_sum.92
  104.2 10.6 %psum.44 = f32[32]{0:T(128)S(1)} all-reduce(f32[32]{0:T(128)S(1)} %reduce_sum.92), channel_id=1, replica_groups=mesh['member'=64,'tile'=4] {'tile'}, use_global_device_ids=true, to_apply=%region_10.11 | all-reduce | flops 32 | bytes 256 | tf_op jit(solution)/shard_map/psum | solution.py:41
  114.8 0.1 sub.56
  114.9 3.5 fusion.23
  118.4 0.1 reduce_sum.94
  118.5 0.1 reduce_sum.95
  118.6 7.3 psum.45
  126.0 0.1 mul.137
  126.1 4.3 fusion.22
  130.5 1.9 copy-done.3
  132.5 1.9 collective-permute-start.2
  134.4 5.4 collective-permute-start.3
  140.4 0.6 fusion.81
  143.1 0.6 fusion.82
  145.1 1.1 collective-permute-done.3
  146.2 6.7 select_maximum_fusion
  153.0 10.9 %fusion.92 = (bf16[128,10,2048]{2,0,1:T(8,128)(2,1)}, bf16[128,10,2048]{2,0,1:T(8,128)(2,1)}) fusion(bf16[128,10,2050]{2,0,1:T(8,128)(2,1)} %select_maximum_fusion), kind=kLoop, calls=%fused_computation.127 | loop fusion | bytes 20971520 | tf_op jit(solution)/shard_map/slice | solution.py:54
  163.8 8.0 pad_maximum_fusion.1
  171.9 5.2 fusion.2
  177.0 2.8 copy-done.2
  179.9 4.6 fusion
  184.5 14.8 %fusion.39 = f32[8,2048,4]{1,2,0:T(4,128)S(1)} fusion(f32[128,8,2048]{2,0,1:T(8,128)} %fusion, f32[128,8,2048]{2,0,1:T(8,128)} %fusion.2, bf16[1,128,8,2048]{3,2,1,0:T(8,128)(2,1)} %param.9, bf16[384,10,2048]{2,0,1:T(8,128)(2,1)} %copy-done.2, bf16[128,128]{1,0:T(8,128)(2,1)S(1)} %get-tuple-element.25, bf16[128,128]{1,0:T(8,128)(2,1)S(1)} %get-tuple-element.26, ...), kind=kOutput, calls=%fused_computation.51 | convolution fusion | flops 1638170624 | bytes 33915904 | tf_op jit(solution)/shard_map/oc,chw->ohw/dot_general | solution.py:86
  199.3 1.0 fusion.90
  200.4 195.0 %all_gather.3 = f32[4,8,2048]{1,0,2:T(4,128)} all-gather(f32[4,8,32]{1,0,2:T(4,128)S(1)} %copy.30), channel_id=1, replica_groups=mesh['member'=64,'tile'=4] {'member'}, dimensions={2}, use_global_device_ids=true | all-gather | bytes 266240 | tf_op jit(solution)/shard_map/all_gather | solution.py:94
  395.4 3.5 copy.33
  398.9 408.4 %all-reduce.5.cloned.1.call-done = (f32[4,8,2048]{2,1,0:T(8,128)}, f32[4,8,2048]{2,1,0:T(8,128)}) async-done(((f32[4,8,2048]{2,1,0:T(8,128)}, f32[4,8,2048]{2,1,0:T(8,128)}), (f32[4,8,2048]{2,1,0:T(8,128)}, f32[4,8,2048]{2,1,0:T(8,128)})) %all-reduce.5.cloned.1.call-update) | async-done | bytes 524304 | tf_op jit(solution)/shard_map/psum | solution.py:95
  807.3 1.9 add_bitcast_fusion
  (39 shorter events, 0.9 us)
Async XLA Ops:
  7.2 177.3 %copy-start = (bf16[4,128]{1,0:T(4,128)(2,1)S(1)}, bf16[4,128]{1,0:T(4,128)(2,1)}, u32[]{:S(2)}) copy-start(bf16[4,128]{1,0:T(4,128)(2,1)} %param.16) | copy-start | bytes 3076
  7.2 800.1 %all-reduce.5.cloned.1.call-start = ((), (), s32[]{:S(2)}) async-start(), calls=%async_computation | async-start | bytes 1048576 | tf_op jit(solution)/shard_map/psum | solution.py:95
  11.7 34.1 %copy-start.6 = (bf16[9,128,128]{2,1,0:T(8,128)(2,1)S(1)}, bf16[9,128,128]{2,1,0:T(8,128)(2,1)}, u32[]{:S(2)}) copy-start(bf16[9,128,128]{2,1,0:T(8,128)(2,1)} %param.14) | copy-start | bytes 884740
  38.4 13.9 %copy-start.4 = (bf16[128,8,2048]{2,0,1:T(8,128)(2,1)}, bf16[128,8,2048]{2,0,1:T(8,128)(2,1)S(1)}, u32[]{:S(2)}) copy-start(bf16[128,8,2048]{2,0,1:T(8,128)(2,1)S(1)} %fusion.30) | copy-start | bytes 12582916
  38.5 12.0 %collective-permute-start = (bf16[128,1,2048]{2,0,1:T(8,128)(2,1)S(1)}, bf16[128,1,2048]{2,0,1:T(8,128)(2,1)S(1)}, u32[]{:S(2)}, u32[]{:S(2)}) collective-permute-start(bf16[128,1,2048]{2,0,1:T(8,128)(2,1)S(1)} %get-tuple-element.18), channel_id=1, source_target_pairs={{0,1},{1,2},{2,3},{4,5},{5,6},{6,7},{8,9},{9,10},{10,11},{12,13},{... | collective-permute-start | bytes 1572872 | tf_op jit(solution)/shard_map/ppermute | solution.py:17
  40.4 11.8 %collective-permute-start.1 = (bf16[128,1,2048]{2,0,1:T(8,128)(2,1)S(1)}, bf16[128,1,2048]{2,0,1:T(8,128)(2,1)S(1)}, u32[]{:S(2)}, u32[]{:S(2)}) collective-permute-start(bf16[128,1,2048]{2,0,1:T(8,128)(2,1)S(1)} %get-tuple-element.19), channel_id=1, source_target_pairs={{1,0},{2,1},{3,2},{5,4},{6,5},{7,6},{9,8},{10,9},{11,10},{13,12},{... | collective-permute-start | bytes 1572872 | tf_op jit(solution)/shard_map/ppermute | solution.py:19
  78.4 8.0 copy-start.1
  104.0 41.1 %copy-start.7 = (bf16[9,128,128]{2,1,0:T(8,128)(2,1)S(1)}, bf16[9,128,128]{2,1,0:T(8,128)(2,1)}, u32[]{:S(2)}) copy-start(bf16[9,128,128]{2,1,0:T(8,128)(2,1)} %param.15) | copy-start | bytes 884740
  130.4 2.0 copy-start.3
  132.5 12.6 %collective-permute-start.2 = (bf16[128,1,2048]{2,0,1:T(8,128)(2,1)S(1)}, bf16[128,1,2048]{2,0,1:T(8,128)(2,1)S(1)}, u32[]{:S(2)}, u32[]{:S(2)}) collective-permute-start(bf16[128,1,2048]{2,0,1:T(8,128)(2,1)S(1)} %get-tuple-element.16), channel_id=1, source_target_pairs={{0,1},{1,2},{2,3},{4,5},{5,6},{6,7},{8,9},{9,10},{10,11},{12,13},{... | collective-permute-start | bytes 1572872 | tf_op jit(solution)/shard_map/ppermute | solution.py:17
  134.4 11.8 %collective-permute-start.3 = (bf16[128,1,2048]{2,0,1:T(8,128)(2,1)S(1)}, bf16[128,1,2048]{2,0,1:T(8,128)(2,1)S(1)}, u32[]{:S(2)}, u32[]{:S(2)}) collective-permute-start(bf16[128,1,2048]{2,0,1:T(8,128)(2,1)S(1)} %get-tuple-element.17), channel_id=1, source_target_pairs={{1,0},{2,1},{3,2},{5,4},{6,5},{7,6},{9,8},{10,9},{11,10},{13,12},{... | collective-permute-start | bytes 1572872 | tf_op jit(solution)/shard_map/ppermute | solution.py:19
  171.9 8.0 copy-start.2
  184.5 14.8 %copy-start.8 = (f32[1,4,8,2048]{3,2,1,0:T(8,128)S(1)}, f32[1,4,8,2048]{3,2,1,0:T(8,128)}, u32[]{:S(2)}) copy-start(f32[1,4,8,2048]{3,2,1,0:T(8,128)} %param.10) | copy-start | bytes 786436
  184.5 14.8 %copy-start.9 = (f32[1,4,8,2048]{3,2,1,0:T(8,128)S(1)}, f32[1,4,8,2048]{3,2,1,0:T(8,128)}, u32[]{:S(2)}) copy-start(f32[1,4,8,2048]{3,2,1,0:T(8,128)} %param.11) | copy-start | bytes 786436
  184.5 15.8 %copy-start.10 = (f32[4,8,32]{2,1,0:T(8,128)S(1)}, f32[4,8,32]{2,1,0:T(8,128)}, u32[]{:S(2)}) copy-start(f32[4,8,32]{2,1,0:T(8,128)} %param.12) | copy-start | bytes 12292
  199.3 608.0 %copy-start.11 = (f32[4]{0:T(128)S(1)}, f32[4]{0:T(128)}, u32[]{:S(2)}) copy-start(f32[4]{0:T(128)} %param.17) | copy-start | bytes 52
  200.3 607.0 %copy-start.5 = (f32[4,8,2048]{2,1,0:T(8,128)S(1)}, f32[4,8,2048]{2,1,0:T(8,128)}, u32[]{:S(2)}) copy-start(f32[4,8,2048]{2,1,0:T(8,128)} %get-tuple-element.11) | copy-start | bytes 786436
Sparse Core Ops, SparseCore 0:
  200.5 606.7 all-reduce.4
where the time goes:
time: 817 us; the launch traced here: 816 us
  waiting for transfers between devices  416 us (51%)
  blocking collectives  229 us (28%)
  other arithmetic  56.8 us (7%)
  matrix products  47.3 us (6%)
  local copies, waits for them, and re-layouts  34.2 us (4%)
  between operations  18.4 us (2%)
  starting transfers between devices  14.6 us (2%)
    psum x1, waiting for transfers between devices, shards(): first, second = lax.psum((advanced, advanced * advanced), 'member')  408 us
    all_gather x1, blocking collectives, shards(): regional = lax.all_gather(regression_mean, 'member', axis=2, tiled=True)  195 us
    dot_general x5, matrix products, convolve(): jnp.einsum('oc,chw->ohw', weight, window, preferred_element_type=jnp.floa...  32.5 us
    slice x2, local copies, waits for them, and re-layouts, convolve(): padded[:, :, col_tap:col_tap + width]  21.7 us
    psum x2, blocking collectives, group_norm(): total = lax.psum(jnp.sum(values, axis=(1, 2, 3)), 'tile')  17.7 us
  transfers between devices with their start and end apart: 5, of which 4 were waited for; matrix products, arithmetic and copies ran while one was open for 1% of the time, Pallas kernels for 0%

commit v1 on v0

v1 whole, which is shorter than its diff:
```python
import functools

import jax
import jax.numpy as jnp
from jax import lax
from jax.experimental import pallas as pl
from jax.experimental.pallas import tpu as pltpu
from jax.sharding import PartitionSpec as P

GROUP = 4
TILES = 4
F32, BF16 = jnp.float32, jnp.bfloat16
VM = pl.BlockSpec(memory_space=pltpu.VMEM)
SM = pl.BlockSpec(memory_space=pltpu.SMEM)
PARAMS = pltpu.CompilerParams(vmem_limit_bytes=56 * 1024 * 1024)


def group_total(row):
    lane = lax.broadcasted_iota(jnp.int32, row.shape, 1)
    size = row.shape[1]
    for step in (1, 2):
        up = pltpu.roll(row, step, 1)
        down = pltpu.roll(row, size - step, 1)
        row = row + jnp.where((lane & step) == 0, down, up)
    return row


def merged(parts, count):
    means = [p[0:1, :] for p in parts]
    devs = [p[1:2, :] for p in parts]
    members = len(parts) * GROUP
    mean = group_total(functools.reduce(jnp.add, means)) / members
    spread = functools.reduce(jnp.add, [(m - mean) * (m - mean) for m in means])
    total = group_total(functools.reduce(jnp.add, devs) + count * spread)
    return mean, lax.rsqrt(total / (members * count) + 1e-05)


def silu(values):
    half = 0.5 * values
    return half + half * jnp.tanh(half)


def row_sum(values):
    return values.reshape(-1, 8, values.shape[1]).sum(0)


def write_stats(st_ref, pivot, first, second, count):
    one = jnp.sum(first, axis=0, keepdims=True)
    two = jnp.sum(second, axis=0, keepdims=True)
    mean = pivot + one / count
    dev = two - one * one / count
    pad = jnp.zeros((6, mean.shape[1]), F32)
    st_ref[...] = jnp.concatenate([mean, dev, pad], axis=0)


def features_kernel(x_ref, head_ref, xt_ref, core_ref, far_ref, hf_ref, st_ref, scr, acc):
    step = pl.program_id(0)
    chans, rows, width = x_ref.shape
    even = (lax.axis_index("tile") & 1) == 0
    for part in range(width // 128):
        at = pl.ds(128 * part, 128)
        scr[part] = x_ref[:, :, at].astype(F32).reshape(chans * rows, 128)
        for r in range(rows):
            nat = scr[part, pl.ds(r, chans, stride=rows), :]
            hf_ref[r, :, at] = jnp.dot(head_ref[...], nat.astype(BF16), preferred_element_type=F32)
            turned = nat.T
            if part == 0 and r == 0:

                @pl.when(step == 0)
                def _():
                    middle = jnp.mean(turned, axis=0, keepdims=True)
                    acc[0] = jnp.broadcast_to(middle, acc.shape[1:])
                    acc[1] = jnp.zeros(acc.shape[1:], F32)
                    acc[2] = jnp.zeros(acc.shape[1:], F32)

                pivot = acc[0, 0:1]
            off = turned - pivot
            acc[1] += row_sum(off)
            acc[2] += row_sum(off * off)
            turned = turned.astype(BF16)
            xt_ref[r, at] = turned
            if r == 0:
                top = turned
        core_ref[at] = jnp.where(even, turned, top)
        far_ref[at] = jnp.where(even, top, turned)

    @pl.when(step == pl.num_programs(0) - 1)
    def _():
        write_stats(st_ref, acc[0, 0:1], acc[1], acc[2], pl.num_programs(0) * rows * width)


def features_call(x, head, block):
    chans, rows, width = x.shape
    edge = jax.ShapeDtypeStruct((width, chans), BF16)
    return pl.pallas_call(
        features_kernel,
        grid=(width // block,),
        out_shape=(
            jax.ShapeDtypeStruct((rows, width, chans), BF16),
            edge,
            edge,
            jax.ShapeDtypeStruct((rows, 8, width), F32),
            jax.ShapeDtypeStruct((8, chans), F32),
        ),
        in_specs=[
            pl.BlockSpec((chans, rows, block), lambda i: (0, 0, i)),
            pl.BlockSpec((8, chans), lambda i: (0, 0)),
        ],
        out_specs=(
            pl.BlockSpec((rows, block, chans), lambda i: (0, i, 0)),
            pl.BlockSpec((block, chans), lambda i: (i, 0)),
            pl.BlockSpec((block, chans), lambda i: (i, 0)),
            pl.BlockSpec((rows, 8, block), lambda i: (0, 0, i)),
            pl.BlockSpec((8, chans), lambda i: (0, 0)),
        ),
        scratch_shapes=[
            pltpu.VMEM((block // 128, chans * rows, 128), F32),
            pltpu.VMEM((3, 8, chans), F32),
        ],
        compiler_params=PARAMS,
        name="features",
    )(x, head)


def weights_kernel(first_ref, second_ref, head_ref, wt_ref, fold_ref):
    chans = first_ref.shape[1]
    wt_ref[...] = jnp.zeros(wt_ref.shape, BF16)
    for tap in range(9):
        turned = first_ref[tap].astype(F32).T.astype(BF16)
        for q in range(2):
            row, col = tap // 3 + q, tap % 3
            wt_ref[pl.ds((3 * row + col) * chans, chans), pl.ds(q * chans, chans)] = turned
    parts = []
    for tap in range(9):
        folded = jnp.dot(head_ref[...], second_ref[tap], preferred_element_type=F32)
        high = folded.astype(BF16).astype(F32)
        parts += [high[0:4], (folded - high)[0:4]]
    fold_ref[...] = jnp.concatenate(parts, axis=0).astype(BF16)


def weights_call(first, second, head):
    chans = first.shape[1]
    return pl.pallas_call(
        weights_kernel,
        out_shape=(
            jax.ShapeDtypeStruct((12 * chans, 2 * chans), BF16),
            jax.ShapeDtypeStruct((72, chans), BF16),
        ),
        in_specs=[VM] * 3,
        out_specs=(VM, VM),
        compiler_params=PARAMS,
        name="weights",
    )(first, second, head)


def first_kernel(
    block, x_ref, core_ref, far_ref, s0, s1, s2, s3, wt_ref, hid_ref, hcore_ref, hfar_ref, st_ref, act, buf
):
    rows, width, chans = x_ref.shape
    tile = lax.axis_index("tile")
    even = (tile & 1) == 0
    inner = ((tile == 1) | (tile == 2)).astype(F32)
    mean, scale = merged([s0[...], s1[...], s2[...], s3[...]], rows * width)
    shift = -mean * scale
    buf[pl.ds(0, 8), :] = jnp.zeros((8, chans), F32)
    buf[pl.ds(width + 8, 8), :] = jnp.zeros((8, chans), F32)
    size = 256

    def put(read, place, factor=None):
        def one(i, _):
            at = pl.multiple_of(i * size, size)
            value = silu(read(at).astype(F32) * scale + shift)
            if factor is not None:
                value = value * factor
            buf[pl.ds(at + 8, size), :] = value
            act[1, place, pl.ds(at, size), :] = value.astype(BF16)
            return 0

        lax.fori_loop(0, width // size, one, 0)

        def two(i, _):
            at = pl.multiple_of(i * size, size)
            act[0, place, pl.ds(at, size), :] = buf[pl.ds(at + 7, size), :].astype(BF16)
            act[2, place, pl.ds(at, size), :] = buf[pl.ds(at + 9, size), :].astype(BF16)
            return 0

        lax.fori_loop(0, width // size, two, 0)

    def own(r, _):
        put(lambda at: x_ref[r, pl.ds(at, size), :], r + 1)
        return 0

    lax.fori_loop(0, rows, own, 0)
    put(lambda at: core_ref[pl.ds(at, size), :], jnp.where(even, rows + 1, 0))
    put(lambda at: far_ref[pl.ds(at, size), :], jnp.where(even, 0, rows + 1), inner)

    per = width // block

    def mm(i, carry):
        pivot, one, two = carry
        pair = i // per
        at = pl.multiple_of((i % per) * block, block)
        left = jnp.concatenate(
            [act[s, 2 * pair + j, pl.ds(at, block), :] for j in range(4) for s in range(3)], axis=1
        )
        out = jnp.dot(left, wt_ref[...], preferred_element_type=F32)
        a, b = out[:, :chans], out[:, chans:]
        hid_ref[2 * pair, pl.ds(at, block), :] = a.astype(BF16)
        hid_ref[2 * pair + 1, pl.ds(at, block), :] = b.astype(BF16)
        pivot = jnp.where(i == 0, jnp.mean(a[0:8], axis=0, keepdims=True), pivot)
        a, b = a - pivot, b - pivot
        return pivot, one + row_sum(a + b), two + row_sum(a * a + b * b)

    zero = jnp.zeros((8, chans), F32)
    pivot, one, two = lax.fori_loop(0, (rows // 2) * per, mm, (zero[0:1], zero, zero))
    write_stats(st_ref, pivot, one, two, rows * width)

    def edges(i, _):
        at = pl.multiple_of(i * size, size)
        top, bottom = hid_ref[0, pl.ds(at, size), :], hid_ref[rows - 1, pl.ds(at, size), :]
        hcore_ref[pl.ds(at, size), :] = jnp.where(even, bottom, top)
        hfar_ref[pl.ds(at, size), :] = jnp.where(even, top, bottom)
        return 0

    lax.fori_loop(0, width // size, edges, 0)


def first_call(xt, core, far, stats, wt, block):
    rows, width, chans = xt.shape
    edge = jax.ShapeDtypeStruct((width, chans), BF16)
    return pl.pallas_call(
        functools.partial(first_kernel, block),
        out_shape=(
            jax.ShapeDtypeStruct(xt.shape, BF16),
            edge,
            edge,
            jax.ShapeDtypeStruct((8, chans), F32),
        ),
        in_specs=[VM] * 8,
        out_specs=(VM,) * 4,
        scratch_shapes=[
            pltpu.VMEM((3, rows + 2, width, chans), BF16),
            pltpu.VMEM((width + 16, chans), F32),
        ],
        compiler_params=PARAMS,
        name="first",
    )(xt, core, far, *stats, wt)


def step_factors(index):
    lane = lax.broadcasted_iota(jnp.int32, (8, 128), 1)
    steps = lane.astype(F32)
    upper = 800.0 ** (1.0 / 7.0)
    lower = 0.002 ** (1.0 / 7.0)
    root = upper + steps / 17.0 * (lower - upper)
    square = root * root
    sigmas = square * square * square * root
    sigma = jnp.sum(jnp.where(lane == index, sigmas, 0.0), axis=1, keepdims=True)
    follow = jnp.sum(jnp.where(lane == index + 1, sigmas, 0.0), axis=1, keepdims=True)
    sigma, follow = jnp.broadcast_to(sigma, lane.shape), jnp.broadcast_to(follow, lane.shape)
    hat = 1.25 * sigma
    spread = hat * hat + 0.25
    skip = 0.25 / spread
    gain = 0.5 * hat / jnp.sqrt(spread)
    rate = (follow - hat) / hat
    keep = 1.0 + rate - rate * skip
    return keep, keep * jnp.sqrt(hat * hat - sigma * sigma), -rate * gain


def second_kernel(
    hid_ref, core_ref, far_ref, s0, s1, s2, s3, fold_ref, hf_ref, state_ref, noise_ref, index_ref,
    next_ref, blocks_ref, act, taps, net,
):
    rows, width, chans = hid_ref.shape
    outs = state_ref.shape[0]
    tile = lax.axis_index("tile")
    even = (tile & 1) == 0
    inner = ((tile == 1) | (tile == 2)).astype(F32)
    mean, scale = merged([s0[...], s1[...], s2[...], s3[...]], rows * width)
    shift = -mean * scale
    size = 256

    def put(read, place, factor=None):
        def one(i, _):
            at = pl.multiple_of(i * size, size)
            value = silu(read(at).astype(F32) * scale + shift)
            if factor is not None:
                value = value * factor
            act[pl.ds(at, size), :] = value.astype(BF16)
            return 0

        lax.fori_loop(0, width // size, one, 0)
        taps[place] = lax.dot_general(
            fold_ref[...], act[...], (((1,), (1,)), ((), ())), preferred_element_type=F32
        )

    def own(r, _):
        put(lambda at: hid_ref[r, pl.ds(at, size), :], r + 1)
        return 0

    lax.fori_loop(0, rows, own, 0)
    put(lambda at: core_ref[pl.ds(at, size), :], jnp.where(even, rows + 1, 0))
    put(lambda at: far_ref[pl.ds(at, size), :], jnp.where(even, 0, rows + 1), inner)

    lane = lax.broadcasted_iota(jnp.int32, (8, width), 1)
    for r in range(rows):
        total = taps[r, 0:24] + taps[r + 1, 24:48] + taps[r + 2, 48:72]
        left = jnp.where(lane == 0, 0.0, pltpu.roll(total[0:8], 1, 1))
        right = jnp.where(lane == width - 1, 0.0, pltpu.roll(total[16:24], width - 1, 1))
        both = left + total[8:16] + right
        both = both[0:4] + both[4:8] + hf_ref[r, 0:4]
        for o in range(outs):
            net[o, r : r + 1, :] = both[o : o + 1]

    keep, stir, push = step_factors(index_ref[0])
    part = width // 16 // outs
    slot = lax.broadcasted_iota(jnp.int32, (rows, 128), 1) // part
    for t in range(width // 128):
        at = pl.ds(t * 128, 128)
        values = []
        for o in range(outs):
            value = keep * state_ref[o, :, at] + stir * noise_ref[o, :, at] + push * net[o, :, at]
            next_ref[o, :, at] = value
            values.append(value)
        for j in range(outs):
            mixed = values[j]
            for o in range(outs):
                if o != j:
                    moved = pltpu.roll(values[o], (part * (o - j)) % 128, 1)
                    mixed = jnp.where(slot == o, moved, mixed)
            blocks_ref[t * outs + j] = mixed


def second_call(hid, core, far, stats, fold, hf, state, noise, index):
    rows, width, chans = hid.shape
    return pl.pallas_call(
        second_kernel,
        out_shape=(
            jax.ShapeDtypeStruct(state.shape, F32),
            jax.ShapeDtypeStruct((width // 32, rows, 128), F32),
        ),
        in_specs=[VM] * 11 + [SM],
        out_specs=(VM, VM),
        scratch_shapes=[
            pltpu.VMEM((width, chans), BF16),
            pltpu.VMEM((rows + 2, 72, width), F32),
            pltpu.VMEM(state.shape, F32),
        ],
        compiler_params=PARAMS,
        name="second",
    )(hid, core, far, *stats, fold, hf, state, noise, index)


def spread_kernel(got_ref, reg_ref, target_ref, out_ref):
    members = got_ref.shape[0]
    zero = jnp.zeros(got_ref.shape[1:], F32)

    def add(m, carry):
        value = got_ref[m]
        return carry[0] + value, carry[1] + value * value

    first, second = lax.fori_loop(0, members, add, (zero, zero), unroll=8)
    slot = lax.broadcasted_iota(jnp.int32, zero.shape, 1) // 32
    target = zero
    for o in range(target_ref.shape[0]):
        target = jnp.where(slot == o, target_ref[o], target)
    mean = first / members
    var = second / members - mean * mean
    scale = jnp.sqrt(1.0 + target / (var + 1.0))
    offset = reg_ref[...] + mean - mean * scale

    def put(m, _):
        out_ref[m, 0] = scale
        out_ref[m, 1] = offset
        return 0

    lax.fori_loop(0, members, put, 0, unroll=8)


def spread_call(got, reg, target):
    members, rows, lanes = got.shape
    return pl.pallas_call(
        spread_kernel,
        out_shape=jax.ShapeDtypeStruct((members, 2, rows, lanes), F32),
        in_specs=[VM, VM, SM],
        out_specs=VM,
        compiler_params=PARAMS,
        name="spread",
    )(got, reg, target)


def field_kernel(blocks_ref, got_ref, out_ref):
    outs, rows, width = out_ref.shape
    part = 128 // outs
    slot = lax.broadcasted_iota(jnp.int32, (rows, 128), 1) // part
    for t in range(width // 128):
        values = [
            blocks_ref[t * outs + j] * got_ref[t * outs + j, 0] + got_ref[t * outs + j, 1]
            for j in range(outs)
        ]
        for o in range(outs):
            mixed = values[o]
            for j in range(outs):
                if j != o:
                    moved = pltpu.roll(values[j], (part * (j - o)) % 128, 1)
                    mixed = jnp.where(slot == j, moved, mixed)
            out_ref[o, :, pl.ds(t * 128, 128)] = mixed


def field_call(blocks, got, shape):
    return pl.pallas_call(
        field_kernel,
        out_shape=jax.ShapeDtypeStruct(shape, F32),
        in_specs=[VM, VM],
        out_specs=VM,
        compiler_params=PARAMS,
        name="field",
    )(blocks, got)


def exchange(core, far, stats):
    swap = lambda bits: [(i, i ^ bits) for i in range(TILES)]
    far = lax.ppermute(far, "tile", [(1, 2), (2, 1)])
    core = lax.ppermute(core, "tile", swap(1))
    return core, far, [stats] + [lax.ppermute(stats, "tile", swap(b)) for b in (1, 2, 3)]


def shards(
    features, residual_state, noise, regression_mean, step_index, conv_first, conv_second, head_weight, spread_target
):
    head = jnp.pad(head_weight, ((0, 8 - head_weight.shape[0]), (0, 0)))
    wt, fold = weights_call(conv_first, conv_second, head)
    xt, core, far, hf, stats = features_call(features[0], head, 256)
    core, far, stats = exchange(core, far, stats)
    hid, core, far, stats = first_call(xt, core, far, stats, wt, 1024)
    core, far, stats = exchange(core, far, stats)
    advanced, blocks = second_call(
        hid, core, far, stats, fold, hf, residual_state[0], noise[0], step_index
    )
    got = lax.all_to_all(blocks, "member", 0, 0, tiled=True)
    reg = jnp.transpose(regression_mean, (1, 0, 2)).reshape(got.shape[1:])
    sent = spread_call(got, reg, spread_target)
    got = lax.all_to_all(sent, "member", 0, 0, tiled=True)
    field = field_call(blocks, got, advanced.shape)
    return (field[None], advanced[None])


def solution(mesh):
    cells = P("member", None, "tile", None)
    return jax.shard_map(
        shards,
        mesh=mesh,
        in_specs=(cells, cells, cells, P(None, "tile", "member"), P(), P(), P(), P(), P()),
        out_specs=(cells, cells),
        check_vma=False,
    )
```

time: 817 us -> 121 us (0.15)
  waiting for transfers between devices: 416 us -> 18.3 us
  blocking collectives: 229 us -> 22.4 us
  other arithmetic: 56.8 us -> 0 us
  matrix products: 47.3 us -> 0 us
  Pallas kernels: 0 us -> 44 us
  local copies, waits for them, and re-layouts: 34.2 us -> 4.56 us
  between operations: 18.4 us -> 1.43 us
  starting transfers between devices: 14.6 us -> 28.9 us
    psum x1 -> x0, waiting for transfers between devices: 408 us -> none  [shards(): first, second = lax.psum((advanced, advanced * advanced), 'member')]
    all_gather x1 -> x0, blocking collectives: 195 us -> none  [shards(): regional = lax.all_gather(regression_mean, 'member', axis=2, tiled=True)]
    dot_general x6 -> x0, matrix products: 47.3 us -> none  [the longest x5 32.5 us: convolve(): jnp.einsum('oc,chw->ohw', weight, window, preferred_element_type=jnp.floa...]
    pallas_call x0 -> x6, Pallas kernels: none -> 44 us  [the longest x1 18.1 us: first_call(): pl.pallas_call(functools.partial(first_kernel, block), out_shape=(jax.Sha...]
    psum x4 -> x0, blocking collectives: 33.9 us -> none  [the longest x2 17.7 us: group_norm(): total = lax.psum(jnp.sum(values, axis=(1, 2, 3)), 'tile')]
    concatenate x4 -> x0, other arithmetic: 30 us -> none  [the longest x2 16.1 us: convolve(): jnp.concatenate([padded[:, :, col_tap:col_tap + width] for col_tap in ran...]
    all_to_all x0 -> x1, blocking collectives: none -> 22.4 us  [shards(): got = lax.all_to_all(sent, 'member', 0, 0, tiled=True)]
    slice x4 -> x0, local copies, waits for them, and re-layouts: 21.9 us -> none  [the longest x2 21.7 us: convolve(): padded[:, :, col_tap:col_tap + width]]
  transfers between devices with their start and end apart: 5 -> 11, of which waited for: 4 -> 5; matrix products, arithmetic and copies ran while one was open for 1% -> 1% of each run, Pallas kernels for 0% -> 2%
where the time goes in v1:
time: 121 us; the launch traced here: 120 us
  Pallas kernels  44 us (36%)
  starting transfers between devices  28.9 us (24%)
  blocking collectives  22.4 us (19%)
  waiting for transfers between devices  18.3 us (15%)
  local copies, waits for them, and re-layouts  4.56 us (4%)
  between operations  1.43 us (1%)
    all_to_all x1, blocking collectives, shards(): got = lax.all_to_all(sent, 'member', 0, 0, tiled=True)  22.4 us
    pallas_call x1, Pallas kernels, first_call(): pl.pallas_call(functools.partial(first_kernel, block), out_shape=(jax.Sha...  18.1 us
    all_to_all x1, starting transfers between devices, shards(): got = lax.all_to_all(blocks, 'member', 0, 0, tiled=True)  12.7 us
    all_to_all x1, waiting for transfers between devices, shards(): got = lax.all_to_all(blocks, 'member', 0, 0, tiled=True)  12.5 us
    pallas_call x1, Pallas kernels, second_call(): pl.pallas_call(second_kernel, out_shape=(jax.ShapeDtypeStruct(state.shape...  10.8 us
    ppermute x2, starting transfers between devices, exchange(): far = lax.ppermute(far, 'tile', [(1, 2), (2, 1)])  9.09 us
    pallas_call x1, Pallas kernels, features_call(): pl.pallas_call(features_kernel, grid=(width // block,), out_shape=(jax.Sh...  8.84 us
    ppermute x6, starting transfers between devices, exchange(): lax.ppermute(stats, 'tile', swap(b))  6.93 us
  transfers between devices with their start and end apart: 11, of which 5 were waited for; matrix products, arithmetic and copies ran while one was open for 1% of the time, Pallas kernels for 2%

profile of v1, /device:TPU:4, one launch (start us, length us, event | category | flops | bytes accessed | tf_op | source)
XLA Modules:
  0.0 119.6 jit_solution(13446053415664414096)
XLA Ops:
  0.6 1.3 %pad.4.head_ref = bf16[8,128]{1,0:T(8,128)(2,1)} pad(bf16[4,128]{1,0:T(4,128)(2,1)} %param.16, bf16[]{:T(256)} %constant.2.clone.1), padding=0_4x0_0 | pad | bytes 3074 | tf_op jit(solution)/shard_map/jit(_pad)/pad | solution.py:431
  1.9 8.8 %features.1 = (bf16[8,2048,128]{2,1,0:T(8,128)(2,1)}, bf16[2048,128]{1,0:T(8,128)(2,1)}, bf16[2048,128]{1,0:T(8,128)(2,1)}, f32[8,8,2048]{2,1,0:T(8,128)}, f32[8,128]{1,0:T(8,128)}) custom-call(bf16[128,8,2048]{2,1,0:T(8,128)(2,1)} %bitcast.6, bf16[8,128]{1,0:T(8,128)(2,1)} %pad.4.head_ref), custom_call_target="tpu_custom_call" | custom-call | tf_op jit(solution)/shard_map/features/pallas_call | solution.py:95
  10.7 0.1 collective-permute-start
  10.8 4.2 %collective-permute-start.1 = (bf16[2048,128]{1,0:T(8,128)(2,1)}, bf16[2048,128]{1,0:T(8,128)(2,1)S(1)}, u32[]{:S(2)}, u32[]{:S(2)}) collective-permute-start(bf16[2048,128]{1,0:T(8,128)(2,1)} %get-tuple-element.17), channel_id=1, source_target_pairs={{1,2},{2,1},{5,6},{6,5},{9,10},{10,9},{13,14},{14,13},{17,18},{18,... | collective-permute-start | bytes 1572872 | tf_op jit(solution)/shard_map/ppermute | solution.py:423
  15.1 0.1 collective-permute-start.2
  15.2 1.3 %collective-permute-start.3 = (f32[8,128]{1,0:T(8,128)}, f32[8,128]{1,0:T(8,128)S(1)}, u32[]{:S(2)}, u32[]{:S(2)}) collective-permute-start(f32[8,128]{1,0:T(8,128)} %get-tuple-element.18.s0), channel_id=1, source_target_pairs={{0,2},{1,3},{2,0},{3,1},{4,6},{5,7},{6,4},{7,5},{8,10},{9,11},{10,... | collective-permute-start | bytes 12296 | tf_op jit(solution)/shard_map/ppermute | solution.py:425
  16.5 2.1 %collective-permute-start.4 = (f32[8,128]{1,0:T(8,128)}, f32[8,128]{1,0:T(8,128)S(1)}, u32[]{:S(2)}, u32[]{:S(2)}) collective-permute-start(f32[8,128]{1,0:T(8,128)} %get-tuple-element.18.s0), channel_id=1, source_target_pairs={{0,3},{1,2},{2,1},{3,0},{4,7},{5,6},{6,5},{7,4},{8,11},{9,10},{10,... | collective-permute-start | bytes 12296 | tf_op jit(solution)/shard_map/ppermute | solution.py:425
  18.5 2.2 %weights.1 = (bf16[1536,256]{1,0:T(8,128)(2,1)}, bf16[72,128]{1,0:T(8,128)(2,1)}) custom-call(bf16[9,128,128]{2,1,0:T(8,128)(2,1)} %first_ref.1, bf16[9,128,128]{2,1,0:T(8,128)(2,1)} %second_ref.1, bf16[8,128]{1,0:T(8,128)(2,1)} %pad.4.head_ref), custom_call_target="tpu_custom_call" | custom-call | tf_op jit(solution)/shard_map/weights/pallas_call | solution.py:143
  20.8 0.0 collective-permute-done.2.s1
  20.8 0.0 copy-start.9
  20.8 1.4 %collective-permute-done.3.s2 = f32[8,128]{1,0:T(8,128)S(1)} collective-permute-done((f32[8,128]{1,0:T(8,128)}, f32[8,128]{1,0:T(8,128)S(1)}, u32[]{:S(2)}, u32[]{:S(2)}) %collective-permute-start.3) | collective-permute-done | bytes 4128 | tf_op jit(solution)/shard_map/ppermute | solution.py:425
  22.1 0.0 copy-start.10
  22.1 1.1 collective-permute-done.4.s3
  23.2 0.0 collective-permute-done.core_ref
  23.2 0.0 collective-permute-done.1.far_ref
  23.2 0.0 copy-start.3
  23.2 0.0 copy-done.9
  23.2 0.0 copy-done.10
  23.2 0.6 copy-done.11
  23.8 0.2 copy-done.1
  24.0 0.2 copy-done.3
  24.2 18.1 %first.1 = (bf16[8,2048,128]{2,1,0:T(8,128)(2,1)}, bf16[2048,128]{1,0:T(8,128)(2,1)}, bf16[2048,128]{1,0:T(8,128)(2,1)}, f32[8,128]{1,0:T(8,128)}) custom-call(bf16[8,2048,128]{2,1,0:T(8,128)(2,1)} %get-tuple-element.15.x_ref, bf16[2048,128]{1,0:T(8,128)(2,1)} %copy-done.1, bf16[2048,128]{1,0:T(8,128)(2,1)} %copy-done.3, f32[8,128]{1,0:T(8,128)} %get-tuple-element.18.s0, ...), custom_call_target="tpu_custom_call" | custom-call | tf_op jit(solution)/shard_map/first/pallas_call | solution.py:231
  42.3 0.0 collective-permute-start.5
  42.3 4.9 %collective-permute-start.6 = (bf16[2048,128]{1,0:T(8,128)(2,1)}, bf16[2048,128]{1,0:T(8,128)(2,1)S(1)}, u32[]{:S(2)}, u32[]{:S(2)}) collective-permute-start(bf16[2048,128]{1,0:T(8,128)(2,1)} %get-tuple-element.22), channel_id=1, source_target_pairs={{1,2},{2,1},{5,6},{6,5},{9,10},{10,9},{13,14},{14,13},{17,18},{18,... | collective-permute-start | bytes 1572872 | tf_op jit(solution)/shard_map/ppermute | solution.py:423
  47.1 0.1 collective-permute-start.7
  47.2 0.7 collective-permute-start.8
  47.9 2.7 %collective-permute-start.9 = (f32[8,128]{1,0:T(8,128)}, f32[8,128]{1,0:T(8,128)S(1)}, u32[]{:S(2)}, u32[]{:S(2)}) collective-permute-start(f32[8,128]{1,0:T(8,128)} %get-tuple-element.23.s0), channel_id=1, source_target_pairs={{0,3},{1,2},{2,1},{3,0},{4,7},{5,6},{6,5},{7,4},{8,11},{9,10},{10,... | collective-permute-start | bytes 12296 | tf_op jit(solution)/shard_map/ppermute | solution.py:425
  51.3 0.0 collective-permute-done.7.s1
  51.3 0.0 copy-start.6
  51.3 2.9 %collective-permute-done.8.s2 = f32[8,128]{1,0:T(8,128)S(1)} collective-permute-done((f32[8,128]{1,0:T(8,128)}, f32[8,128]{1,0:T(8,128)S(1)}, u32[]{:S(2)}, u32[]{:S(2)}) %collective-permute-start.8) | collective-permute-done | bytes 4128 | tf_op jit(solution)/shard_map/ppermute | solution.py:425
  54.2 0.5 collective-permute-done.9.s3
  54.7 0.0 collective-permute-done.5.core_ref
  54.7 0.0 collective-permute-done.6.far_ref
  54.7 0.0 copy-start.4
  54.7 0.0 copy-done.6
  54.7 0.1 copy-done.7
  54.8 0.5 copy-done.8
  55.3 0.2 copy-done.2
  55.5 0.2 copy-done.4
  55.7 10.8 %second.1 = (f32[4,8,2048]{2,1,0:T(8,128)}, f32[64,8,128]{2,1,0:T(8,128)}) custom-call(bf16[8,2048,128]{2,1,0:T(8,128)(2,1)} %get-tuple-element.20.hid_ref, bf16[2048,128]{1,0:T(8,128)(2,1)} %copy-done.2, bf16[2048,128]{1,0:T(8,128)(2,1)} %copy-done.4, f32[8,128]{1,0:T(8,128)} %get-tuple-element.23.s0, f32[8,128]{1,0:T(8,128)} %copy-done.6, ...), custom_call_target="tpu_custom_call" | custom-call | tf_op jit(solution)/shard_map/second/pallas_call | solution.py:336
  66.5 12.7 %all-to-all-start = ((f32[64,8,128]{2,1,0:T(8,128)}), f32[64,8,128]{2,1,0:T(8,128)S(1)}, u32[]{:S(2)}, u32[]{:S(2)}) async-start(f32[64,8,128]{2,1,0:T(8,128)} %get-tuple-element.26.blocks_ref), calls=%async_computation | async-start | bytes 524288 | tf_op jit(solution)/shard_map/all_to_all | solution.py:440
  79.2 0.0 copy-done.5
  79.3 0.7 reshape.7.reg_ref
  79.9 12.5 %all-to-all-done.got_ref = f32[64,8,128]{2,1,0:T(8,128)S(1)} async-done(((f32[64,8,128]{2,1,0:T(8,128)}), f32[64,8,128]{2,1,0:T(8,128)S(1)}, u32[]{:S(2)}, u32[]{:S(2)}) %all-to-all-start) | async-done | bytes 262176 | tf_op jit(solution)/shard_map/all_to_all | solution.py:440
  92.4 0.7 copy-done
  93.1 1.9 %spread.1 = f32[64,2,8,128]{3,2,1,0:T(8,128)} custom-call(f32[64,8,128]{2,1,0:T(8,128)} %copy-done, f32[8,128]{1,0:T(8,128)} %reshape.7.reg_ref, f32[4]{0:T(128)} %target_ref.1), custom_call_target="tpu_custom_call" | custom-call | tf_op jit(solution)/shard_map/spread/pallas_call | solution.py:382
  95.0 22.4 %all_to_all.10.got_ref = f32[64,2,8,128]{3,2,1,0:T(8,128)} all-to-all(f32[64,2,8,128]{3,2,1,0:T(8,128)} %spread.1), channel_id=1, replica_groups=mesh['member'=64,'tile'=4] {'member'}, dimensions={0} | all-to-all | bytes 1048576 | tf_op jit(solution)/shard_map/all_to_all | solution.py:443
  117.5 2.1 %field.1 = f32[4,8,2048]{2,1,0:T(8,128)} custom-call(f32[64,8,128]{2,1,0:T(8,128)} %get-tuple-element.26.blocks_ref, f32[64,2,8,128]{3,2,1,0:T(8,128)} %all_to_all.10.got_ref), custom_call_target="tpu_custom_call" | custom-call | tf_op jit(solution)/shard_map/field/pallas_call | solution.py:411
  (8 shorter events, 0.0 us)
Async XLA Ops:
  10.7 12.5 %collective-permute-start = (bf16[2048,128]{1,0:T(8,128)(2,1)}, bf16[2048,128]{1,0:T(8,128)(2,1)S(1)}, u32[]{:S(2)}, u32[]{:S(2)}) collective-permute-start(bf16[2048,128]{1,0:T(8,128)(2,1)} %get-tuple-element.16), channel_id=1, source_target_pairs={{0,1},{1,0},{2,3},{3,2},{4,5},{5,4},{6,7},{7,6},{8,9},{9,8},{10,11... | collective-permute-start | bytes 1572872 | tf_op jit(solution)/shard_map/ppermute | solution.py:424
  10.8 12.4 %collective-permute-start.1 = (bf16[2048,128]{1,0:T(8,128)(2,1)}, bf16[2048,128]{1,0:T(8,128)(2,1)S(1)}, u32[]{:S(2)}, u32[]{:S(2)}) collective-permute-start(bf16[2048,128]{1,0:T(8,128)(2,1)} %get-tuple-element.17), channel_id=1, source_target_pairs={{1,2},{2,1},{5,6},{6,5},{9,10},{10,9},{13,14},{14,13},{17,18},{18,... | collective-permute-start | bytes 1572872 | tf_op jit(solution)/shard_map/ppermute | solution.py:423
  15.1 5.7 %collective-permute-start.2 = (f32[8,128]{1,0:T(8,128)}, f32[8,128]{1,0:T(8,128)S(1)}, u32[]{:S(2)}, u32[]{:S(2)}) collective-permute-start(f32[8,128]{1,0:T(8,128)} %get-tuple-element.18.s0), channel_id=1, source_target_pairs={{0,1},{1,0},{2,3},{3,2},{4,5},{5,4},{6,7},{7,6},{8,9},{9,8},{10,11... | collective-permute-start | bytes 12296 | tf_op jit(solution)/shard_map/ppermute | solution.py:425
  15.2 7.0 %collective-permute-start.3 = (f32[8,128]{1,0:T(8,128)}, f32[8,128]{1,0:T(8,128)S(1)}, u32[]{:S(2)}, u32[]{:S(2)}) collective-permute-start(f32[8,128]{1,0:T(8,128)} %get-tuple-element.18.s0), channel_id=1, source_target_pairs={{0,2},{1,3},{2,0},{3,1},{4,6},{5,7},{6,4},{7,5},{8,10},{9,11},{10,... | collective-permute-start | bytes 12296 | tf_op jit(solution)/shard_map/ppermute | solution.py:425
  16.5 6.7 %collective-permute-start.4 = (f32[8,128]{1,0:T(8,128)}, f32[8,128]{1,0:T(8,128)S(1)}, u32[]{:S(2)}, u32[]{:S(2)}) collective-permute-start(f32[8,128]{1,0:T(8,128)} %get-tuple-element.18.s0), channel_id=1, source_target_pairs={{0,3},{1,2},{2,1},{3,0},{4,7},{5,6},{6,5},{7,4},{8,11},{9,10},{10,... | collective-permute-start | bytes 12296 | tf_op jit(solution)/shard_map/ppermute | solution.py:425
  20.8 2.5 %copy-start.9 = (f32[8,128]{1,0:T(8,128)}, f32[8,128]{1,0:T(8,128)S(1)}, u32[]{:S(2)}) copy-start(f32[8,128]{1,0:T(8,128)S(1)} %collective-permute-done.2.s1) | copy-start | bytes 12292
  22.1 1.1 copy-start.10
  23.2 0.6 copy-start.11
  23.2 0.8 copy-start.1
  23.2 1.0 copy-start.3
  42.3 37.0 %copy-start.5 = (f32[4,8,32]{2,1,0:T(8,128)S(1)}, f32[4,8,32]{2,1,0:T(8,128)}, u32[]{:S(2)}) copy-start(f32[4,8,32]{2,1,0:T(8,128)} %param.12) | copy-start | bytes 12292
  42.3 12.4 %collective-permute-start.5 = (bf16[2048,128]{1,0:T(8,128)(2,1)}, bf16[2048,128]{1,0:T(8,128)(2,1)S(1)}, u32[]{:S(2)}, u32[]{:S(2)}) collective-permute-start(bf16[2048,128]{1,0:T(8,128)(2,1)} %get-tuple-element.21), channel_id=1, source_target_pairs={{0,1},{1,0},{2,3},{3,2},{4,5},{5,4},{6,7},{7,6},{8,9},{9,8},{10,11... | collective-permute-start | bytes 1572872 | tf_op jit(solution)/shard_map/ppermute | solution.py:424
  42.3 12.4 %collective-permute-start.6 = (bf16[2048,128]{1,0:T(8,128)(2,1)}, bf16[2048,128]{1,0:T(8,128)(2,1)S(1)}, u32[]{:S(2)}, u32[]{:S(2)}) collective-permute-start(bf16[2048,128]{1,0:T(8,128)(2,1)} %get-tuple-element.22), channel_id=1, source_target_pairs={{1,2},{2,1},{5,6},{6,5},{9,10},{10,9},{13,14},{14,13},{17,18},{18,... | collective-permute-start | bytes 1572872 | tf_op jit(solution)/shard_map/ppermute | solution.py:423
  47.1 4.1 %collective-permute-start.7 = (f32[8,128]{1,0:T(8,128)}, f32[8,128]{1,0:T(8,128)S(1)}, u32[]{:S(2)}, u32[]{:S(2)}) collective-permute-start(f32[8,128]{1,0:T(8,128)} %get-tuple-element.23.s0), channel_id=1, source_target_pairs={{0,1},{1,0},{2,3},{3,2},{4,5},{5,4},{6,7},{7,6},{8,9},{9,8},{10,11... | collective-permute-start | bytes 12296 | tf_op jit(solution)/shard_map/ppermute | solution.py:425
  47.2 6.9 %collective-permute-start.8 = (f32[8,128]{1,0:T(8,128)}, f32[8,128]{1,0:T(8,128)S(1)}, u32[]{:S(2)}, u32[]{:S(2)}) collective-permute-start(f32[8,128]{1,0:T(8,128)} %get-tuple-element.23.s0), channel_id=1, source_target_pairs={{0,2},{1,3},{2,0},{3,1},{4,6},{5,7},{6,4},{7,5},{8,10},{9,11},{10,... | collective-permute-start | bytes 12296 | tf_op jit(solution)/shard_map/ppermute | solution.py:425
  47.9 6.7 %collective-permute-start.9 = (f32[8,128]{1,0:T(8,128)}, f32[8,128]{1,0:T(8,128)S(1)}, u32[]{:S(2)}, u32[]{:S(2)}) collective-permute-start(f32[8,128]{1,0:T(8,128)} %get-tuple-element.23.s0), channel_id=1, source_target_pairs={{0,3},{1,2},{2,1},{3,0},{4,7},{5,6},{6,5},{7,4},{8,11},{9,10},{10,... | collective-permute-start | bytes 12296 | tf_op jit(solution)/shard_map/ppermute | solution.py:425
  51.3 3.4 %copy-start.6 = (f32[8,128]{1,0:T(8,128)}, f32[8,128]{1,0:T(8,128)S(1)}, u32[]{:S(2)}) copy-start(f32[8,128]{1,0:T(8,128)S(1)} %collective-permute-done.7.s1) | copy-start | bytes 12292
  54.2 0.6 copy-start.7
  54.7 0.6 copy-start.8
  54.7 0.8 copy-start.2
  54.7 1.0 copy-start.4
  66.5 25.9 %all-to-all-start = ((f32[64,8,128]{2,1,0:T(8,128)}), f32[64,8,128]{2,1,0:T(8,128)S(1)}, u32[]{:S(2)}, u32[]{:S(2)}) async-start(f32[64,8,128]{2,1,0:T(8,128)} %get-tuple-element.26.blocks_ref), calls=%async_computation | async-start | bytes 524288 | tf_op jit(solution)/shard_map/all_to_all | solution.py:440
  92.4 0.7 copy-start

commit v2 on v1

v2 whole, which is shorter than its diff:
```python
import functools

import jax
import jax.numpy as jnp
from jax import lax
from jax.experimental import pallas as pl
from jax.experimental.pallas import tpu as pltpu
from jax.sharding import PartitionSpec as P

GROUP = 4
TILES = 4
F32, BF16 = jnp.float32, jnp.bfloat16
VM = pl.BlockSpec(memory_space=pltpu.VMEM)
SM = pl.BlockSpec(memory_space=pltpu.SMEM)


def limit(mib):
    return pltpu.CompilerParams(vmem_limit_bytes=mib * 1024 * 1024)


def group_total(row):
    lane = lax.broadcasted_iota(jnp.int32, row.shape, 1)
    size = row.shape[1]
    for step in (1, 2):
        up = pltpu.roll(row, step, 1)
        down = pltpu.roll(row, size - step, 1)
        row = row + jnp.where((lane & step) == 0, down, up)
    return row


def merged(parts, count):
    means = [p[0:1, :] for p in parts]
    devs = [p[1:2, :] for p in parts]
    members = len(parts) * GROUP
    mean = group_total(functools.reduce(jnp.add, means)) / members
    spread = functools.reduce(jnp.add, [(m - mean) * (m - mean) for m in means])
    total = group_total(functools.reduce(jnp.add, devs) + count * spread)
    return mean, lax.rsqrt(total / (members * count) + 1e-05)


def silu(values):
    half = 0.5 * values
    return half + half * jnp.tanh(half)


def row_sum(values):
    return values.reshape(-1, 8, values.shape[1]).sum(0)


def write_stats(st_ref, pivot, first, second, count):
    one = jnp.sum(first, axis=0, keepdims=True)
    two = jnp.sum(second, axis=0, keepdims=True)
    mean = pivot + one / count
    dev = two - one * one / count
    pad = jnp.zeros((6, mean.shape[1]), F32)
    st_ref[...] = jnp.concatenate([mean, dev, pad], axis=0)


def features_kernel(x_ref, xt_ref, core_ref, far_ref, st_ref, scr, acc):
    step = pl.program_id(0)
    chans, rows, width = x_ref.shape
    even = (lax.axis_index("tile") & 1) == 0
    for part in range(width // 128):
        at = pl.ds(128 * part, 128)
        scr[part] = x_ref[:, :, at].astype(F32).reshape(chans * rows, 128)
        one = two = jnp.zeros((8, chans), F32)
        for r in range(rows):
            turned = scr[part, pl.ds(r, chans, stride=rows), :].T
            if part == 0 and r == 0:

                @pl.when(step == 0)
                def _():
                    middle = jnp.mean(turned, axis=0, keepdims=True)
                    acc[0] = jnp.broadcast_to(middle, acc.shape[1:])
                    acc[1] = jnp.zeros(acc.shape[1:], F32)
                    acc[2] = jnp.zeros(acc.shape[1:], F32)

            if r == 0:
                pivot = acc[0, 0:1]
            off = turned - pivot
            one = one + row_sum(off)
            two = two + row_sum(off * off)
            turned = turned.astype(BF16)
            xt_ref[r, at] = turned
            if r == 0:
                top = turned
        acc[1] += one
        acc[2] += two
        core_ref[at] = jnp.where(even, turned, top)
        far_ref[at] = jnp.where(even, top, turned)

    @pl.when(step == pl.num_programs(0) - 1)
    def _():
        write_stats(st_ref, acc[0, 0:1], acc[1], acc[2], pl.num_programs(0) * rows * width)


def features_call(x, block):
    chans, rows, width = x.shape
    edge = jax.ShapeDtypeStruct((width, chans), BF16)
    return pl.pallas_call(
        features_kernel,
        grid=(width // block,),
        out_shape=(
            jax.ShapeDtypeStruct((rows, width, chans), BF16),
            edge,
            edge,
            jax.ShapeDtypeStruct((8, chans), F32),
        ),
        in_specs=[pl.BlockSpec((chans, rows, block), lambda i: (0, 0, i))],
        out_specs=(
            pl.BlockSpec((rows, block, chans), lambda i: (0, i, 0)),
            pl.BlockSpec((block, chans), lambda i: (i, 0)),
            pl.BlockSpec((block, chans), lambda i: (i, 0)),
            pl.BlockSpec((8, chans), lambda i: (0, 0)),
        ),
        scratch_shapes=[
            pltpu.VMEM((block // 128, chans * rows, 128), F32),
            pltpu.VMEM((3, 8, chans), F32),
        ],
        compiler_params=limit(16),
        name="features",
    )(x)


def step_factors(index):
    lane = lax.broadcasted_iota(jnp.int32, (8, 128), 1)
    steps = lane.astype(F32)
    upper = 800.0 ** (1.0 / 7.0)
    lower = 0.002 ** (1.0 / 7.0)
    root = upper + steps / 17.0 * (lower - upper)
    square = root * root
    sigmas = square * square * square * root
    sigma = jnp.sum(jnp.where(lane == index, sigmas, 0.0), axis=1, keepdims=True)
    follow = jnp.sum(jnp.where(lane == index + 1, sigmas, 0.0), axis=1, keepdims=True)
    sigma, follow = jnp.broadcast_to(sigma, lane.shape), jnp.broadcast_to(follow, lane.shape)
    hat = 1.25 * sigma
    spread = hat * hat + 0.25
    skip = 0.25 / spread
    gain = 0.5 * hat / jnp.sqrt(spread)
    rate = (follow - hat) / hat
    keep = 1.0 + rate - rate * skip
    return keep, keep * jnp.sqrt(hat * hat - sigma * sigma), -rate * gain


def weights_kernel(first_ref, second_ref, head_ref, wt_ref, fold_ref):
    chans = first_ref.shape[1]
    wt_ref[...] = jnp.zeros(wt_ref.shape, BF16)
    for tap in range(9):
        turned = first_ref[tap].astype(F32).T.astype(BF16)
        for q in range(2):
            row, col = tap // 3 + q, tap % 3
            wt_ref[pl.ds((3 * row + col) * chans, chans), pl.ds(q * chans, chans)] = turned
    head = jnp.concatenate([head_ref[...].astype(F32)] * 2, axis=0).astype(BF16)
    low = lax.broadcasted_iota(jnp.int32, (8, chans), 0) >= 4
    lines = []
    for row in range(3):
        parts = []
        for col in range(3):
            folded = jnp.dot(head, second_ref[3 * row + col], preferred_element_type=F32)
            high = folded.astype(BF16).astype(F32)
            parts.append(jnp.where(low, folded - high, high))
        lines.append(jnp.concatenate(parts, axis=0))
    none = jnp.zeros_like(lines[0])
    left = jnp.concatenate([lines[2], lines[1], lines[0], none], axis=0)
    right = jnp.concatenate([none, lines[2], lines[1], lines[0]], axis=0)
    fold_ref[...] = jnp.concatenate([left, right], axis=1).astype(BF16)


def weights_call(first, second, head):
    chans = first.shape[1]
    return pl.pallas_call(
        weights_kernel,
        out_shape=(
            jax.ShapeDtypeStruct((12 * chans, 2 * chans), BF16),
            jax.ShapeDtypeStruct((96, 2 * chans), BF16),
        ),
        in_specs=[VM] * 3,
        out_specs=(VM, VM),
        compiler_params=limit(16),
        cost_estimate=pl.CostEstimate(flops=1 << 22, bytes_accessed=1 << 21, transcendentals=0),
        name="weights",
    )(first, second, head)


def turned_on():
    tile = lax.axis_index("tile")
    even = (tile & 1) == 0
    inner = ((tile == 1) | (tile == 2)).astype(F32)
    return even, jnp.where(even, inner, 1.0), jnp.where(even, 1.0, inner)


def norm_factors(refs, count):
    mean, scale = merged([ref[...] for ref in refs], count)
    return scale, -mean * scale


def fill(act, buf, value, at, size):
    buf[pl.ds(at + 8, size), :] = value
    act[1, pl.ds(at, size), :] = value.astype(BF16)


def fill_sides(act, buf, at, size):
    act[0, pl.ds(at, size), :] = buf[pl.ds(at + 7, size), :].astype(BF16)
    act[2, pl.ds(at, size), :] = buf[pl.ds(at + 9, size), :].astype(BF16)


def clear_ends(buf):
    size, chans = buf.shape
    buf[pl.ds(0, 8), :] = jnp.zeros((8, chans), F32)
    buf[pl.ds(size - 8, 8), :] = jnp.zeros((8, chans), F32)


def two_rows(acts, wt_ref, at, block):
    left = jnp.concatenate([act[s, pl.ds(at, block), :] for act in acts for s in range(3)], axis=1)
    out = jnp.dot(left, wt_ref[...], preferred_element_type=F32)
    chans = out.shape[1] // 2
    return out[:, :chans], out[:, chans:]


def inner_kernel(block, x_ref, s0, s1, s2, s3, wt_ref, hid_ref, sum_ref, *rest):
    rows, width, chans = x_ref.shape
    acts, bufs = rest[:rows], rest[rows:]
    scale, shift = norm_factors([s0, s1, s2, s3], rows * width)
    for buf in bufs:
        clear_ends(buf)

    def centre(row, at, size):
        value = silu(x_ref[row, pl.ds(at, size), :].astype(F32) * scale + shift)
        fill(acts[row], bufs[row % 2], value, at, size)

    def sides(row, at, size):
        fill_sides(acts[row], bufs[row % 2], at, size)

    for row in range(1, 5):
        centre(row, 0, width)
        sides(row, 0, width)
    one = two = jnp.zeros((8, chans), F32)
    pivot = None
    for pair, fresh in ((0, (5, 6)), (1, (7, 0))):
        for at in range(0, width, block):
            a, b = two_rows(acts[2 * pair + 1 : 2 * pair + 5], wt_ref, at, block)
            for row in fresh:
                centre(row, at, block)
                if at > 0:
                    sides(row, at - block, block)
            hid_ref[2 * pair, pl.ds(at, block), :] = a.astype(BF16)
            hid_ref[2 * pair + 1, pl.ds(at, block), :] = b.astype(BF16)
            if pivot is None:
                pivot = jnp.mean(a[0:8], axis=0, keepdims=True)
            a, b = a - pivot, b - pivot
            one = one + row_sum(a + b)
            two = two + row_sum(a * a + b * b)
        for row in fresh:
            sides(row, width - block, block)
    sum_ref[0] = jnp.broadcast_to(pivot, one.shape)
    sum_ref[1] = one
    sum_ref[2] = two


def inner_call(xt, stats, wt, block):
    rows, width, chans = xt.shape
    act = jax.ShapeDtypeStruct((3, width, chans), BF16)
    hid, sums, *acts = pl.pallas_call(
        functools.partial(inner_kernel, block),
        out_shape=(
            jax.ShapeDtypeStruct((rows - 4, width, chans), BF16),
            jax.ShapeDtypeStruct((3, 8, chans), F32),
        )
        + (act,) * rows,
        in_specs=[VM] * 6,
        out_specs=(VM,) * (rows + 2),
        scratch_shapes=[pltpu.VMEM((width + 16, chans), F32)] * 2,
        compiler_params=limit(26),
        cost_estimate=pl.CostEstimate(
            flops=12 * rows * width * chans * chans * 2, bytes_accessed=1 << 22, transcendentals=xt.size
        ),
        name="inner",
    )(xt, *stats, wt)
    return hid, sums, acts


def outer_kernel(block, *refs):
    acts, refs = list(refs[:6]), refs[6:]
    core_ref, far_ref, s0, s1, s2, s3, sum_ref, wt_ref, hid_ref, hcore_ref, hfar_ref, st_ref, top, bottom, b0, b1 = refs
    width, chans = core_ref.shape
    rows = hid_ref.shape[0] + 4
    even, top_on, bottom_on = turned_on()
    scale, shift = norm_factors([s0, s1, s2, s3], rows * width)

    def halo(act, buf, pick, factor, at):
        clear_ends(buf)
        value = silu(pick(pl.ds(at, block)).astype(F32) * scale + shift) * factor
        fill(act, buf, value, at, block)
        if at > 0:
            fill_sides(act, buf, at - block, block)
        if at + block == width:
            fill_sides(act, buf, at, block)

    upper = lambda at: jnp.where(even, far_ref[at, :], core_ref[at, :])
    lower = lambda at: jnp.where(even, core_ref[at, :], far_ref[at, :])
    for at in range(0, width, block):
        halo(top, b0, upper, top_on, at)
    pivot, one, two = sum_ref[0, 0:1], sum_ref[1], sum_ref[2]
    groups = ([top] + acts[:3], acts[3:] + [bottom])
    for pair, group in enumerate(groups):
        for at in range(0, width, block):
            a, b = two_rows(group, wt_ref, at, block)
            if pair == 0:
                halo(bottom, b1, lower, bottom_on, at)
            high, low = a.astype(BF16), b.astype(BF16)
            hid_ref[2 * pair, pl.ds(at, block), :] = high
            hid_ref[2 * pair + 1, pl.ds(at, block), :] = low
            if pair == 0:
                hcore_ref[pl.ds(at, block), :] = high
            else:
                first = hcore_ref[pl.ds(at, block), :]
                hcore_ref[pl.ds(at, block), :] = jnp.where(even, low, first)
                hfar_ref[pl.ds(at, block), :] = jnp.where(even, first, low)
            a, b = a - pivot, b - pivot
            one = one + row_sum(a + b)
            two = two + row_sum(a * a + b * b)
    write_stats(st_ref, pivot, one, two, rows * width)


def outer_call(acts, core, far, stats, sums, wt, block):
    width, chans = core.shape
    edge = jax.ShapeDtypeStruct((width, chans), BF16)
    act = pltpu.VMEM((3, width, chans), BF16)
    return pl.pallas_call(
        functools.partial(outer_kernel, block),
        out_shape=(
            jax.ShapeDtypeStruct((4, width, chans), BF16),
            edge,
            edge,
            jax.ShapeDtypeStruct((8, chans), F32),
        ),
        in_specs=[VM] * 14,
        out_specs=(VM,) * 4,
        scratch_shapes=[act] * 2 + [pltpu.VMEM((width + 16, chans), F32)] * 2,
        compiler_params=limit(20),
        name="outer",
    )(*acts[:3], *acts[-3:], core, far, *stats, sums, wt)


def turn_quarters(values, slot):
    out = []
    for j in range(4):
        mixed = values[j]
        for k in range(4):
            if k != j:
                moved = pltpu.roll(values[k], (32 * (k - j)) % 128, 1)
                mixed = jnp.where(slot == k, moved, mixed)
        out.append(mixed)
    return out


def taps_kernel(x_ref, mid_ref, rim_ref, s0, s1, s2, s3, fold_ref, head_ref, sum_ref, *rest):
    half, width, chans = mid_ref.shape
    rows = 2 * half
    acts, taps = rest[:half], rest[half]
    scale, shift = norm_factors([s0, s1, s2, s3], rows * width)
    head = head_ref[...].astype(F32)
    head = jnp.concatenate([head, jnp.zeros_like(head)], axis=0)
    none = jnp.zeros_like(head)
    head = jnp.concatenate(
        [jnp.concatenate([head, none], axis=1), jnp.concatenate([none, head], axis=1)], axis=0
    ).astype(BF16)
    direct = []
    for pair in range(half):
        features = jnp.concatenate([x_ref[2 * pair], x_ref[2 * pair + 1]], axis=1)
        direct.append(
            lax.dot_general(head, features, (((1,), (1,)), ((), ())), preferred_element_type=F32)
        )
        for side in range(2):
            row = 2 * pair + side
            if row < 2:
                value = rim_ref[row]
            elif row < rows - 2:
                value = mid_ref[row - 2]
            else:
                value = rim_ref[row - half]
            value = silu(value.astype(F32) * scale + shift)
            acts[pair][:, pl.ds(side * chans, chans)] = value.astype(BF16)
        taps[pair] = lax.dot_general(
            fold_ref[...], acts[pair][...], (((1,), (1,)), ((), ())), preferred_element_type=F32
        )
    for pair in range(half):
        total = taps[pair, 24:48]
        if pair > 0:
            total = total + taps[pair - 1, 72:96]
        sum_ref[2 * pair] = total
        sum_ref[2 * pair, 8:16] += direct[pair][0:8]
        total = taps[pair, 48:72]
        if pair + 1 < half:
            total = total + taps[pair + 1, 0:24]
        sum_ref[2 * pair + 1] = total
        sum_ref[2 * pair + 1, 8:16] += direct[pair][8:16]


def taps_call(xt, mid, rim, stats, fold, head):
    half, width, chans = mid.shape
    return pl.pallas_call(
        taps_kernel,
        out_shape=jax.ShapeDtypeStruct((2 * half, 24, width), F32),
        in_specs=[VM] * 9,
        out_specs=VM,
        scratch_shapes=[pltpu.VMEM((width, 2 * chans), BF16)] * half + [pltpu.VMEM((half, 96, width), F32)],
        compiler_params=limit(24),
        cost_estimate=pl.CostEstimate(
            flops=768 * width * chans * half * 8, bytes_accessed=1 << 22, transcendentals=2 * mid.size
        ),
        name="taps",
    )(xt, mid, rim, *stats, fold, head)


def step_kernel(
    core_ref, far_ref, s0, s1, s2, s3, fold_ref, sum_ref, state_ref, noise_ref, index_ref,
    next_ref, blocks_ref, act, net,
):
    width, chans = core_ref.shape
    rows = sum_ref.shape[0]
    outs = state_ref.shape[0]
    even, top_on, bottom_on = turned_on()
    scale, shift = norm_factors([s0, s1, s2, s3], rows * width)
    upper = jnp.where(even, far_ref[...], core_ref[...])
    lower = jnp.where(even, core_ref[...], far_ref[...])
    upper = silu(upper.astype(F32) * scale + shift) * top_on
    lower = silu(lower.astype(F32) * scale + shift) * bottom_on
    act[:, pl.ds(0, chans)] = upper.astype(BF16)
    act[:, pl.ds(chans, chans)] = lower.astype(BF16)
    none = jnp.zeros((24, chans), BF16)
    ends = jnp.concatenate(
        [
            jnp.concatenate([fold_ref[72:96, chans:], none], axis=1),
            jnp.concatenate([none, fold_ref[0:24, :chans]], axis=1),
        ],
        axis=0,
    )
    ends = lax.dot_general(ends, act[...], (((1,), (1,)), ((), ())), preferred_element_type=F32)
    lane = lax.broadcasted_iota(jnp.int32, (8, width), 1)
    for r in range(rows):
        total = sum_ref[r]
        if r == 0:
            total = total + ends[0:24]
        if r == rows - 1:
            total = total + ends[24:48]
        left = jnp.where(lane == 0, 0.0, pltpu.roll(total[0:8], 1, 1))
        right = jnp.where(lane == width - 1, 0.0, pltpu.roll(total[16:24], width - 1, 1))
        both = left + total[8:16] + right
        both = both[0:4] + both[4:8]
        for o in range(outs):
            net[o, r : r + 1, :] = both[o : o + 1]

    keep, stir, push = step_factors(index_ref[0])
    quarter = width // 512
    for t in range(width // 128):
        at = pl.ds(t * 128, 128)
        for o in range(outs):
            direct = keep * state_ref[o, :, at] + stir * noise_ref[o, :, at]
            next_ref[o, :, at] = direct + push * net[o, :, at]
    slot = lax.broadcasted_iota(jnp.int32, (rows, 128), 1) // 32
    for t in range(quarter):
        for o in range(outs):
            values = [next_ref[o, :, pl.ds((quarter * k + t) * 128, 128)] for k in range(4)]
            for j, mixed in enumerate(turn_quarters(values, slot)):
                blocks_ref[4 * t + j, o] = mixed


def step_call(core, far, stats, fold, sums, state, noise, index):
    width, chans = core.shape
    rows = sums.shape[0]
    return pl.pallas_call(
        step_kernel,
        out_shape=(
            jax.ShapeDtypeStruct(state.shape, F32),
            jax.ShapeDtypeStruct((width // 128, state.shape[0], rows, 128), F32),
        ),
        in_specs=[VM] * 10 + [SM],
        out_specs=(VM, VM),
        scratch_shapes=[pltpu.VMEM((width, 2 * chans), BF16), pltpu.VMEM(state.shape, F32)],
        compiler_params=limit(12),
        name="step",
    )(core, far, *stats, fold, sums, state, noise, index)


def sums_kernel(got_ref, reg_ref, out_ref):
    count = got_ref.shape[0]
    shape = got_ref.shape[2:]
    own = lax.broadcasted_iota(jnp.int32, shape, 1) // 32 == lax.axis_index("member") // count
    for o in range(got_ref.shape[1]):
        first = got_ref[0, o]
        second = first * first
        for m in range(1, count):
            value = got_ref[m, o]
            first = first + value
            second = second + value * value
        out_ref[0, o] = first
        out_ref[1, o] = second
        out_ref[2, o] = jnp.where(own, reg_ref[o], 0.0)


def sums_call(got, reg):
    return pl.pallas_call(
        sums_kernel,
        out_shape=jax.ShapeDtypeStruct((3,) + got.shape[1:], F32),
        in_specs=[VM, VM],
        out_specs=VM,
        compiler_params=limit(8),
        name="sums",
    )(got, reg)


def spread_kernel(members, one_ref, two_ref, target_ref, out_ref):
    copies, _, outs = out_ref.shape[:3]
    for o in range(outs):
        mean = (one_ref[0, o] + two_ref[0, o]) / members
        var = (one_ref[1, o] + two_ref[1, o]) / members - mean * mean
        scale = jnp.sqrt(1.0 + target_ref[o] / (var + 1.0))
        offset = one_ref[2, o] + two_ref[2, o] + mean - mean * scale
        for k in range(copies):
            out_ref[k, 0, o] = scale
            out_ref[k, 1, o] = offset


def spread_call(one, two, target, copies, members):
    return pl.pallas_call(
        functools.partial(spread_kernel, members),
        out_shape=jax.ShapeDtypeStruct((copies, 2) + one.shape[1:], F32),
        in_specs=[VM, VM, SM],
        out_specs=VM,
        compiler_params=limit(8),
        name="spread",
    )(one, two, target)


def field_kernel(blocks_ref, got_ref, out_ref):
    outs, rows, width = out_ref.shape
    quarter = width // 512
    slot = lax.broadcasted_iota(jnp.int32, (rows, 128), 1) // 32
    for t in range(quarter):
        for o in range(outs):
            values = [
                blocks_ref[4 * t + j, o] * got_ref[4 * t + j, 0, o] + got_ref[4 * t + j, 1, o] for j in range(4)
            ]
            for k, mixed in enumerate(turn_quarters(values, slot)):
                out_ref[o, :, pl.ds((quarter * k + t) * 128, 128)] = mixed


def field_call(blocks, got, shape):
    return pl.pallas_call(
        field_kernel,
        out_shape=jax.ShapeDtypeStruct(shape, F32),
        in_specs=[VM, VM],
        out_specs=VM,
        compiler_params=limit(8),
        name="field",
    )(blocks, got)


def exchange(core, far, stats):
    swap = lambda bits: [(i, i ^ bits) for i in range(TILES)]
    parts = [stats] + [lax.ppermute(stats, "tile", swap(b)) for b in (1, 2, 3)]
    far = lax.ppermute(far, "tile", [(1, 2), (2, 1)])
    core = lax.ppermute(core, "tile", swap(1))
    return core, far, parts


def shards(
    features, residual_state, noise, regression_mean, step_index, conv_first, conv_second, head_weight, spread_target
):
    member = pltpu.with_memory_space_constraint(features[0], pltpu.HBM)
    xt, core, far, stats = features_call(member, 256)
    core, far, stats = exchange(core, far, stats)
    wt, fold = weights_call(conv_first, conv_second, head_weight)
    mid, sums, acts = inner_call(xt, stats, wt, 1024)
    rim, core, far, stats = outer_call(acts, core, far, stats, sums, wt, 1024)
    core, far, stats = exchange(core, far, stats)
    sums = taps_call(xt, mid, rim, stats, fold, head_weight)
    advanced, blocks = step_call(
        core, far, stats, fold, sums, residual_state[0], noise[0], step_index
    )
    members = lax.axis_size("member")
    size = blocks.shape[0]
    runs = [list(range(i, i + size)) for i in range(0, members, size)]
    got = lax.all_to_all(blocks, "member", 0, 0, tiled=True, axis_index_groups=runs)
    reg = jnp.tile(regression_mean, (1, 1, 4))
    sums = sums_call(got, reg)
    sums = sums + lax.ppermute(sums, "member", [(i, i ^ size) for i in range(members)])
    other = lax.ppermute(sums, "member", [(i, i ^ (3 * size)) for i in range(members)])
    sent = spread_call(sums, other, spread_target, size, members)
    got = lax.all_to_all(sent, "member", 0, 0, tiled=True, axis_index_groups=runs)
    field = field_call(blocks, got, advanced.shape)
    return (field[None], advanced[None])


def solution(mesh):
    cells = P("member", None, "tile", None)
    return jax.shard_map(
        shards,
        mesh=mesh,
        in_specs=(cells, cells, cells, P(None, "tile", "member"), P(), P(), P(), P(), P()),
        out_specs=(cells, cells),
        check_vma=False,
    )
```

time: 121 us -> 90.6 us (0.75)
  Pallas kernels: 44 us -> 25.6 us
  blocking collectives: 22.4 us -> 12.8 us
  local copies, waits for them, and re-layouts: 4.56 us -> 0.14 us
  waiting for transfers between devices: 18.3 us -> 20 us
  starting transfers between devices: 28.9 us -> 30.2 us
    pallas_call x3 -> x6, Pallas kernels: 30.8 us -> 16.5 us  [the longest x1 5.84 us: inner_call(): pl.pallas_call(functools.partial(inner_kernel, block), out_shape=(jax.Sha...]
    all_to_all x1, blocking collectives: 22.4 us -> 12.8 us  [shards(): lax.all_to_all(sent, 'member', 0, 0, tiled=True, axis_index_groups=runs)]
    ppermute x6 -> x8, starting transfers between devices: 6.93 us -> 14.9 us  [the longest x6 6.93 us: exchange(): parts = [stats] + [lax.ppermute(stats, 'tile', swap(b)) for b in (1, 2, 3)]]
    ppermute x2, waiting for transfers between devices: 0.01 us -> 6.98 us  [exchange(): far = lax.ppermute(far, 'tile', [(1, 2), (2, 1)])]
    all_to_all x1, starting transfers between devices: 12.7 us -> 6.57 us  [shards(): lax.all_to_all(blocks, 'member', 0, 0, tiled=True, axis_index_groups=runs)]
    all_to_all x1, waiting for transfers between devices: 12.5 us -> 7.73 us  [shards(): lax.all_to_all(blocks, 'member', 0, 0, tiled=True, axis_index_groups=runs)]
    unnamed x24 -> x14, local copies, waits for them, and re-layouts: 2.63 us -> 0.03 us
    pallas_call x1, Pallas kernels: 2.23 us -> 0.2 us  [weights_call(): pl.pallas_call(weights_kernel, out_shape=(jax.ShapeDtypeStruct((12 * chan...]
  transfers between devices with their start and end apart: 11 -> 13, of which waited for: 5 -> 5; matrix products, arithmetic and copies ran while one was open for 1% -> 0% of each run, Pallas kernels for 2% -> 10%
where the time goes in v2:
time: 90.6 us; the launch traced here: 90.2 us
  starting transfers between devices  30.2 us (33%)
  Pallas kernels  25.6 us (28%)
  waiting for transfers between devices  20 us (22%)
  blocking collectives  12.8 us (14%)
  between operations  1.51 us (2%)
    all_to_all x1, blocking collectives, shards(): lax.all_to_all(sent, 'member', 0, 0, tiled=True, axis_index_groups=runs)  12.8 us
    all_to_all x1, waiting for transfers between devices, shards(): lax.all_to_all(blocks, 'member', 0, 0, tiled=True, axis_index_groups=runs)  7.73 us
    ppermute x2, starting transfers between devices, exchange(): far = lax.ppermute(far, 'tile', [(1, 2), (2, 1)])  7.71 us
    ppermute x2, waiting for transfers between devices, exchange(): far = lax.ppermute(far, 'tile', [(1, 2), (2, 1)])  6.98 us
    pallas_call x1, Pallas kernels, features_call(): pl.pallas_call(features_kernel, grid=(width // block,), out_shape=(jax.Sh...  6.94 us
    ppermute x6, starting transfers between devices, exchange(): parts = [stats] + [lax.ppermute(stats, 'tile', swap(b)) for b in (1, 2, 3)]  6.93 us
    all_to_all x1, starting transfers between devices, shards(): lax.all_to_all(blocks, 'member', 0, 0, tiled=True, axis_index_groups=runs)  6.57 us
    pallas_call x1, Pallas kernels, inner_call(): pl.pallas_call(functools.partial(inner_kernel, block), out_shape=(jax.Sha...  5.84 us
  transfers between devices with their start and end apart: 13, of which 5 were waited for; matrix products, arithmetic and copies ran while one was open for 0% of the time, Pallas kernels for 10%

profile of v2, /device:TPU:4, one launch (start us, length us, event | category | flops | bytes accessed | tf_op | source)
XLA Modules:
  0.0 90.2 jit_solution(17883964512678685781)
XLA Ops:
  0.6 0.0 copy-start
  0.6 0.0 copy-start.1
  0.7 0.0 copy-start.4
  0.7 6.9 %features.1 = (bf16[8,2048,128]{2,1,0:T(8,128)(2,1)S(1)}, bf16[2048,128]{1,0:T(8,128)(2,1)S(1)}, bf16[2048,128]{1,0:T(8,128)(2,1)S(1)}, f32[8,128]{1,0:T(8,128)S(1)}) custom-call(bf16[128,8,2048]{2,1,0:T(8,128)(2,1)} %bitcast.7), custom_call_target="tpu_custom_call" | custom-call | tf_op jit(solution)/shard_map/features/pallas_call | solution.py:100
  7.6 0.1 collective-permute-start
  7.7 2.3 %collective-permute-start.1 = (f32[8,128]{1,0:T(8,128)S(1)}, f32[8,128]{1,0:T(8,128)S(1)}, u32[]{:S(2)}, u32[]{:S(2)}) collective-permute-start(f32[8,128]{1,0:T(8,128)S(1)} %get-tuple-element.23.s0.refs_8_), channel_id=1, source_target_pairs={{0,2},{1,3},{2,0},{3,1},{4,6},{5,7},{6,4},{7,5},{8,10},{9,11},{10,... | collective-permute-start | bytes 12296 | tf_op jit(solution)/shard_map/ppermute | solution.py:562
  10.0 1.0 %collective-permute-start.2 = (f32[8,128]{1,0:T(8,128)S(1)}, f32[8,128]{1,0:T(8,128)S(1)}, u32[]{:S(2)}, u32[]{:S(2)}) collective-permute-start(f32[8,128]{1,0:T(8,128)S(1)} %get-tuple-element.23.s0.refs_8_), channel_id=1, source_target_pairs={{0,3},{1,2},{2,1},{3,0},{4,7},{5,6},{6,5},{7,4},{8,11},{9,10},{10,... | collective-permute-start | bytes 12296 | tf_op jit(solution)/shard_map/ppermute | solution.py:562
  11.1 0.4 collective-permute-start.3
  11.4 3.9 %collective-permute-start.4 = (bf16[2048,128]{1,0:T(8,128)(2,1)S(1)}, bf16[2048,128]{1,0:T(8,128)(2,1)S(1)}, u32[]{:S(2)}, u32[]{:S(2)}) collective-permute-start(bf16[2048,128]{1,0:T(8,128)(2,1)S(1)} %get-tuple-element.32), channel_id=1, source_target_pairs={{1,2},{2,1},{5,6},{6,5},{9,10},{10,9},{13,14},{14,13},{17,18},{18,... | collective-permute-start | bytes 1572872 | tf_op jit(solution)/shard_map/ppermute | solution.py:563
  15.3 0.0 copy-done
  15.3 0.0 copy-done.1
  15.4 0.0 copy-done.4
  15.4 0.2 weights.1
  15.6 0.0 collective-permute-done.s1.refs_9_
  15.6 0.0 collective-permute-done.1.s2.refs_10_
  15.6 0.0 collective-permute-done.2.s3.refs_11_
  15.6 5.8 %inner.1 = (bf16[4,2048,128]{2,1,0:T(8,128)(2,1)S(1)}, f32[3,8,128]{2,1,0:T(8,128)S(1)}, bf16[3,2048,128]{2,1,0:T(8,128)(2,1)S(1)}, bf16[3,2048,128]{2,1,0:T(8,1...) custom-call(bf16[8,2048,128]{2,1,0:T(8,128)(2,1)S(1)} %get-tuple-ele, ...), custom_call_target="tpu_custom_call" | custom-call | flops 6442450944 | bytes 4194304 | tf_op jit(solution)/shard_map/inner/pallas_call | solution.py:263
  21.4 0.0 collective-permute-done.3.refs_6_
  21.5 2.0 %collective-permute-done.4.refs_7_ = bf16[2048,128]{1,0:T(8,128)(2,1)S(1)} collective-permute-done((bf16[2048,128]{1,0:T(8,128)(2,1)S(1)}, bf16[2048,128]{1,0:T(8,128)(2,1)S(1)}, u32[]{:S(2)}, u32[]{:S(2)}) %collective-permute-start.4) | collective-permute-done | bytes 524320 | tf_op jit(solution)/shard_map/ppermute | solution.py:563
  23.4 4.4 %outer.1 = (bf16[4,2048,128]{2,1,0:T(8,128)(2,1)S(1)}, bf16[2048,128]{1,0:T(8,128)(2,1)S(1)}, bf16[2048,128]{1,0:T(8,128)(2,1)S(1)}, f32[8,128]{1,0:T(8,128)S(1)}) custom-call(bf16[3,2048,128]{2,1,0:T(8,128)(2,1)S(1)} %get-tuple-element.25.refs_0_, bf16[3,2048,128]{2,1,0:T(8,128)(2,1)S(1)} %get-tuple-element.26.refs_1_, ...), custom_call_target="tpu_custom_call" | custom-call | tf_op jit(solution)/shard_map/outer/pallas_call | solution.py:329
  27.8 0.1 collective-permute-start.7
  27.9 2.4 %collective-permute-start.8 = (f32[8,128]{1,0:T(8,128)S(1)}, f32[8,128]{1,0:T(8,128)S(1)}, u32[]{:S(2)}, u32[]{:S(2)}) collective-permute-start(f32[8,128]{1,0:T(8,128)S(1)} %get-tuple-element.36.s0), channel_id=1, source_target_pairs={{0,2},{1,3},{2,0},{3,1},{4,6},{5,7},{6,4},{7,5},{8,10},{9,11},{10,... | collective-permute-start | bytes 12296 | tf_op jit(solution)/shard_map/ppermute | solution.py:562
  30.3 1.0 %collective-permute-start.9 = (f32[8,128]{1,0:T(8,128)S(1)}, f32[8,128]{1,0:T(8,128)S(1)}, u32[]{:S(2)}, u32[]{:S(2)}) collective-permute-start(f32[8,128]{1,0:T(8,128)S(1)} %get-tuple-element.36.s0), channel_id=1, source_target_pairs={{0,3},{1,2},{2,1},{3,0},{4,7},{5,6},{6,5},{7,4},{8,11},{9,10},{10,... | collective-permute-start | bytes 12296 | tf_op jit(solution)/shard_map/ppermute | solution.py:562
  31.9 0.6 collective-permute-start.5
  32.6 3.8 %collective-permute-start.6 = (bf16[2048,128]{1,0:T(8,128)(2,1)S(1)}, bf16[2048,128]{1,0:T(8,128)(2,1)S(1)}, u32[]{:S(2)}, u32[]{:S(2)}) collective-permute-start(bf16[2048,128]{1,0:T(8,128)(2,1)S(1)} %get-tuple-element.35), channel_id=1, source_target_pairs={{1,2},{2,1},{5,6},{6,5},{9,10},{10,9},{13,14},{14,13},{17,18},{18,... | collective-permute-start | bytes 1572872 | tf_op jit(solution)/shard_map/ppermute | solution.py:563
  36.4 0.0 collective-permute-done.7.s1
  36.4 0.0 collective-permute-done.8.s2
  36.4 0.0 collective-permute-done.9.s3
  36.4 0.0 copy-start.2
  36.4 0.0 copy-start.3
  36.5 3.1 %taps.1.sum_ref = f32[8,24,2048]{2,1,0:T(8,128)S(1)} custom-call(bf16[8,2048,128]{2,1,0:T(8,128)(2,1)S(1)} %get-tuple-element.22.x_ref, bf16[4,2048,128]{2,1,0:T(8,128)(2,1)S(1)} %get-tuple-element.38.mid_ref, bf16[4,2048,128]{2,1,0:T(8,128)(2,1)S(1)} %get-tuple-element.39.rim_ref, f32[8,128]{1,0:T(8,128)S(1)} %get-tuple-element.36.s0, ...), custom_call_target="tpu_custom_call" | custom-call | flops 6442450944 | bytes 4194304 | tf_op jit(solution)/shard_map/taps/pallas_call | solution.py:402
  39.5 0.0 collective-permute-done.5.core_ref
  39.6 5.0 %collective-permute-done.6.far_ref = bf16[2048,128]{1,0:T(8,128)(2,1)S(1)} collective-permute-done((bf16[2048,128]{1,0:T(8,128)(2,1)S(1)}, bf16[2048,128]{1,0:T(8,128)(2,1)S(1)}, u32[]{:S(2)}, u32[]{:S(2)}) %collective-permute-start.6) | collective-permute-done | bytes 524320 | tf_op jit(solution)/shard_map/ppermute | solution.py:563
  44.6 0.0 copy-done.2
  44.6 0.0 copy-done.3
  44.6 2.6 %step.1 = (f32[4,8,2048]{2,1,0:T(8,128)}, f32[16,4,8,128]{3,2,1,0:T(8,128)}) custom-call(bf16[2048,128]{1,0:T(8,128)(2,1)S(1)} %collective-permute-done.5.core_ref, bf16[2048,128]{1,0:T(8,128)(2,1)S(1)} %collective-permute-done.6.far_ref, f32[8,128]{1,0:T(8,128)S(1)} %get-tuple-element.36.s0, f32[8,128]{1,0:T(8,128)S(1)} %collective-permute-done.7.s1, ...), custom_call_target="tpu_custom_call" | custom-call | tf_op jit(solution)/shard_map/step/pallas_call | solution.py:472
  47.1 6.6 %all-to-all-start = ((f32[16,4,8,128]{3,2,1,0:T(8,128)}), f32[16,4,8,128]{3,2,1,0:T(8,128)S(1)}, u32[]{:S(2)}, u32[]{:S(2)}) async-start(f32[16,4,8,128]{3,2,1,0:T(8,128)} %get-tuple-element.40.blocks_ref), calls=%async_computation | async-start | bytes 524288 | tf_op jit(solution)/shard_map/all_to_all | solution.py:585
  53.7 0.0 copy-done.6
  53.8 0.1 tile.10.reg_ref
  53.8 7.7 %all-to-all-done.got_ref = f32[16,4,8,128]{3,2,1,0:T(8,128)S(1)} async-done(((f32[16,4,8,128]{3,2,1,0:T(8,128)}), f32[16,4,8,128]{3,2,1,0:T(8,128)S(1)}, u32[]{:S(2)}, u32[]{:S(2)}) %all-to-all-start) | async-done | bytes 262176 | tf_op jit(solution)/shard_map/all_to_all | solution.py:585
  61.6 3.4 %collective-permute-start.10 = (f32[3,4,8,128]{3,2,1,0:T(8,128)S(1)}, f32[3,4,8,128]{3,2,1,0:T(8,128)S(1)}, u32[]{:S(2)}, u32[]{:S(2)}) collective-permute-start(f32[3,4,8,128]{3,2,1,0:T(8,128)S(1)} %sums.1), channel_id=1, source_target_pairs={{0,64},{4,68},{8,72},{12,76},{16,80},{20,84},{24,88},{28,92},{32,9... | collective-permute-start | bytes 147464 | tf_op jit(solution)/shard_map/ppermute | solution.py:588
  65.0 2.6 %collective-permute-done.10 = f32[3,4,8,128]{3,2,1,0:T(8,128)S(1)} collective-permute-done((f32[3,4,8,128]{3,2,1,0:T(8,128)S(1)}, f32[3,4,8,128]{3,2,1,0:T(8,128)S(1)}, u32[]{:S(2)}, u32[]{:S(2)}) %collective-permute-start.10) | collective-permute-done | bytes 49184 | tf_op jit(solution)/shard_map/ppermute | solution.py:588
  67.6 4.6 %collective-permute-start.11 = (f32[3,4,8,128]{3,2,1,0:T(8,128)S(1)}, f32[3,4,8,128]{3,2,1,0:T(8,128)S(1)}, u32[]{:S(2)}, u32[]{:S(2)}) collective-permute-start(f32[3,4,8,128]{3,2,1,0:T(8,128)S(1)} %add.3.one_ref), channel_id=1, source_target_pairs={{0,192},{4,196},{8,200},{12,204},{16,208},{20,212},{24,216},{28,22... | collective-permute-start | bytes 147464 | tf_op jit(solution)/shard_map/ppermute | solution.py:589
  72.2 2.7 %collective-permute-done.11.two_ref = f32[3,4,8,128]{3,2,1,0:T(8,128)S(1)} collective-permute-done((f32[3,4,8,128]{3,2,1,0:T(8,128)S(1)}, f32[3,4,8,128]{3,2,1,0:T(8,128)S(1)}, u32[]{:S(2)}, u32[]{:S(2)}) %collective-permute-start.11) | collective-permute-done | bytes 49184 | tf_op jit(solution)/shard_map/ppermute | solution.py:589
  74.8 0.0 copy-done.5
  74.8 0.6 spread.1
  75.5 12.8 %all_to_all.10.got_ref = f32[16,2,4,8,128]{4,3,2,1,0:T(8,128)S(1)} all-to-all(f32[16,2,4,8,128]{4,3,2,1,0:T(8,128)S(1)} %spread.1), channel_id=1, replica_groups={{0,4,8,12,16,20,24,28,32,36,40,44,48,52,56,60},{64,68,72,76,80,84,88,92..., dimensions={0} | all-to-all | bytes 1048576 | tf_op jit(solution)/shard_map/all_to_all | solution.py:591
  88.2 1.9 %field.1 = f32[4,8,2048]{2,1,0:T(8,128)} custom-call(f32[16,4,8,128]{3,2,1,0:T(8,128)} %get-tuple-element.40.blocks_ref, f32[16,2,4,8,128]{4,3,2,1,0:T(8,128)S(1)} %all_to_all.10.got_ref), custom_call_target="tpu_custom_call" | custom-call | tf_op jit(solution)/shard_map/field/pallas_call | solution.py:550
  (5 shorter events, 0.1 us)
Async XLA Ops:
  0.6 14.7 %copy-start = (bf16[9,128,128]{2,1,0:T(8,128)(2,1)S(1)}, bf16[9,128,128]{2,1,0:T(8,128)(2,1)}, u32[]{:S(2)}) copy-start(bf16[9,128,128]{2,1,0:T(8,128)(2,1)} %first_ref.1) | copy-start | bytes 884740
  0.6 14.7 %copy-start.1 = (bf16[9,128,128]{2,1,0:T(8,128)(2,1)S(1)}, bf16[9,128,128]{2,1,0:T(8,128)(2,1)}, u32[]{:S(2)}) copy-start(bf16[9,128,128]{2,1,0:T(8,128)(2,1)} %second_ref.1) | copy-start | bytes 884740
  0.7 14.7 %copy-start.4 = (bf16[4,128]{1,0:T(4,128)(2,1)S(1)}, bf16[4,128]{1,0:T(4,128)(2,1)}, u32[]{:S(2)}) copy-start(bf16[4,128]{1,0:T(4,128)(2,1)} %head_ref.3) | copy-start | bytes 3076
  7.6 8.0 %collective-permute-start = (f32[8,128]{1,0:T(8,128)S(1)}, f32[8,128]{1,0:T(8,128)S(1)}, u32[]{:S(2)}, u32[]{:S(2)}) collective-permute-start(f32[8,128]{1,0:T(8,128)S(1)} %get-tuple-element.23.s0.refs_8_), channel_id=1, source_target_pairs={{0,1},{1,0},{2,3},{3,2},{4,5},{5,4},{6,7},{7,6},{8,9},{9,8},{10,11... | collective-permute-start | bytes 12296 | tf_op jit(solution)/shard_map/ppermute | solution.py:562
  7.7 7.9 %collective-permute-start.1 = (f32[8,128]{1,0:T(8,128)S(1)}, f32[8,128]{1,0:T(8,128)S(1)}, u32[]{:S(2)}, u32[]{:S(2)}) collective-permute-start(f32[8,128]{1,0:T(8,128)S(1)} %get-tuple-element.23.s0.refs_8_), channel_id=1, source_target_pairs={{0,2},{1,3},{2,0},{3,1},{4,6},{5,7},{6,4},{7,5},{8,10},{9,11},{10,... | collective-permute-start | bytes 12296 | tf_op jit(solution)/shard_map/ppermute | solution.py:562
  10.0 5.6 %collective-permute-start.2 = (f32[8,128]{1,0:T(8,128)S(1)}, f32[8,128]{1,0:T(8,128)S(1)}, u32[]{:S(2)}, u32[]{:S(2)}) collective-permute-start(f32[8,128]{1,0:T(8,128)S(1)} %get-tuple-element.23.s0.refs_8_), channel_id=1, source_target_pairs={{0,3},{1,2},{2,1},{3,0},{4,7},{5,6},{6,5},{7,4},{8,11},{9,10},{10,... | collective-permute-start | bytes 12296 | tf_op jit(solution)/shard_map/ppermute | solution.py:562
  11.1 10.4 %collective-permute-start.3 = (bf16[2048,128]{1,0:T(8,128)(2,1)S(1)}, bf16[2048,128]{1,0:T(8,128)(2,1)S(1)}, u32[]{:S(2)}, u32[]{:S(2)}) collective-permute-start(bf16[2048,128]{1,0:T(8,128)(2,1)S(1)} %get-tuple-element.31), channel_id=1, source_target_pairs={{0,1},{1,0},{2,3},{3,2},{4,5},{5,4},{6,7},{7,6},{8,9},{9,8},{10,11... | collective-permute-start | bytes 1572872 | tf_op jit(solution)/shard_map/ppermute | solution.py:564
  11.4 12.0 %collective-permute-start.4 = (bf16[2048,128]{1,0:T(8,128)(2,1)S(1)}, bf16[2048,128]{1,0:T(8,128)(2,1)S(1)}, u32[]{:S(2)}, u32[]{:S(2)}) collective-permute-start(bf16[2048,128]{1,0:T(8,128)(2,1)S(1)} %get-tuple-element.32), channel_id=1, source_target_pairs={{1,2},{2,1},{5,6},{6,5},{9,10},{10,9},{13,14},{14,13},{17,18},{18,... | collective-permute-start | bytes 1572872 | tf_op jit(solution)/shard_map/ppermute | solution.py:563
  27.8 8.6 %collective-permute-start.7 = (f32[8,128]{1,0:T(8,128)S(1)}, f32[8,128]{1,0:T(8,128)S(1)}, u32[]{:S(2)}, u32[]{:S(2)}) collective-permute-start(f32[8,128]{1,0:T(8,128)S(1)} %get-tuple-element.36.s0), channel_id=1, source_target_pairs={{0,1},{1,0},{2,3},{3,2},{4,5},{5,4},{6,7},{7,6},{8,9},{9,8},{10,11... | collective-permute-start | bytes 12296 | tf_op jit(solution)/shard_map/ppermute | solution.py:562
  27.9 8.5 %collective-permute-start.8 = (f32[8,128]{1,0:T(8,128)S(1)}, f32[8,128]{1,0:T(8,128)S(1)}, u32[]{:S(2)}, u32[]{:S(2)}) collective-permute-start(f32[8,128]{1,0:T(8,128)S(1)} %get-tuple-element.36.s0), channel_id=1, source_target_pairs={{0,2},{1,3},{2,0},{3,1},{4,6},{5,7},{6,4},{7,5},{8,10},{9,11},{10,... | collective-permute-start | bytes 12296 | tf_op jit(solution)/shard_map/ppermute | solution.py:562
  30.3 6.1 %collective-permute-start.9 = (f32[8,128]{1,0:T(8,128)S(1)}, f32[8,128]{1,0:T(8,128)S(1)}, u32[]{:S(2)}, u32[]{:S(2)}) collective-permute-start(f32[8,128]{1,0:T(8,128)S(1)} %get-tuple-element.36.s0), channel_id=1, source_target_pairs={{0,3},{1,2},{2,1},{3,0},{4,7},{5,6},{6,5},{7,4},{8,11},{9,10},{10,... | collective-permute-start | bytes 12296 | tf_op jit(solution)/shard_map/ppermute | solution.py:562
  31.9 7.6 %collective-permute-start.5 = (bf16[2048,128]{1,0:T(8,128)(2,1)S(1)}, bf16[2048,128]{1,0:T(8,128)(2,1)S(1)}, u32[]{:S(2)}, u32[]{:S(2)}) collective-permute-start(bf16[2048,128]{1,0:T(8,128)(2,1)S(1)} %get-tuple-element.34), channel_id=1, source_target_pairs={{0,1},{1,0},{2,3},{3,2},{4,5},{5,4},{6,7},{7,6},{8,9},{9,8},{10,11... | collective-permute-start | bytes 1572872 | tf_op jit(solution)/shard_map/ppermute | solution.py:564
  32.6 12.0 %collective-permute-start.6 = (bf16[2048,128]{1,0:T(8,128)(2,1)S(1)}, bf16[2048,128]{1,0:T(8,128)(2,1)S(1)}, u32[]{:S(2)}, u32[]{:S(2)}) collective-permute-start(bf16[2048,128]{1,0:T(8,128)(2,1)S(1)} %get-tuple-element.35), channel_id=1, source_target_pairs={{1,2},{2,1},{5,6},{6,5},{9,10},{10,9},{13,14},{14,13},{17,18},{18,... | collective-permute-start | bytes 1572872 | tf_op jit(solution)/shard_map/ppermute | solution.py:563
  36.4 8.1 %copy-start.2 = (f32[1,4,8,2048]{3,2,1,0:T(8,128)S(1)}, f32[1,4,8,2048]{3,2,1,0:T(8,128)}, u32[]{:S(2)}) copy-start(f32[1,4,8,2048]{3,2,1,0:T(8,128)} %param.10) | copy-start | bytes 786436
  36.4 8.1 %copy-start.3 = (f32[1,4,8,2048]{3,2,1,0:T(8,128)S(1)}, f32[1,4,8,2048]{3,2,1,0:T(8,128)}, u32[]{:S(2)}) copy-start(f32[1,4,8,2048]{3,2,1,0:T(8,128)} %param.11) | copy-start | bytes 786436
  44.6 9.2 %copy-start.6 = (f32[4,8,32]{2,1,0:T(8,128)S(1)}, f32[4,8,32]{2,1,0:T(8,128)}, u32[]{:S(2)}) copy-start(f32[4,8,32]{2,1,0:T(8,128)} %param.12) | copy-start | bytes 12292
  44.6 30.3 %copy-start.5 = (f32[4]{0:T(128)S(1)}, f32[4]{0:T(128)}, u32[]{:S(2)}) copy-start(f32[4]{0:T(128)} %target_ref.1) | copy-start | bytes 52
  47.1 14.4 %all-to-all-start = ((f32[16,4,8,128]{3,2,1,0:T(8,128)}), f32[16,4,8,128]{3,2,1,0:T(8,128)S(1)}, u32[]{:S(2)}, u32[]{:S(2)}) async-start(f32[16,4,8,128]{3,2,1,0:T(8,128)} %get-tuple-element.40.blocks_ref), calls=%async_computation | async-start | bytes 524288 | tf_op jit(solution)/shard_map/all_to_all | solution.py:585
  61.6 5.9 %collective-permute-start.10 = (f32[3,4,8,128]{3,2,1,0:T(8,128)S(1)}, f32[3,4,8,128]{3,2,1,0:T(8,128)S(1)}, u32[]{:S(2)}, u32[]{:S(2)}) collective-permute-start(f32[3,4,8,128]{3,2,1,0:T(8,128)S(1)} %sums.1), channel_id=1, source_target_pairs={{0,64},{4,68},{8,72},{12,76},{16,80},{20,84},{24,88},{28,92},{32,9... | collective-permute-start | bytes 147464 | tf_op jit(solution)/shard_map/ppermute | solution.py:588
  67.6 7.3 %collective-permute-start.11 = (f32[3,4,8,128]{3,2,1,0:T(8,128)S(1)}, f32[3,4,8,128]{3,2,1,0:T(8,128)S(1)}, u32[]{:S(2)}, u32[]{:S(2)}) collective-permute-start(f32[3,4,8,128]{3,2,1,0:T(8,128)S(1)} %add.3.one_ref), channel_id=1, source_target_pairs={{0,192},{4,196},{8,200},{12,204},{16,208},{20,212},{24,216},{28,22... | collective-permute-start | bytes 147464 | tf_op jit(solution)/shard_map/ppermute | solution.py:589

commit v3 on v2

v3 whole, which is shorter than its diff:
```python
import functools

import jax
import jax.numpy as jnp
from jax import lax
from jax.experimental import pallas as pl
from jax.experimental.pallas import tpu as pltpu
from jax.sharding import PartitionSpec as P

GROUP = 4
TILES = 4
F32, BF16 = jnp.float32, jnp.bfloat16
VM = pl.BlockSpec(memory_space=pltpu.VMEM)
SM = pl.BlockSpec(memory_space=pltpu.SMEM)


def limit(mib):
    return pltpu.CompilerParams(vmem_limit_bytes=mib * 1024 * 1024)


def group_total(row):
    lane = lax.broadcasted_iota(jnp.int32, row.shape, 1)
    size = row.shape[1]
    for step in (1, 2):
        up = pltpu.roll(row, step, 1)
        down = pltpu.roll(row, size - step, 1)
        row = row + jnp.where((lane & step) == 0, down, up)
    return row


def merged(parts, count):
    means = [p[0:1, :] for p in parts]
    devs = [p[1:2, :] for p in parts]
    members = len(parts) * GROUP
    mean = group_total(functools.reduce(jnp.add, means)) / members
    spread = functools.reduce(jnp.add, [(m - mean) * (m - mean) for m in means])
    total = group_total(functools.reduce(jnp.add, devs) + count * spread)
    return mean, lax.rsqrt(total / (members * count) + 1e-05)


def silu(values):
    half = 0.5 * values
    return half + half * jnp.tanh(half)


def row_sum(values):
    return values.reshape(-1, 8, values.shape[1]).sum(0)


def write_stats(st_ref, pivot, first, second, count):
    one = jnp.sum(first, axis=0, keepdims=True)
    two = jnp.sum(second, axis=0, keepdims=True)
    mean = pivot + one / count
    dev = two - one * one / count
    pad = jnp.zeros((6, mean.shape[1]), F32)
    st_ref[...] = jnp.concatenate([mean, dev, pad], axis=0)


def features_kernel(x_ref, xt_ref, core_ref, far_ref, st_ref, scr, acc):
    step = pl.program_id(0)
    chans, rows, width = x_ref.shape
    even = (lax.axis_index("tile") & 1) == 0
    for part in range(width // 128):
        at = pl.ds(128 * part, 128)
        scr[part] = x_ref[:, :, at].astype(F32).reshape(chans * rows, 128)
        one = two = jnp.zeros((8, chans), F32)
        for r in range(rows):
            turned = scr[part, pl.ds(r, chans, stride=rows), :].T
            if part == 0 and r == 0:

                @pl.when(step == 0)
                def _():
                    middle = jnp.mean(turned, axis=0, keepdims=True)
                    acc[0] = jnp.broadcast_to(middle, acc.shape[1:])
                    acc[1] = jnp.zeros(acc.shape[1:], F32)
                    acc[2] = jnp.zeros(acc.shape[1:], F32)

            if r == 0:
                pivot = acc[0, 0:1]
            off = turned - pivot
            one = one + row_sum(off)
            two = two + row_sum(off * off)
            turned = turned.astype(BF16)
            xt_ref[jnp.where(even, r, rows - 1 - r), at] = turned
            if r == 0:
                top = turned
        acc[1] += one
        acc[2] += two
        core_ref[at] = jnp.where(even, turned, top)
        far_ref[at] = jnp.where(even, top, turned)

    @pl.when(step == pl.num_programs(0) - 1)
    def _():
        write_stats(st_ref, acc[0, 0:1], acc[1], acc[2], pl.num_programs(0) * rows * width)


def features_call(x, block):
    chans, rows, width = x.shape
    edge = jax.ShapeDtypeStruct((width, chans), BF16)
    return pl.pallas_call(
        features_kernel,
        grid=(width // block,),
        out_shape=(
            jax.ShapeDtypeStruct((rows, width, chans), BF16),
            edge,
            edge,
            jax.ShapeDtypeStruct((8, chans), F32),
        ),
        in_specs=[pl.BlockSpec((chans, rows, block), lambda i: (0, 0, i))],
        out_specs=(
            pl.BlockSpec((rows, block, chans), lambda i: (0, i, 0)),
            pl.BlockSpec((block, chans), lambda i: (i, 0)),
            pl.BlockSpec((block, chans), lambda i: (i, 0)),
            pl.BlockSpec((8, chans), lambda i: (0, 0)),
        ),
        scratch_shapes=[
            pltpu.VMEM((block // 128, chans * rows, 128), F32),
            pltpu.VMEM((3, 8, chans), F32),
        ],
        compiler_params=limit(16),
        name="features",
    )(x)


def step_factors(index):
    lane = lax.broadcasted_iota(jnp.int32, (8, 128), 1)
    steps = lane.astype(F32)
    upper = 800.0 ** (1.0 / 7.0)
    lower = 0.002 ** (1.0 / 7.0)
    root = upper + steps / 17.0 * (lower - upper)
    square = root * root
    sigmas = square * square * square * root
    sigma = jnp.sum(jnp.where(lane == index, sigmas, 0.0), axis=1, keepdims=True)
    follow = jnp.sum(jnp.where(lane == index + 1, sigmas, 0.0), axis=1, keepdims=True)
    sigma, follow = jnp.broadcast_to(sigma, lane.shape), jnp.broadcast_to(follow, lane.shape)
    hat = 1.25 * sigma
    spread = hat * hat + 0.25
    skip = 0.25 / spread
    gain = 0.5 * hat / jnp.sqrt(spread)
    rate = (follow - hat) / hat
    keep = 1.0 + rate - rate * skip
    return keep, keep * jnp.sqrt(hat * hat - sigma * sigma), -rate * gain


def place(even, tap):
    return jnp.where(even, tap, 3 * (2 - tap // 3) + tap % 3)


def weights_kernel(first_ref, second_ref, head_ref, wt_ref, fold_ref):
    chans = first_ref.shape[1]
    even = (lax.axis_index("tile") & 1) == 0
    wt_ref[...] = jnp.zeros(wt_ref.shape, BF16)
    for tap in range(9):
        turned = first_ref[place(even, tap)].astype(F32).T.astype(BF16)
        for q in range(2):
            row, col = tap // 3 + q, tap % 3
            wt_ref[pl.ds((3 * row + col) * chans, chans), pl.ds(q * chans, chans)] = turned
    head = jnp.concatenate([head_ref[...].astype(F32)] * 2, axis=0).astype(BF16)
    low = lax.broadcasted_iota(jnp.int32, (8, chans), 0) >= 4
    lines = []
    for row in range(3):
        parts = []
        for col in range(3):
            tap = second_ref[place(even, 3 * row + col)]
            folded = jnp.dot(head, tap, preferred_element_type=F32)
            high = folded.astype(BF16).astype(F32)
            parts.append(jnp.where(low, folded - high, high))
        lines.append(jnp.concatenate(parts, axis=0))
    none = jnp.zeros_like(lines[0])
    left = jnp.concatenate([lines[2], lines[1], lines[0], none], axis=0)
    right = jnp.concatenate([none, lines[2], lines[1], lines[0]], axis=0)
    fold_ref[...] = jnp.concatenate([left, right], axis=1).astype(BF16)


def weights_call(first, second, head):
    chans = first.shape[1]
    return pl.pallas_call(
        weights_kernel,
        out_shape=(
            jax.ShapeDtypeStruct((12 * chans, 2 * chans), BF16),
            jax.ShapeDtypeStruct((96, 2 * chans), BF16),
        ),
        in_specs=[VM] * 3,
        out_specs=(VM, VM),
        compiler_params=limit(16),
        cost_estimate=pl.CostEstimate(flops=1 << 22, bytes_accessed=1 << 21, transcendentals=0),
        name="weights",
    )(first, second, head)


def norm_factors(refs, count):
    mean, scale = merged([ref[...] for ref in refs], count)
    return scale, -mean * scale


def fill(act, buf, value, at, size):
    buf[pl.ds(at + 8, size), :] = value
    act[1, pl.ds(at, size), :] = value.astype(BF16)


def fill_sides(act, buf, at, size):
    act[0, pl.ds(at, size), :] = buf[pl.ds(at + 7, size), :].astype(BF16)
    act[2, pl.ds(at, size), :] = buf[pl.ds(at + 9, size), :].astype(BF16)


def clear_ends(buf):
    size, chans = buf.shape
    buf[pl.ds(0, 8), :] = jnp.zeros((8, chans), F32)
    buf[pl.ds(size - 8, 8), :] = jnp.zeros((8, chans), F32)


def two_rows(acts, wt_ref, at, block):
    left = jnp.concatenate([act[s, pl.ds(at, block), :] for act in acts for s in range(3)], axis=1)
    out = jnp.dot(left, wt_ref[...], preferred_element_type=F32)
    chans = out.shape[1] // 2
    return out[:, :chans], out[:, chans:]


def join(acts, wt_ref, hid_ref, lines, block, fresh, carry):
    width = hid_ref.shape[1]
    pivot, one, two = carry
    for at in range(0, width, block):
        a, b = two_rows(acts, wt_ref, at, block)
        for act, buf, read in fresh:
            fill(act, buf, read(at, block), at, block)
            if at > 0:
                fill_sides(act, buf, at - block, block)
        hid_ref[lines[0], pl.ds(at, block), :] = a.astype(BF16)
        hid_ref[lines[1], pl.ds(at, block), :] = b.astype(BF16)
        if pivot is None:
            pivot = jnp.mean(a[0:8], axis=0, keepdims=True)
        a, b = a - pivot, b - pivot
        one = one + row_sum(a + b)
        two = two + row_sum(a * a + b * b)
    for act, buf, read in fresh:
        fill_sides(act, buf, width - block, block)
    return pivot, one, two


def inner_kernel(block, x_ref, core_ref, s0, s1, s2, s3, wt_ref, hid_ref, sum_ref, *rest):
    rows, width, chans = x_ref.shape
    acts, bufs = rest[: rows + 1], rest[rows + 1 :]
    scale, shift = norm_factors([s0, s1, s2, s3], rows * width)
    for buf in bufs:
        clear_ends(buf)

    def line(row):
        def read(at, size):
            span = pl.ds(at, size)
            value = core_ref[span, :] if row == rows else x_ref[row, span, :]
            return silu(value.astype(F32) * scale + shift)

        return acts[row], bufs[row % 2], read

    for row in range(1, 5):
        act, buf, read = line(row)
        fill(act, buf, read(0, width), 0, width)
        fill_sides(act, buf, 0, width)
    zero = jnp.zeros((8, chans), F32)
    carry = (None, zero, zero)
    for pair, fresh in ((0, (5, 6)), (1, (7, 8)), (2, (0,))):
        group = acts[2 * pair + 1 : 2 * pair + 5]
        lines = (2 * pair, 2 * pair + 1)
        carry = join(group, wt_ref, hid_ref, lines, block, [line(row) for row in fresh], carry)
    pivot, one, two = carry
    sum_ref[0] = jnp.broadcast_to(pivot, one.shape)
    sum_ref[1] = one
    sum_ref[2] = two


def inner_call(xt, core, stats, wt, block):
    rows, width, chans = xt.shape
    act = jax.ShapeDtypeStruct((3, width, chans), BF16)
    hid, sums, *acts = pl.pallas_call(
        functools.partial(inner_kernel, block),
        out_shape=(
            jax.ShapeDtypeStruct((rows - 2, width, chans), BF16),
            jax.ShapeDtypeStruct((3, 8, chans), F32),
            act,
            act,
            act,
        ),
        in_specs=[VM] * 7,
        out_specs=(VM,) * 5,
        scratch_shapes=[pltpu.VMEM(act.shape, BF16)] * (rows - 2)
        + [pltpu.VMEM((width + 16, chans), F32)] * 2,
        compiler_params=limit(28),
        cost_estimate=pl.CostEstimate(
            flops=24 * rows * width * chans * chans, bytes_accessed=1 << 22, transcendentals=xt.size
        ),
        name="inner",
    )(xt, core, *stats, wt)
    return hid, sums, acts


def outer_kernel(block, far_ref, a0, a1, a2, s0, s1, s2, s3, sum_ref, wt_ref, hid_ref, st_ref, act, buf):
    width, chans = far_ref.shape
    tile = lax.axis_index("tile")
    linked = ((tile == 1) | (tile == 2)).astype(F32)
    count = TILES * 2 * width
    scale, shift = norm_factors([s0, s1, s2, s3], count)
    clear_ends(buf)
    for at in range(0, width, block):
        value = silu(far_ref[pl.ds(at, block), :].astype(F32) * scale + shift) * linked
        fill(act, buf, value, at, block)
        if at > 0:
            fill_sides(act, buf, at - block, block)
    fill_sides(act, buf, width - block, block)
    carry = (sum_ref[0, 0:1], sum_ref[1], sum_ref[2])
    pivot, one, two = join([act, a0, a1, a2], wt_ref, hid_ref, (0, 1), block, [], carry)
    write_stats(st_ref, pivot, one, two, count)


def outer_call(acts, far, stats, sums, wt, block):
    width, chans = far.shape
    return pl.pallas_call(
        functools.partial(outer_kernel, block),
        out_shape=(
            jax.ShapeDtypeStruct((2, width, chans), BF16),
            jax.ShapeDtypeStruct((8, chans), F32),
        ),
        in_specs=[VM] * 10,
        out_specs=(VM,) * 2,
        scratch_shapes=[pltpu.VMEM((3, width, chans), BF16), pltpu.VMEM((width + 16, chans), F32)],
        compiler_params=limit(12),
        name="outer",
    )(far, *acts, *stats, sums, wt)


def turn_quarters(values, slot):
    low, right = slot < 2, (slot & 1) == 0
    halves = []
    for a, b in ((values[0], values[2]), (values[1], values[3])):
        moved = pltpu.roll(jnp.where(low, b, a), 64, 1)
        halves.append((jnp.where(low, a, moved), jnp.where(low, moved, b)))
    out = [None] * 4
    for k in range(2):
        a, b = halves[0][k], halves[1][k]
        out[2 * k] = jnp.where(right, a, pltpu.roll(b, 32, 1))
        out[2 * k + 1] = jnp.where(right, pltpu.roll(a, 96, 1), b)
    return out


def columns_joined(total):
    width = total.shape[1]
    lane = lax.broadcasted_iota(jnp.int32, (8, width), 1)
    left = jnp.where(lane == 0, 0.0, pltpu.roll(total[0:8], 1, 1))
    right = jnp.where(lane == width - 1, 0.0, pltpu.roll(total[16:24], width - 1, 1))
    both = left + total[8:16] + right
    return both[0:4] + both[4:8]


def product(left, right):
    return lax.dot_general(left, right, (((1,), (1,)), ((), ())), preferred_element_type=F32)


def rim_kernel(first_ref, last_ref, s0, s1, s2, s3, fold_ref, core_ref, far_ref, act):
    width, chans = act.shape[0], act.shape[1] // 2
    scale, shift = norm_factors([s0, s1, s2, s3], TILES * 2 * width)
    value = silu(first_ref[0].astype(F32) * scale + shift)
    act[:, pl.ds(0, chans)] = value.astype(BF16)
    value = silu(last_ref[last_ref.shape[0] - 1].astype(F32) * scale + shift)
    act[:, pl.ds(chans, chans)] = value.astype(BF16)
    none = jnp.zeros((24, chans), BF16)
    before = jnp.concatenate([fold_ref[0:24, :chans], none], axis=1)
    after = jnp.concatenate([none, fold_ref[72:96, chans:]], axis=1)
    ends = product(jnp.concatenate([before, after], axis=0), act[...])
    far_ref[...] = columns_joined(ends[0:24])
    core_ref[...] = columns_joined(ends[24:48])


def rim_call(first, last, stats, fold):
    width, chans = first.shape[1:]
    part = jax.ShapeDtypeStruct((4, width), F32)
    return pl.pallas_call(
        rim_kernel,
        out_shape=(part, part),
        in_specs=[VM] * 7,
        out_specs=(VM, VM),
        scratch_shapes=[pltpu.VMEM((width, 2 * chans), BF16)],
        compiler_params=limit(8),
        name="rim",
    )(first, last, *stats, fold)


def taps_kernel(
    x_ref, first_ref, last_ref, s0, s1, s2, s3, fold_ref, head_ref, state_ref, noise_ref, index_ref, out_ref, *rest
):
    rows, width, chans = x_ref.shape
    outs = state_ref.shape[0]
    half = rows // 2
    acts, taps, net = rest[:half], rest[half], rest[half + 1]
    even = (lax.axis_index("tile") & 1) == 0
    scale, shift = norm_factors([s0, s1, s2, s3], rows * width)
    head = head_ref[...].astype(F32)
    head = jnp.concatenate([head, jnp.zeros_like(head)], axis=0)
    none = jnp.zeros_like(head)
    head = jnp.concatenate(
        [jnp.concatenate([head, none], axis=1), jnp.concatenate([none, head], axis=1)], axis=0
    ).astype(BF16)
    direct = []
    for pair in range(half):
        features = jnp.concatenate([x_ref[2 * pair], x_ref[2 * pair + 1]], axis=1)
        direct.append(product(head, features))
        for side in range(2):
            row = 2 * pair + side
            value = first_ref[row] if row < 2 else last_ref[row - 2]
            value = silu(value.astype(F32) * scale + shift)
            acts[pair][:, pl.ds(side * chans, chans)] = value.astype(BF16)
        taps[pair] = product(fold_ref[...], acts[pair][...])
    for r in range(rows):
        pair, side = r // 2, r % 2
        total = taps[pair, 24 + 24 * side : 48 + 24 * side]
        if side == 0 and pair > 0:
            total = total + taps[pair - 1, 72:96]
        if side == 1 and pair + 1 < half:
            total = total + taps[pair + 1, 0:24]
        both = columns_joined(total) + direct[pair][8 * side : 8 * side + 4]
        for o in range(outs):
            net[o, pl.ds(jnp.where(even, r, rows - 1 - r), 1), :] = both[o : o + 1]
    keep, stir, push = step_factors(index_ref[0])
    for t in range(width // 128):
        at = pl.ds(t * 128, 128)
        for o in range(outs):
            direct = keep * state_ref[o, :, at] + stir * noise_ref[o, :, at]
            out_ref[o, :, at] = direct + push * net[o, :, at]


def taps_call(xt, first, last, stats, fold, head, state, noise, index):
    rows, width, chans = xt.shape
    half = rows // 2
    return pl.pallas_call(
        taps_kernel,
        out_shape=jax.ShapeDtypeStruct(state.shape, F32),
        in_specs=[VM] * 11 + [SM],
        out_specs=VM,
        scratch_shapes=[pltpu.VMEM((width, 2 * chans), BF16)] * half
        + [pltpu.VMEM((half, 96, width), F32), pltpu.VMEM(state.shape, F32)],
        compiler_params=limit(24),
        cost_estimate=pl.CostEstimate(
            flops=6144 * width * chans * half, bytes_accessed=1 << 22, transcendentals=2 * xt.size
        ),
        name="taps",
    )(xt, first, last, *stats, fold, head, state, noise, index)


def step_kernel(part_ref, core_ref, far_ref, index_ref, next_ref, blocks_ref):
    outs, rows, width = part_ref.shape
    even = (lax.axis_index("tile") & 1) == 0
    push = step_factors(index_ref[0])[2]
    quarter = width // 512
    line = lax.broadcasted_iota(jnp.int32, (rows, 128), 0)
    at_far = line == jnp.where(even, 0, rows - 1)
    at_core = line == jnp.where(even, rows - 1, 0)
    slot = lax.broadcasted_iota(jnp.int32, (rows, 128), 1) // 32
    for t in range(quarter):
        for o in range(outs):
            values = []
            for k in range(4):
                at = pl.ds((quarter * k + t) * 128, 128)
                extra = jnp.where(at_far, far_ref[o : o + 1, at], 0.0)
                extra = jnp.where(at_core, core_ref[o : o + 1, at], extra)
                values.append(part_ref[o, :, at] + push * extra)
                next_ref[o, :, at] = values[-1]
            for j, mixed in enumerate(turn_quarters(values, slot)):
                blocks_ref[4 * t + j, o] = mixed


def step_call(part, core, far, index):
    outs, rows, width = part.shape
    return pl.pallas_call(
        step_kernel,
        out_shape=(
            jax.ShapeDtypeStruct(part.shape, F32),
            jax.ShapeDtypeStruct((width // 128, outs, rows, 128), F32),
        ),
        in_specs=[VM] * 3 + [SM],
        out_specs=(VM, VM),
        compiler_params=limit(8),
        name="step",
    )(part, core, far, index)


def sums_kernel(got_ref, reg_ref, out_ref):
    count = got_ref.shape[0]
    shape = got_ref.shape[2:]
    own = lax.broadcasted_iota(jnp.int32, shape, 1) // 32 == lax.axis_index("member") // count
    for o in range(got_ref.shape[1]):
        first = got_ref[0, o]
        second = first * first
        for m in range(1, count):
            value = got_ref[m, o]
            first = first + value
            second = second + value * value
        out_ref[0, o] = first
        out_ref[1, o] = second
        out_ref[2, o] = jnp.where(own, reg_ref[o], 0.0)


def sums_call(got, reg):
    return pl.pallas_call(
        sums_kernel,
        out_shape=jax.ShapeDtypeStruct((3,) + got.shape[1:], F32),
        in_specs=[VM, VM],
        out_specs=VM,
        compiler_params=limit(8),
        name="sums",
    )(got, reg)


def spread_kernel(members, one_ref, two_ref, target_ref, out_ref):
    copies, _, outs = out_ref.shape[:3]
    for o in range(outs):
        mean = (one_ref[0, o] + two_ref[0, o]) / members
        var = (one_ref[1, o] + two_ref[1, o]) / members - mean * mean
        scale = jnp.sqrt(1.0 + target_ref[o] / (var + 1.0))
        offset = one_ref[2, o] + two_ref[2, o] + mean - mean * scale
        for k in range(copies):
            out_ref[k, 0, o] = scale
            out_ref[k, 1, o] = offset


def spread_call(one, two, target, copies, members):
    return pl.pallas_call(
        functools.partial(spread_kernel, members),
        out_shape=jax.ShapeDtypeStruct((copies, 2) + one.shape[1:], F32),
        in_specs=[VM, VM, SM],
        out_specs=VM,
        compiler_params=limit(8),
        name="spread",
    )(one, two, target)


def field_kernel(blocks_ref, got_ref, out_ref):
    outs, rows, width = out_ref.shape
    quarter = width // 512
    slot = lax.broadcasted_iota(jnp.int32, (rows, 128), 1) // 32
    for t in range(quarter):
        for o in range(outs):
            values = [
                blocks_ref[4 * t + j, o] * got_ref[4 * t + j, 0, o] + got_ref[4 * t + j, 1, o] for j in range(4)
            ]
            for k, mixed in enumerate(turn_quarters(values, slot)):
                out_ref[o, :, pl.ds((quarter * k + t) * 128, 128)] = mixed


def field_call(blocks, got, shape):
    return pl.pallas_call(
        field_kernel,
        out_shape=jax.ShapeDtypeStruct(shape, F32),
        in_specs=[VM, VM],
        out_specs=VM,
        compiler_params=limit(8),
        name="field",
    )(blocks, got)


def swap(value, bits):
    return lax.ppermute(value, "tile", [(i, i ^ bits) for i in range(TILES)])


def far_swap(value):
    return lax.ppermute(value, "tile", [(1, 2), (2, 1)])


def spread_stats(stats):
    return [stats] + [swap(stats, bits) for bits in (1, 2, 3)]


def shards(
    features, residual_state, noise, regression_mean, step_index, conv_first, conv_second, head_weight, spread_target
):
    member = pltpu.with_memory_space_constraint(features[0], pltpu.HBM)
    xt, core, far, stats = features_call(member, 256)
    stats = spread_stats(stats)
    core, far = swap(core, 1), far_swap(far)
    wt, fold = weights_call(conv_first, conv_second, head_weight)
    last, sums, acts = inner_call(xt, core, stats, wt, 1024)
    first, stats = outer_call(acts, far, stats, sums, wt, 1024)
    stats = spread_stats(stats)
    core, far = rim_call(first, last, stats, fold)
    core, far = swap(core, 1), far_swap(far)
    part = taps_call(
        xt, first, last, stats, fold, head_weight, residual_state[0], noise[0], step_index
    )
    advanced, blocks = step_call(part, core, far, step_index)
    members = lax.axis_size("member")
    size = blocks.shape[0]
    runs = [list(range(i, i + size)) for i in range(0, members, size)]
    got = lax.all_to_all(blocks, "member", 0, 0, tiled=True, axis_index_groups=runs)
    reg = jnp.tile(regression_mean, (1, 1, 4))
    sums = sums_call(got, reg)
    sums = sums + lax.ppermute(sums, "member", [(i, i ^ size) for i in range(members)])
    other = lax.ppermute(sums, "member", [(i, i ^ (3 * size)) for i in range(members)])
    sent = spread_call(sums, other, spread_target, size, members)
    got = lax.all_to_all(sent, "member", 0, 0, tiled=True, axis_index_groups=runs)
    field = field_call(blocks, got, advanced.shape)
    return (field[None], advanced[None])


def solution(mesh):
    cells = P("member", None, "tile", None)
    return jax.shard_map(
        shards,
        mesh=mesh,
        in_specs=(cells, cells, cells, P(None, "tile", "member"), P(), P(), P(), P(), P()),
        out_specs=(cells, cells),
        check_vma=False,
    )
```

time: 90.6 us -> 85.2 us (0.940)
  the two profiles are of different devices: /device:TPU:4 before, /device:TPU:1 now
where the time goes in v3:
time: 85.2 us; the launch traced here: 84.8 us
  starting transfers between devices  30.2 us (35%)
  Pallas kernels  24.6 us (29%)
  waiting for transfers between devices  14.2 us (17%)
  blocking collectives  14.1 us (17%)
  between operations  1.54 us (2%)
    all_to_all x1, blocking collectives, shards(): lax.all_to_all(sent, 'member', 0, 0, tiled=True, axis_index_groups=runs)  14.1 us
    ppermute x8, starting transfers between devices, swap(): return lax.ppermute(value, 'tile', [(i, i ^ bits) for i in range(TILES)])  11.1 us
    ppermute x2, starting transfers between devices, far_swap(): return lax.ppermute(value, 'tile', [(1, 2), (2, 1)])  7.1 us
    pallas_call x1, Pallas kernels, features_call(): pl.pallas_call(features_kernel, grid=(width // block,), out_shape=(jax.Sh...  6.93 us
    pallas_call x1, Pallas kernels, inner_call(): pl.pallas_call(functools.partial(inner_kernel, block), out_shape=(jax.Sha...  6.84 us
    all_to_all x1, waiting for transfers between devices, shards(): lax.all_to_all(blocks, 'member', 0, 0, tiled=True, axis_index_groups=runs)  6.58 us
    all_to_all x1, starting transfers between devices, shards(): lax.all_to_all(blocks, 'member', 0, 0, tiled=True, axis_index_groups=runs)  4.84 us
    ppermute x1, starting transfers between devices, shards(): lax.ppermute(sums, 'member', [(i, i ^ 3 * size) for i in range(members)])  4.05 us
  transfers between devices with their start and end apart: 13, of which 5 were waited for; matrix products, arithmetic and copies ran while one was open for 0% of the time, Pallas kernels for 12%

profile of v3, /device:TPU:1, one launch (start us, length us, event | category | flops | bytes accessed | tf_op | source)
XLA Modules:
  0.0 84.8 jit_solution(13905164057753745051)
XLA Ops:
  0.6 0.0 copy-start
  0.6 0.0 copy-start.1
  0.7 0.0 copy-start.2
  0.7 6.9 %features.1 = (bf16[8,2048,128]{2,1,0:T(8,128)(2,1)S(1)}, bf16[2048,128]{1,0:T(8,128)(2,1)S(1)}, bf16[2048,128]{1,0:T(8,128)(2,1)S(1)}, f32[8,128]{1,0:T(8,128)S(1)}) custom-call(bf16[128,8,2048]{2,1,0:T(8,128)(2,1)} %bitcast.7), custom_call_target="tpu_custom_call" | custom-call | tf_op jit(solution)/shard_map/features/pallas_call | solution.py:100
  7.6 3.3 %collective-permute-start.1 = (bf16[2048,128]{1,0:T(8,128)(2,1)S(1)}, bf16[2048,128]{1,0:T(8,128)(2,1)S(1)}, u32[]{:S(2)}, u32[]{:S(2)}) collective-permute-start(bf16[2048,128]{1,0:T(8,128)(2,1)S(1)} %get-tuple-element.21), channel_id=1, source_target_pairs={{0,1},{1,0},{2,3},{3,2},{4,5},{5,4},{6,7},{7,6},{8,9},{9,8},{10,11... | collective-permute-start | bytes 1572872 | tf_op jit(solution)/shard_map/ppermute | solution.py:559
  10.9 0.1 collective-permute-start.2
  11.0 1.0 %collective-permute-start.3 = (f32[8,128]{1,0:T(8,128)S(1)}, f32[8,128]{1,0:T(8,128)S(1)}, u32[]{:S(2)}, u32[]{:S(2)}) collective-permute-start(f32[8,128]{1,0:T(8,128)S(1)} %get-tuple-element.22.s0), channel_id=1, source_target_pairs={{0,2},{1,3},{2,0},{3,1},{4,6},{5,7},{6,4},{7,5},{8,10},{9,11},{10,... | collective-permute-start | bytes 12296 | tf_op jit(solution)/shard_map/ppermute | solution.py:559
  12.0 2.5 %collective-permute-start.4 = (f32[8,128]{1,0:T(8,128)S(1)}, f32[8,128]{1,0:T(8,128)S(1)}, u32[]{:S(2)}, u32[]{:S(2)}) collective-permute-start(f32[8,128]{1,0:T(8,128)S(1)} %get-tuple-element.22.s0), channel_id=1, source_target_pairs={{0,3},{1,2},{2,1},{3,0},{4,7},{5,6},{6,5},{7,4},{8,11},{9,10},{10,... | collective-permute-start | bytes 12296 | tf_op jit(solution)/shard_map/ppermute | solution.py:559
  14.6 2.6 %collective-permute-start = (bf16[2048,128]{1,0:T(8,128)(2,1)S(1)}, bf16[2048,128]{1,0:T(8,128)(2,1)S(1)}, u32[]{:S(2)}, u32[]{:S(2)}) collective-permute-start(bf16[2048,128]{1,0:T(8,128)(2,1)S(1)} %get-tuple-element.20), channel_id=1, source_target_pairs={{1,2},{2,1},{5,6},{6,5},{9,10},{10,9},{13,14},{14,13},{17,18},{18,... | collective-permute-start | bytes 1572872 | tf_op jit(solution)/shard_map/ppermute | solution.py:563
  17.2 0.0 copy-done
  17.2 0.0 copy-done.1
  17.2 0.0 copy-done.2
  17.2 0.2 weights.1
  17.4 0.0 collective-permute-done.2.s1
  17.4 0.0 collective-permute-done.3.s2
  17.4 0.0 collective-permute-done.4.s3
  17.5 0.0 collective-permute-done.1.core_ref
  17.5 6.8 %inner.1 = (bf16[6,2048,128]{2,1,0:T(8,128)(2,1)S(1)}, f32[3,8,128]{2,1,0:T(8,128)S(1)}, bf16[3,2048,128]{2,1,0:T(8,128)(2,1)S(1)}, bf16[3,2048,128]{2,1,0:T(8,128)(2,1)S(1)}, bf16[3,2048,128]{2,1,0:T(8,128)(2,1)S(1)}) custom-call(bf16[8,2048,128]{2,1,0:T(8,128)(2,1)S(1)} %get-tuple-element.19.x_ref, bf16[2048,128]{1,0:T(8,128)(2,1)S(1)} %collective-permute-done.1.core_ref, ...), custom_call_target="tpu_custom_call" | custom-call | flops 6442450944 | bytes 4194304 | tf_op jit(solution)/shard_map/inner/pallas_call | solution.py:274
  24.3 2.2 %collective-permute-done.far_ref = bf16[2048,128]{1,0:T(8,128)(2,1)S(1)} collective-permute-done((bf16[2048,128]{1,0:T(8,128)(2,1)S(1)}, bf16[2048,128]{1,0:T(8,128)(2,1)S(1)}, u32[]{:S(2)}, u32[]{:S(2)}) %collective-permute-start) | collective-permute-done | bytes 524320 | tf_op jit(solution)/shard_map/ppermute | solution.py:563
  26.6 2.3 %outer.1 = (bf16[2,2048,128]{2,1,0:T(8,128)(2,1)S(1)}, f32[8,128]{1,0:T(8,128)S(1)}) custom-call(bf16[2048,128]{1,0:T(8,128)(2,1)S(1)} %collective-permute-done.far_ref, bf16[3,2048,128]{2,1,0:T(8,128)(2,1)S(1)} %get-tuple-element.24.a0, bf16[3,2048,128]{2,1,0:T(8,128)(2,1)S(1)} %get-tuple-element.25.a1, bf16[3,2048,128]{2,1,0:T(8,128)(2,1)S(1)} %get-tuple-element.26.a2, ...), custom_call_target="tpu_custom_call" | custom-call | tf_op jit(solution)/shard_map/outer/pallas_call | solution.py:316
  28.9 0.0 copy-start.4
  28.9 0.0 copy-start.5
  28.9 0.1 collective-permute-start.5
  29.0 0.8 collective-permute-start.6
  29.9 2.8 %collective-permute-start.7 = (f32[8,128]{1,0:T(8,128)S(1)}, f32[8,128]{1,0:T(8,128)S(1)}, u32[]{:S(2)}, u32[]{:S(2)}) collective-permute-start(f32[8,128]{1,0:T(8,128)S(1)} %get-tuple-element.30.s0), channel_id=1, source_target_pairs={{0,3},{1,2},{2,1},{3,0},{4,7},{5,6},{6,5},{7,4},{8,11},{9,10},{10,... | collective-permute-start | bytes 12296 | tf_op jit(solution)/shard_map/ppermute | solution.py:559
  33.3 0.0 collective-permute-done.5.s1
  33.3 0.0 collective-permute-done.6.s2
  33.3 1.1 %collective-permute-done.7.s3 = f32[8,128]{1,0:T(8,128)S(1)} collective-permute-done((f32[8,128]{1,0:T(8,128)S(1)}, f32[8,128]{1,0:T(8,128)S(1)}, u32[]{:S(2)}, u32[]{:S(2)}) %collective-permute-start.7) | collective-permute-done | bytes 4128 | tf_op jit(solution)/shard_map/ppermute | solution.py:559
  34.4 1.3 %rim.1 = (f32[4,2048]{1,0:T(4,128)S(1)}, f32[4,2048]{1,0:T(4,128)S(1)}) custom-call(bf16[2,2048,128]{2,1,0:T(8,128)(2,1)S(1)} %get-tuple-element.28.first_ref, bf16[6,2048,128]{2,1,0:T(8,128)(2,1)S(1)} %get-tuple-element.29.last_ref, f32[8,128]{1,0:T(8,128)S(1)} %get-tuple-element.30.s0, f32[8,128]{1,0:T(8,128)S(1)} %collective-permute-done.5.s1, ...), custom_call_target="tpu_custom_call" | custom-call | tf_op jit(solution)/shard_map/rim/pallas_call | solution.py:375
  35.7 0.4 collective-permute-start.8
  36.1 4.5 %collective-permute-start.9 = (f32[4,2048]{1,0:T(4,128)S(1)}, f32[4,2048]{1,0:T(4,128)S(1)}, u32[]{:S(2)}, u32[]{:S(2)}) collective-permute-start(f32[4,2048]{1,0:T(4,128)S(1)} %get-tuple-element.33), channel_id=1, source_target_pairs={{1,2},{2,1},{5,6},{6,5},{9,10},{10,9},{13,14},{14,13},{17,18},{18,... | collective-permute-start | bytes 98312 | tf_op jit(solution)/shard_map/ppermute | solution.py:563
  40.6 0.0 copy-done.4
  40.6 0.0 copy-start.6
  40.6 0.0 copy-start.3
  40.6 3.5 %taps.1.part_ref = f32[4,8,2048]{2,1,0:T(8,128)S(1)} custom-call(bf16[8,2048,128]{2,1,0:T(8,128)(2,1)S(1)} %get-tuple-element.19.x_ref, bf16[2,2048,128]{2,1,0:T(8,128)(2,1)S(1)} %get-tuple-element.28.first_ref, bf16[6,2048,128]{2,1,0:T(8,128)(2,1)S(1)} %get-tuple-element.29.last_ref, f32[8,128]{1,0:T(8,128)S(1)} %get-tuple-element.30.s0, ...), custom_call_target="tpu_custom_call" | custom-call | flops 6442450944 | bytes 4194304 | tf_op jit(solution)/shard_map/taps/pallas_call | solution.py:432
  44.1 0.0 collective-permute-done.8.core_ref
  44.1 0.0 collective-permute-done.9.far_ref
  44.2 1.0 %step.1 = (f32[4,8,2048]{2,1,0:T(8,128)}, f32[16,4,8,128]{3,2,1,0:T(8,128)}) custom-call(f32[4,8,2048]{2,1,0:T(8,128)S(1)} %taps.1.part_ref, f32[4,2048]{1,0:T(4,128)S(1)} %collective-permute-done.8.core_ref, f32[4,2048]{1,0:T(4,128)S(1)} %collective-permute-done.9.far_ref, s32[1]{0:T(128)S(6)} %copy.11.index_ref), custom_call_target="tpu_custom_call" | custom-call | tf_op jit(solution)/shard_map/step/pallas_call | solution.py:471
  45.2 4.8 %all-to-all-start = ((f32[16,4,8,128]{3,2,1,0:T(8,128)}), f32[16,4,8,128]{3,2,1,0:T(8,128)S(1)}, u32[]{:S(2)}, u32[]{:S(2)}) async-start(f32[16,4,8,128]{3,2,1,0:T(8,128)} %get-tuple-element.34.blocks_ref), calls=%async_computation | async-start | bytes 524288 | tf_op jit(solution)/shard_map/all_to_all | solution.py:590
  50.1 0.1 tile.10.reg_ref
  50.2 6.6 %all-to-all-done.got_ref = f32[16,4,8,128]{3,2,1,0:T(8,128)S(1)} async-done(((f32[16,4,8,128]{3,2,1,0:T(8,128)}), f32[16,4,8,128]{3,2,1,0:T(8,128)S(1)}, u32[]{:S(2)}, u32[]{:S(2)}) %all-to-all-start) | async-done | bytes 262176 | tf_op jit(solution)/shard_map/all_to_all | solution.py:590
  56.8 3.1 %collective-permute-start.10 = (f32[3,4,8,128]{3,2,1,0:T(8,128)S(1)}, f32[3,4,8,128]{3,2,1,0:T(8,128)S(1)}, u32[]{:S(2)}, u32[]{:S(2)}) collective-permute-start(f32[3,4,8,128]{3,2,1,0:T(8,128)S(1)} %sums.1), channel_id=1, source_target_pairs={{0,64},{4,68},{8,72},{12,76},{16,80},{20,84},{24,88},{28,92},{32,9... | collective-permute-start | bytes 147464 | tf_op jit(solution)/shard_map/ppermute | solution.py:593
  59.8 2.0 %collective-permute-done.10 = f32[3,4,8,128]{3,2,1,0:T(8,128)S(1)} collective-permute-done((f32[3,4,8,128]{3,2,1,0:T(8,128)S(1)}, f32[3,4,8,128]{3,2,1,0:T(8,128)S(1)}, u32[]{:S(2)}, u32[]{:S(2)}) %collective-permute-start.10) | collective-permute-done | bytes 49184 | tf_op jit(solution)/shard_map/ppermute | solution.py:593
  61.9 4.1 %collective-permute-start.11 = (f32[3,4,8,128]{3,2,1,0:T(8,128)S(1)}, f32[3,4,8,128]{3,2,1,0:T(8,128)S(1)}, u32[]{:S(2)}, u32[]{:S(2)}) collective-permute-start(f32[3,4,8,128]{3,2,1,0:T(8,128)S(1)} %add.3.one_ref), channel_id=1, source_target_pairs={{0,192},{4,196},{8,200},{12,204},{16,208},{20,212},{24,216},{28,22... | collective-permute-start | bytes 147464 | tf_op jit(solution)/shard_map/ppermute | solution.py:594
  65.9 2.2 %collective-permute-done.11.two_ref = f32[3,4,8,128]{3,2,1,0:T(8,128)S(1)} collective-permute-done((f32[3,4,8,128]{3,2,1,0:T(8,128)S(1)}, f32[3,4,8,128]{3,2,1,0:T(8,128)S(1)}, u32[]{:S(2)}, u32[]{:S(2)}) %collective-permute-start.11) | collective-permute-done | bytes 49184 | tf_op jit(solution)/shard_map/ppermute | solution.py:594
  68.2 0.6 spread.1
  68.8 14.1 %all_to_all.10.got_ref = f32[16,2,4,8,128]{4,3,2,1,0:T(8,128)S(1)} all-to-all(f32[16,2,4,8,128]{4,3,2,1,0:T(8,128)S(1)} %spread.1), channel_id=1, replica_groups={{0,4,8,12,16,20,24,28,32,36,40,44,48,52,56,60},{64,68,72,76,80,84,88,92..., dimensions={0} | all-to-all | bytes 1048576 | tf_op jit(solution)/shard_map/all_to_all | solution.py:596
  82.9 1.9 %field.1 = f32[4,8,2048]{2,1,0:T(8,128)} custom-call(f32[16,4,8,128]{3,2,1,0:T(8,128)} %get-tuple-element.34.blocks_ref, f32[16,2,4,8,128]{4,3,2,1,0:T(8,128)S(1)} %all_to_all.10.got_ref), custom_call_target="tpu_custom_call" | custom-call | tf_op jit(solution)/shard_map/field/pallas_call | solution.py:548
  (6 shorter events, 0.1 us)
Async XLA Ops:
  0.6 16.6 %copy-start = (bf16[9,128,128]{2,1,0:T(8,128)(2,1)S(1)}, bf16[9,128,128]{2,1,0:T(8,128)(2,1)}, u32[]{:S(2)}) copy-start(bf16[9,128,128]{2,1,0:T(8,128)(2,1)} %first_ref.1) | copy-start | bytes 884740
  0.6 16.6 %copy-start.1 = (bf16[9,128,128]{2,1,0:T(8,128)(2,1)S(1)}, bf16[9,128,128]{2,1,0:T(8,128)(2,1)}, u32[]{:S(2)}) copy-start(bf16[9,128,128]{2,1,0:T(8,128)(2,1)} %second_ref.1) | copy-start | bytes 884740
  0.7 16.6 %copy-start.2 = (bf16[4,128]{1,0:T(4,128)(2,1)S(1)}, bf16[4,128]{1,0:T(4,128)(2,1)}, u32[]{:S(2)}) copy-start(bf16[4,128]{1,0:T(4,128)(2,1)} %head_ref.3) | copy-start | bytes 3076
  7.6 9.9 %collective-permute-start.1 = (bf16[2048,128]{1,0:T(8,128)(2,1)S(1)}, bf16[2048,128]{1,0:T(8,128)(2,1)S(1)}, u32[]{:S(2)}, u32[]{:S(2)}) collective-permute-start(bf16[2048,128]{1,0:T(8,128)(2,1)S(1)} %get-tuple-element.21), channel_id=1, source_target_pairs={{0,1},{1,0},{2,3},{3,2},{4,5},{5,4},{6,7},{7,6},{8,9},{9,8},{10,11... | collective-permute-start | bytes 1572872 | tf_op jit(solution)/shard_map/ppermute | solution.py:559
  10.9 6.5 %collective-permute-start.2 = (f32[8,128]{1,0:T(8,128)S(1)}, f32[8,128]{1,0:T(8,128)S(1)}, u32[]{:S(2)}, u32[]{:S(2)}) collective-permute-start(f32[8,128]{1,0:T(8,128)S(1)} %get-tuple-element.22.s0), channel_id=1, source_target_pairs={{0,1},{1,0},{2,3},{3,2},{4,5},{5,4},{6,7},{7,6},{8,9},{9,8},{10,11... | collective-permute-start | bytes 12296 | tf_op jit(solution)/shard_map/ppermute | solution.py:559
  11.0 6.4 %collective-permute-start.3 = (f32[8,128]{1,0:T(8,128)S(1)}, f32[8,128]{1,0:T(8,128)S(1)}, u32[]{:S(2)}, u32[]{:S(2)}) collective-permute-start(f32[8,128]{1,0:T(8,128)S(1)} %get-tuple-element.22.s0), channel_id=1, source_target_pairs={{0,2},{1,3},{2,0},{3,1},{4,6},{5,7},{6,4},{7,5},{8,10},{9,11},{10,... | collective-permute-start | bytes 12296 | tf_op jit(solution)/shard_map/ppermute | solution.py:559
  12.0 5.4 %collective-permute-start.4 = (f32[8,128]{1,0:T(8,128)S(1)}, f32[8,128]{1,0:T(8,128)S(1)}, u32[]{:S(2)}, u32[]{:S(2)}) collective-permute-start(f32[8,128]{1,0:T(8,128)S(1)} %get-tuple-element.22.s0), channel_id=1, source_target_pairs={{0,3},{1,2},{2,1},{3,0},{4,7},{5,6},{6,5},{7,4},{8,11},{9,10},{10,... | collective-permute-start | bytes 12296 | tf_op jit(solution)/shard_map/ppermute | solution.py:559
  14.6 12.0 %collective-permute-start = (bf16[2048,128]{1,0:T(8,128)(2,1)S(1)}, bf16[2048,128]{1,0:T(8,128)(2,1)S(1)}, u32[]{:S(2)}, u32[]{:S(2)}) collective-permute-start(bf16[2048,128]{1,0:T(8,128)(2,1)S(1)} %get-tuple-element.20), channel_id=1, source_target_pairs={{1,2},{2,1},{5,6},{6,5},{9,10},{10,9},{13,14},{14,13},{17,18},{18,... | collective-permute-start | bytes 1572872 | tf_op jit(solution)/shard_map/ppermute | solution.py:563
  28.9 11.7 %copy-start.4 = (f32[1,4,8,2048]{3,2,1,0:T(8,128)S(1)}, f32[1,4,8,2048]{3,2,1,0:T(8,128)}, u32[]{:S(2)}) copy-start(f32[1,4,8,2048]{3,2,1,0:T(8,128)} %param.10) | copy-start | bytes 786436
  28.9 11.7 %copy-start.5 = (f32[1,4,8,2048]{3,2,1,0:T(8,128)S(1)}, f32[1,4,8,2048]{3,2,1,0:T(8,128)}, u32[]{:S(2)}) copy-start(f32[1,4,8,2048]{3,2,1,0:T(8,128)} %param.11) | copy-start | bytes 786436
  28.9 4.4 %collective-permute-start.5 = (f32[8,128]{1,0:T(8,128)S(1)}, f32[8,128]{1,0:T(8,128)S(1)}, u32[]{:S(2)}, u32[]{:S(2)}) collective-permute-start(f32[8,128]{1,0:T(8,128)S(1)} %get-tuple-element.30.s0), channel_id=1, source_target_pairs={{0,1},{1,0},{2,3},{3,2},{4,5},{5,4},{6,7},{7,6},{8,9},{9,8},{10,11... | collective-permute-start | bytes 12296 | tf_op jit(solution)/shard_map/ppermute | solution.py:559
  29.0 4.3 %collective-permute-start.6 = (f32[8,128]{1,0:T(8,128)S(1)}, f32[8,128]{1,0:T(8,128)S(1)}, u32[]{:S(2)}, u32[]{:S(2)}) collective-permute-start(f32[8,128]{1,0:T(8,128)S(1)} %get-tuple-element.30.s0), channel_id=1, source_target_pairs={{0,2},{1,3},{2,0},{3,1},{4,6},{5,7},{6,4},{7,5},{8,10},{9,11},{10,... | collective-permute-start | bytes 12296 | tf_op jit(solution)/shard_map/ppermute | solution.py:559
  29.9 4.5 %collective-permute-start.7 = (f32[8,128]{1,0:T(8,128)S(1)}, f32[8,128]{1,0:T(8,128)S(1)}, u32[]{:S(2)}, u32[]{:S(2)}) collective-permute-start(f32[8,128]{1,0:T(8,128)S(1)} %get-tuple-element.30.s0), channel_id=1, source_target_pairs={{0,3},{1,2},{2,1},{3,0},{4,7},{5,6},{6,5},{7,4},{8,11},{9,10},{10,... | collective-permute-start | bytes 12296 | tf_op jit(solution)/shard_map/ppermute | solution.py:559
  35.7 8.5 %collective-permute-start.8 = (f32[4,2048]{1,0:T(4,128)S(1)}, f32[4,2048]{1,0:T(4,128)S(1)}, u32[]{:S(2)}, u32[]{:S(2)}) collective-permute-start(f32[4,2048]{1,0:T(4,128)S(1)} %get-tuple-element.32), channel_id=1, source_target_pairs={{0,1},{1,0},{2,3},{3,2},{4,5},{5,4},{6,7},{7,6},{8,9},{9,8},{10,11... | collective-permute-start | bytes 98312 | tf_op jit(solution)/shard_map/ppermute | solution.py:559
  36.1 8.0 %collective-permute-start.9 = (f32[4,2048]{1,0:T(4,128)S(1)}, f32[4,2048]{1,0:T(4,128)S(1)}, u32[]{:S(2)}, u32[]{:S(2)}) collective-permute-start(f32[4,2048]{1,0:T(4,128)S(1)} %get-tuple-element.33), channel_id=1, source_target_pairs={{1,2},{2,1},{5,6},{6,5},{9,10},{10,9},{13,14},{14,13},{17,18},{18,... | collective-permute-start | bytes 98312 | tf_op jit(solution)/shard_map/ppermute | solution.py:563
  40.6 9.4 %copy-start.6 = (f32[4,8,32]{2,1,0:T(8,128)S(1)}, f32[4,8,32]{2,1,0:T(8,128)}, u32[]{:S(2)}) copy-start(f32[4,8,32]{2,1,0:T(8,128)} %param.12) | copy-start | bytes 12292
  40.6 27.5 %copy-start.3 = (f32[4]{0:T(128)S(1)}, f32[4]{0:T(128)}, u32[]{:S(2)}) copy-start(f32[4]{0:T(128)} %target_ref.1) | copy-start | bytes 52
  45.2 11.5 %all-to-all-start = ((f32[16,4,8,128]{3,2,1,0:T(8,128)}), f32[16,4,8,128]{3,2,1,0:T(8,128)S(1)}, u32[]{:S(2)}, u32[]{:S(2)}) async-start(f32[16,4,8,128]{3,2,1,0:T(8,128)} %get-tuple-element.34.blocks_ref), calls=%async_computation | async-start | bytes 524288 | tf_op jit(solution)/shard_map/all_to_all | solution.py:590
  56.8 5.1 %collective-permute-start.10 = (f32[3,4,8,128]{3,2,1,0:T(8,128)S(1)}, f32[3,4,8,128]{3,2,1,0:T(8,128)S(1)}, u32[]{:S(2)}, u32[]{:S(2)}) collective-permute-start(f32[3,4,8,128]{3,2,1,0:T(8,128)S(1)} %sums.1), channel_id=1, source_target_pairs={{0,64},{4,68},{8,72},{12,76},{16,80},{20,84},{24,88},{28,92},{32,9... | collective-permute-start | bytes 147464 | tf_op jit(solution)/shard_map/ppermute | solution.py:593
  61.9 6.3 %collective-permute-start.11 = (f32[3,4,8,128]{3,2,1,0:T(8,128)S(1)}, f32[3,4,8,128]{3,2,1,0:T(8,128)S(1)}, u32[]{:S(2)}, u32[]{:S(2)}) collective-permute-start(f32[3,4,8,128]{3,2,1,0:T(8,128)S(1)} %add.3.one_ref), channel_id=1, source_target_pairs={{0,192},{4,196},{8,200},{12,204},{16,208},{20,212},{24,216},{28,22... | collective-permute-start | bytes 147464 | tf_op jit(solution)/shard_map/ppermute | solution.py:594

commit v4 on v3

--- a/solution.py
+++ b/solution.py
@@ -56,42 +56,42 @@
     st_ref[...] = jnp.concatenate([mean, dev, pad], axis=0)
 
 
-def features_kernel(x_ref, xt_ref, core_ref, far_ref, st_ref, scr, acc):
-    step = pl.program_id(0)
-    chans, rows, width = x_ref.shape
+def features_kernel(x_ref, xt_ref, core_ref, far_ref, st_ref, held, scr, sems):
+    rows, full, chans = xt_ref.shape
+    pieces, _, _, width = held.shape
     even = (lax.axis_index("tile") & 1) == 0
-    for part in range(width // 128):
-        at = pl.ds(128 * part, 128)
-        scr[part] = x_ref[:, :, at].astype(F32).reshape(chans * rows, 128)
-        one = two = jnp.zeros((8, chans), F32)
-        for r in range(rows):
-            turned = scr[part, pl.ds(r, chans, stride=rows), :].T
-            if part == 0 and r == 0:
-
-                @pl.when(step == 0)
-                def _():
-                    middle = jnp.mean(turned, axis=0, keepdims=True)
-                    acc[0] = jnp.broadcast_to(middle, acc.shape[1:])
-                    acc[1] = jnp.zeros(acc.shape[1:], F32)
-                    acc[2] = jnp.zeros(acc.shape[1:], F32)
-
-            if r == 0:
-                pivot = acc[0, 0:1]
-            off = turned - pivot
-            one = one + row_sum(off)
-            two = two + row_sum(off * off)
-            turned = turned.astype(BF16)
-            xt_ref[jnp.where(even, r, rows - 1 - r), at] = turned
-            if r == 0:
-                top = turned
-        acc[1] += one
-        acc[2] += two
-        core_ref[at] = jnp.where(even, turned, top)
-        far_ref[at] = jnp.where(even, top, turned)
-
-    @pl.when(step == pl.num_programs(0) - 1)
-    def _():
-        write_stats(st_ref, acc[0, 0:1], acc[1], acc[2], pl.num_programs(0) * rows * width)
+
+    def piece(i):
+        at = pl.ds(pl.multiple_of(i * width, width), width)
+        return pltpu.make_async_copy(x_ref.at[:, :, at], held.at[i], sems.at[i])
+
+    for i in range(pieces):
+        piece(i).start()
+
+    def work(i, carry):
+        pivot, one, two = carry
+        piece(i).wait()
+        for part in range(width // 128):
+            at = pl.ds(pl.multiple_of(i * width + 128 * part, 128), 128)
+            scr[part] = held[i, :, :, pl.ds(128 * part, 128)].astype(F32).reshape(chans * rows, 128)
+            for r in range(rows):
+                turned = scr[part, pl.ds(r, chans, stride=rows), :].T
+                if part == 0 and r == 0:
+                    pivot = jnp.where(i == 0, jnp.mean(turned, axis=0, keepdims=True), pivot)
+                off = turned - pivot
+                one = one + row_sum(off)
+                two = two + row_sum(off * off)
+                turned = turned.astype(BF16)
+                xt_ref[jnp.where(even, r, rows - 1 - r), at] = turned
+                if r == 0:
+                    top = turned
+            core_ref[at] = jnp.where(even, turned, top)
+            far_ref[at] = jnp.where(even, top, turned)
+        return pivot, one, two
+
+    zero = jnp.zeros((8, chans), F32)
+    pivot, one, two = lax.fori_loop(0, pieces, work, (zero[0:1], zero, zero))
+    write_stats(st_ref, pivot, one, two, rows * full)
 
 
 def features_call(x, block):
@@ -99,23 +99,18 @@
     edge = jax.ShapeDtypeStruct((width, chans), BF16)
     return pl.pallas_call(
         features_kernel,
-        grid=(width // block,),
         out_shape=(
             jax.ShapeDtypeStruct((rows, width, chans), BF16),
             edge,
             edge,
             jax.ShapeDtypeStruct((8, chans), F32),
         ),
-        in_specs=[pl.BlockSpec((chans, rows, block), lambda i: (0, 0, i))],
-        out_specs=(
-            pl.BlockSpec((rows, block, chans), lambda i: (0, i, 0)),
-            pl.BlockSpec((block, chans), lambda i: (i, 0)),
-            pl.BlockSpec((block, chans), lambda i: (i, 0)),
-            pl.BlockSpec((8, chans), lambda i: (0, 0)),
-        ),
+        in_specs=[pl.BlockSpec(memory_space=pl.ANY)],
+        out_specs=(VM,) * 4,
         scratch_shapes=[
+            pltpu.VMEM((width // block, chans, rows, block), BF16),
             pltpu.VMEM((block // 128, chans * rows, 128), F32),
-            pltpu.VMEM((3, 8, chans), F32),
+            pltpu.SemaphoreType.DMA((width // block,)),
         ],
         compiler_params=limit(16),
         name="features",
@@ -216,15 +211,23 @@
     return out[:, :chans], out[:, chans:]
 
 
-def join(acts, wt_ref, hid_ref, lines, block, fresh, carry):
+def join(acts, wt_ref, hid_ref, lines, block, late, fresh, carry):
     width = hid_ref.shape[1]
     pivot, one, two = carry
     for at in range(0, width, block):
         a, b = two_rows(acts, wt_ref, at, block)
-        for act, buf, read in fresh:
-            fill(act, buf, read(at, block), at, block)
-            if at > 0:
-                fill_sides(act, buf, at - block, block)
+        if at == 0:
+            for act, buf, read in late:
+                rest = width - block - 16
+                fill(act, buf, read(block + 16, rest), block + 16, rest)
+                fill_sides(act, buf, block, width - block)
+        if not late or at > 0:
+            start = 0 if late else at
+            size = at + block - start
+            for act, buf, read in fresh:
+                fill(act, buf, read(start, size), start, size)
+                if start > 0:
+                    fill_sides(act, buf, start - block, block)
         hid_ref[lines[0], pl.ds(at, block), :] = a.astype(BF16)
         hid_ref[lines[1], pl.ds(at, block), :] = b.astype(BF16)
         if pivot is None:
@@ -233,7 +236,8 @@
         one = one + row_sum(a + b)
         two = two + row_sum(a * a + b * b)
     for act, buf, read in fresh:
-        fill_sides(act, buf, width - block, block)
+        start = 0 if late else width - block
+        fill_sides(act, buf, start, width - start)
     return pivot, one, two
 
 
@@ -250,18 +254,19 @@
             value = core_ref[span, :] if row == rows else x_ref[row, span, :]
             return silu(value.astype(F32) * scale + shift)
 
-        return acts[row], bufs[row % 2], read
-
-    for row in range(1, 5):
-        act, buf, read = line(row)
-        fill(act, buf, read(0, width), 0, width)
-        fill_sides(act, buf, 0, width)
+        return acts[row], bufs[row % len(bufs)], read
+
+    early = [line(row) for row in range(1, 5)]
+    for act, buf, read in early:
+        fill(act, buf, read(0, block + 16), 0, block + 16)
+        fill_sides(act, buf, 0, block)
     zero = jnp.zeros((8, chans), F32)
     carry = (None, zero, zero)
     for pair, fresh in ((0, (5, 6)), (1, (7, 8)), (2, (0,))):
         group = acts[2 * pair + 1 : 2 * pair + 5]
         lines = (2 * pair, 2 * pair + 1)
-        carry = join(group, wt_ref, hid_ref, lines, block, [line(row) for row in fresh], carry)
+        fresh = [line(row) for row in fresh]
+        carry = join(group, wt_ref, hid_ref, lines, block, early if pair == 0 else [], fresh, carry)
     pivot, one, two = carry
     sum_ref[0] = jnp.broadcast_to(pivot, one.shape)
     sum_ref[1] = one
@@ -283,8 +288,8 @@
         in_specs=[VM] * 7,
         out_specs=(VM,) * 5,
         scratch_shapes=[pltpu.VMEM(act.shape, BF16)] * (rows - 2)
-        + [pltpu.VMEM((width + 16, chans), F32)] * 2,
-        compiler_params=limit(28),
+        + [pltpu.VMEM((width + 16, chans), F32)] * 4,
+        compiler_params=limit(32),
         cost_estimate=pl.CostEstimate(
             flops=24 * rows * width * chans * chans, bytes_accessed=1 << 22, transcendentals=xt.size
         ),
@@ -300,14 +305,15 @@
     count = TILES * 2 * width
     scale, shift = norm_factors([s0, s1, s2, s3], count)
     clear_ends(buf)
-    for at in range(0, width, block):
-        value = silu(far_ref[pl.ds(at, block), :].astype(F32) * scale + shift) * linked
-        fill(act, buf, value, at, block)
-        if at > 0:
-            fill_sides(act, buf, at - block, block)
-    fill_sides(act, buf, width - block, block)
+
+    def read(at, size):
+        return silu(far_ref[pl.ds(at, size), :].astype(F32) * scale + shift) * linked
+
+    fill(act, buf, read(0, block + 16), 0, block + 16)
+    fill_sides(act, buf, 0, block)
     carry = (sum_ref[0, 0:1], sum_ref[1], sum_ref[2])
-    pivot, one, two = join([act, a0, a1, a2], wt_ref, hid_ref, (0, 1), block, [], carry)
+    early = [(act, buf, read)]
+    pivot, one, two = join([act, a0, a1, a2], wt_ref, hid_ref, (0, 1), block, early, [], carry)
     write_stats(st_ref, pivot, one, two, count)
 
 
@@ -444,7 +450,7 @@
     )(xt, first, last, *stats, fold, head, state, noise, index)
 
 
-def step_kernel(part_ref, core_ref, far_ref, index_ref, next_ref, blocks_ref):
+def step_kernel(part_ref, core_ref, far_ref, index_ref, next_ref, blocks_ref, kept_ref):
     outs, rows, width = part_ref.shape
     even = (lax.axis_index("tile") & 1) == 0
     push = step_factors(index_ref[0])[2]
@@ -464,6 +470,7 @@
                 next_ref[o, :, at] = values[-1]
             for j, mixed in enumerate(turn_quarters(values, slot)):
                 blocks_ref[4 * t + j, o] = mixed
+                kept_ref[4 * t + j, o] = mixed
 
 
 def step_call(part, core, far, index):
@@ -473,9 +480,10 @@
         out_shape=(
             jax.ShapeDtypeStruct(part.shape, F32),
             jax.ShapeDtypeStruct((width // 128, outs, rows, 128), F32),
+            pltpu.VMEM((width // 128, outs, rows, 128), F32),
         ),
         in_specs=[VM] * 3 + [SM],
-        out_specs=(VM, VM),
+        out_specs=(VM, VM, VM),
         compiler_params=limit(8),
         name="step",
     )(part, core, far, index)
@@ -571,7 +579,7 @@
     features, residual_state, noise, regression_mean, step_index, conv_first, conv_second, head_weight, spread_target
 ):
     member = pltpu.with_memory_space_constraint(features[0], pltpu.HBM)
-    xt, core, far, stats = features_call(member, 256)
+    xt, core, far, stats = features_call(member, 512)
     stats = spread_stats(stats)
     core, far = swap(core, 1), far_swap(far)
     wt, fold = weights_call(conv_first, conv_second, head_weight)
@@ -583,7 +591,7 @@
     part = taps_call(
         xt, first, last, stats, fold, head_weight, residual_state[0], noise[0], step_index
     )
-    advanced, blocks = step_call(part, core, far, step_index)
+    advanced, blocks, kept = step_call(part, core, far, step_index)
     members = lax.axis_size("member")
     size = blocks.shape[0]
     runs = [list(range(i, i + size)) for i in range(0, members, size)]
@@ -594,7 +602,7 @@
     other = lax.ppermute(sums, "member", [(i, i ^ (3 * size)) for i in range(members)])
     sent = spread_call(sums, other, spread_target, size, members)
     got = lax.all_to_all(sent, "member", 0, 0, tiled=True, axis_index_groups=runs)
-    field = field_call(blocks, got, advanced.shape)
+    field = field_call(kept, got, advanced.shape)
     return (field[None], advanced[None])
 
 

time: 85.2 us -> 81.4 us (0.955)
  Pallas kernels: 24.6 us -> 21 us
    pallas_call x1, Pallas kernels: 6.93 us -> 4.13 us  [features_call(): pl.pallas_call(features_kernel, out_shape=(jax.ShapeDtypeStruct((rows, wi...]
    pallas_call x1, Pallas kernels: 1.88 us -> 0.93 us  [field_call(): pl.pallas_call(field_kernel, out_shape=jax.ShapeDtypeStruct(shape, F32),...]
  transfers between devices with their start and end apart: 13 -> 13, of which waited for: 5 -> 5; matrix products, arithmetic and copies ran while one was open for 0% -> 0% of each run, Pallas kernels for 12% -> 13%
where the time goes in v4:
time: 81.4 us; the launch traced here: 81 us
  starting transfers between devices  30.2 us (37%)
  Pallas kernels  21 us (26%)
  blocking collectives  14.1 us (17%)
  waiting for transfers between devices  14 us (17%)
  between operations  1.54 us (2%)
    all_to_all x1, blocking collectives, shards(): lax.all_to_all(sent, 'member', 0, 0, tiled=True, axis_index_groups=runs)  14.1 us
    ppermute x8, starting transfers between devices, swap(): return lax.ppermute(value, 'tile', [(i, i ^ bits) for i in range(TILES)])  11.1 us
    ppermute x2, starting transfers between devices, far_swap(): return lax.ppermute(value, 'tile', [(1, 2), (2, 1)])  7.1 us
    pallas_call x1, Pallas kernels, inner_call(): pl.pallas_call(functools.partial(inner_kernel, block), out_shape=(jax.Sha...  6.96 us
    all_to_all x1, waiting for transfers between devices, shards(): lax.all_to_all(blocks, 'member', 0, 0, tiled=True, axis_index_groups=runs)  6.58 us
    all_to_all x1, starting transfers between devices, shards(): lax.all_to_all(blocks, 'member', 0, 0, tiled=True, axis_index_groups=runs)  4.84 us
    pallas_call x1, Pallas kernels, features_call(): pl.pallas_call(features_kernel, out_shape=(jax.ShapeDtypeStruct((rows, wi...  4.13 us
    ppermute x1, starting transfers between devices, shards(): lax.ppermute(sums, 'member', [(i, i ^ 3 * size) for i in range(members)])  4.05 us
  transfers between devices with their start and end apart: 13, of which 5 were waited for; matrix products, arithmetic and copies ran while one was open for 0% of the time, Pallas kernels for 13%

profile of v4, /device:TPU:1, one launch (start us, length us, event | category | flops | bytes accessed | tf_op | source)
XLA Modules:
  0.0 81.0 jit_solution(11533698487432267052)
XLA Ops:
  0.6 0.0 copy-start
  0.6 0.0 copy-start.1
  0.7 0.0 copy-start.2
  0.7 4.1 %features.1 = (bf16[8,2048,128]{2,1,0:T(8,128)(2,1)S(1)}, bf16[2048,128]{1,0:T(8,128)(2,1)S(1)}, bf16[2048,128]{1,0:T(8,128)(2,1)S(1)}, f32[8,128]{1,0:T(8,128)S(1)}) custom-call(bf16[128,8,2048]{2,1,0:T(8,128)(2,1)} %bitcast.7), custom_call_target="tpu_custom_call" | custom-call | tf_op jit(solution)/shard_map/features/pallas_call | solution.py:100
  4.8 3.3 %collective-permute-start.1 = (bf16[2048,128]{1,0:T(8,128)(2,1)S(1)}, bf16[2048,128]{1,0:T(8,128)(2,1)S(1)}, u32[]{:S(2)}, u32[]{:S(2)}) collective-permute-start(bf16[2048,128]{1,0:T(8,128)(2,1)S(1)} %get-tuple-element.22), channel_id=1, source_target_pairs={{0,1},{1,0},{2,3},{3,2},{4,5},{5,4},{6,7},{7,6},{8,9},{9,8},{10,11... | collective-permute-start | bytes 1572872 | tf_op jit(solution)/shard_map/ppermute | solution.py:567
  8.1 0.1 collective-permute-start.2
  8.2 1.0 %collective-permute-start.3 = (f32[8,128]{1,0:T(8,128)S(1)}, f32[8,128]{1,0:T(8,128)S(1)}, u32[]{:S(2)}, u32[]{:S(2)}) collective-permute-start(f32[8,128]{1,0:T(8,128)S(1)} %get-tuple-element.23.s0), channel_id=1, source_target_pairs={{0,2},{1,3},{2,0},{3,1},{4,6},{5,7},{6,4},{7,5},{8,10},{9,11},{10,... | collective-permute-start | bytes 12296 | tf_op jit(solution)/shard_map/ppermute | solution.py:567
  9.2 2.5 %collective-permute-start.4 = (f32[8,128]{1,0:T(8,128)S(1)}, f32[8,128]{1,0:T(8,128)S(1)}, u32[]{:S(2)}, u32[]{:S(2)}) collective-permute-start(f32[8,128]{1,0:T(8,128)S(1)} %get-tuple-element.23.s0), channel_id=1, source_target_pairs={{0,3},{1,2},{2,1},{3,0},{4,7},{5,6},{6,5},{7,4},{8,11},{9,10},{10,... | collective-permute-start | bytes 12296 | tf_op jit(solution)/shard_map/ppermute | solution.py:567
  11.8 2.6 %collective-permute-start = (bf16[2048,128]{1,0:T(8,128)(2,1)S(1)}, bf16[2048,128]{1,0:T(8,128)(2,1)S(1)}, u32[]{:S(2)}, u32[]{:S(2)}) collective-permute-start(bf16[2048,128]{1,0:T(8,128)(2,1)S(1)} %get-tuple-element.21), channel_id=1, source_target_pairs={{1,2},{2,1},{5,6},{6,5},{9,10},{10,9},{13,14},{14,13},{17,18},{18,... | collective-permute-start | bytes 1572872 | tf_op jit(solution)/shard_map/ppermute | solution.py:571
  14.4 0.0 copy-done
  14.4 0.0 copy-done.1
  14.4 0.0 copy-done.2
  14.4 0.2 weights.1
  14.6 0.0 collective-permute-done.2.s1
  14.6 0.0 collective-permute-done.3.s2
  14.7 0.0 collective-permute-done.4.s3
  14.7 0.0 collective-permute-done.1.core_ref
  14.7 7.0 %inner.1 = (bf16[6,2048,128]{2,1,0:T(8,128)(2,1)S(1)}, f32[3,8,128]{2,1,0:T(8,128)S(1)}, bf16[3,2048,128]{2,1,0:T(8,128)(2,1)S(1)}, bf16[3,2048,128]{2,1,0:T(8,128)(2,1)S(1)}, bf16[3,2048,128]{2,1,0:T(8,128)(2,1)S(1)}) custom-call(bf16[8,2048,128]{2,1,0:T(8,128)(2,1)S(1)} %get-tuple-element.20.x_ref, bf16[2048,128]{1,0:T(8,128)(2,1)S(1)} %collective-permute-done.1.core_ref, ...), custom_call_target="tpu_custom_call" | custom-call | flops 6442450944 | bytes 4194304 | tf_op jit(solution)/shard_map/inner/pallas_call | solution.py:279
  21.6 2.1 %collective-permute-done.far_ref = bf16[2048,128]{1,0:T(8,128)(2,1)S(1)} collective-permute-done((bf16[2048,128]{1,0:T(8,128)(2,1)S(1)}, bf16[2048,128]{1,0:T(8,128)(2,1)S(1)}, u32[]{:S(2)}, u32[]{:S(2)}) %collective-permute-start) | collective-permute-done | bytes 524320 | tf_op jit(solution)/shard_map/ppermute | solution.py:571
  23.8 2.3 %outer.1 = (bf16[2,2048,128]{2,1,0:T(8,128)(2,1)S(1)}, f32[8,128]{1,0:T(8,128)S(1)}) custom-call(bf16[2048,128]{1,0:T(8,128)(2,1)S(1)} %collective-permute-done.far_ref, bf16[3,2048,128]{2,1,0:T(8,128)(2,1)S(1)} %get-tuple-element.25.a0, bf16[3,2048,128]{2,1,0:T(8,128)(2,1)S(1)} %get-tuple-element.26.a1, bf16[3,2048,128]{2,1,0:T(8,128)(2,1)S(1)} %get-tuple-element.27.a2, ...), custom_call_target="tpu_custom_call" | custom-call | tf_op jit(solution)/shard_map/outer/pallas_call | solution.py:322
  26.1 0.0 copy-start.4
  26.1 0.0 copy-start.5
  26.1 0.1 collective-permute-start.5
  26.2 0.8 %collective-permute-start.6 = (f32[8,128]{1,0:T(8,128)S(1)}, f32[8,128]{1,0:T(8,128)S(1)}, u32[]{:S(2)}, u32[]{:S(2)}) collective-permute-start(f32[8,128]{1,0:T(8,128)S(1)} %get-tuple-element.31.s0), channel_id=1, source_target_pairs={{0,2},{1,3},{2,0},{3,1},{4,6},{5,7},{6,4},{7,5},{8,10},{9,11},{10,... | collective-permute-start | bytes 12296 | tf_op jit(solution)/shard_map/ppermute | solution.py:567
  27.1 2.8 %collective-permute-start.7 = (f32[8,128]{1,0:T(8,128)S(1)}, f32[8,128]{1,0:T(8,128)S(1)}, u32[]{:S(2)}, u32[]{:S(2)}) collective-permute-start(f32[8,128]{1,0:T(8,128)S(1)} %get-tuple-element.31.s0), channel_id=1, source_target_pairs={{0,3},{1,2},{2,1},{3,0},{4,7},{5,6},{6,5},{7,4},{8,11},{9,10},{10,... | collective-permute-start | bytes 12296 | tf_op jit(solution)/shard_map/ppermute | solution.py:567
  30.5 0.0 collective-permute-done.5.s1
  30.5 0.0 collective-permute-done.6.s2
  30.5 1.1 %collective-permute-done.7.s3 = f32[8,128]{1,0:T(8,128)S(1)} collective-permute-done((f32[8,128]{1,0:T(8,128)S(1)}, f32[8,128]{1,0:T(8,128)S(1)}, u32[]{:S(2)}, u32[]{:S(2)}) %collective-permute-start.7) | collective-permute-done | bytes 4128 | tf_op jit(solution)/shard_map/ppermute | solution.py:567
  31.6 1.3 %rim.1 = (f32[4,2048]{1,0:T(4,128)S(1)}, f32[4,2048]{1,0:T(4,128)S(1)}) custom-call(bf16[2,2048,128]{2,1,0:T(8,128)(2,1)S(1)} %get-tuple-element.29.first_ref, bf16[6,2048,128]{2,1,0:T(8,128)(2,1)S(1)} %get-tuple-element.30.last_ref, f32[8,128]{1,0:T(8,128)S(1)} %get-tuple-element.31.s0, f32[8,128]{1,0:T(8,128)S(1)} %collective-permute-done.5.s1, ...), custom_call_target="tpu_custom_call" | custom-call | tf_op jit(solution)/shard_map/rim/pallas_call | solution.py:381
  32.9 0.4 collective-permute-start.8
  33.3 4.5 %collective-permute-start.9 = (f32[4,2048]{1,0:T(4,128)S(1)}, f32[4,2048]{1,0:T(4,128)S(1)}, u32[]{:S(2)}, u32[]{:S(2)}) collective-permute-start(f32[4,2048]{1,0:T(4,128)S(1)} %get-tuple-element.34), channel_id=1, source_target_pairs={{1,2},{2,1},{5,6},{6,5},{9,10},{10,9},{13,14},{14,13},{17,18},{18,... | collective-permute-start | bytes 98312 | tf_op jit(solution)/shard_map/ppermute | solution.py:571
  37.8 0.0 copy-done.4
  37.8 0.0 copy-start.6
  37.8 0.0 copy-start.3
  37.9 3.5 %taps.1.part_ref = f32[4,8,2048]{2,1,0:T(8,128)S(1)} custom-call(bf16[8,2048,128]{2,1,0:T(8,128)(2,1)S(1)} %get-tuple-element.20.x_ref, bf16[2,2048,128]{2,1,0:T(8,128)(2,1)S(1)} %get-tuple-element.29.first_ref, bf16[6,2048,128]{2,1,0:T(8,128)(2,1)S(1)} %get-tuple-element.30.last_ref, f32[8,128]{1,0:T(8,128)S(1)} %get-tuple-element.31.s0, ...), custom_call_target="tpu_custom_call" | custom-call | flops 6442450944 | bytes 4194304 | tf_op jit(solution)/shard_map/taps/pallas_call | solution.py:438
  41.3 0.0 collective-permute-done.8.core_ref
  41.4 0.0 collective-permute-done.9.far_ref
  41.4 1.0 %step.1 = (f32[4,8,2048]{2,1,0:T(8,128)}, f32[16,4,8,128]{3,2,1,0:T(8,128)}, f32[16,4,8,128]{3,2,1,0:T(8,128)S(1)}) custom-call(f32[4,8,2048]{2,1,0:T(8,128)S(1)} %taps.1.part_ref, f32[4,2048]{1,0:T(4,128)S(1)} %collective-permute-done.8.core_ref, f32[4,2048]{1,0:T(4,128)S(1)} %collective-permute-done.9.far_ref, s32[1]{0:T(128)S(6)} %copy.11.index_ref), custom_call_target="tpu_custom_call" | custom-call | tf_op jit(solution)/shard_map/step/pallas_call | solution.py:478
  42.4 4.8 %all-to-all-start = ((f32[16,4,8,128]{3,2,1,0:T(8,128)}), f32[16,4,8,128]{3,2,1,0:T(8,128)S(1)}, u32[]{:S(2)}, u32[]{:S(2)}) async-start(f32[16,4,8,128]{3,2,1,0:T(8,128)} %get-tuple-element.36), calls=%async_computation | async-start | bytes 524288 | tf_op jit(solution)/shard_map/all_to_all | solution.py:598
  47.3 0.1 tile.10.reg_ref
  47.4 6.6 %all-to-all-done.got_ref = f32[16,4,8,128]{3,2,1,0:T(8,128)S(1)} async-done(((f32[16,4,8,128]{3,2,1,0:T(8,128)}), f32[16,4,8,128]{3,2,1,0:T(8,128)S(1)}, u32[]{:S(2)}, u32[]{:S(2)}) %all-to-all-start) | async-done | bytes 262176 | tf_op jit(solution)/shard_map/all_to_all | solution.py:598
  54.0 3.1 %collective-permute-start.10 = (f32[3,4,8,128]{3,2,1,0:T(8,128)S(1)}, f32[3,4,8,128]{3,2,1,0:T(8,128)S(1)}, u32[]{:S(2)}, u32[]{:S(2)}) collective-permute-start(f32[3,4,8,128]{3,2,1,0:T(8,128)S(1)} %sums.1), channel_id=1, source_target_pairs={{0,64},{4,68},{8,72},{12,76},{16,80},{20,84},{24,88},{28,92},{32,9... | collective-permute-start | bytes 147464 | tf_op jit(solution)/shard_map/ppermute | solution.py:601
  57.1 2.0 %collective-permute-done.10 = f32[3,4,8,128]{3,2,1,0:T(8,128)S(1)} collective-permute-done((f32[3,4,8,128]{3,2,1,0:T(8,128)S(1)}, f32[3,4,8,128]{3,2,1,0:T(8,128)S(1)}, u32[]{:S(2)}, u32[]{:S(2)}) %collective-permute-start.10) | collective-permute-done | bytes 49184 | tf_op jit(solution)/shard_map/ppermute | solution.py:601
  59.1 4.1 %collective-permute-start.11 = (f32[3,4,8,128]{3,2,1,0:T(8,128)S(1)}, f32[3,4,8,128]{3,2,1,0:T(8,128)S(1)}, u32[]{:S(2)}, u32[]{:S(2)}) collective-permute-start(f32[3,4,8,128]{3,2,1,0:T(8,128)S(1)} %add.3.one_ref), channel_id=1, source_target_pairs={{0,192},{4,196},{8,200},{12,204},{16,208},{20,212},{24,216},{28,22... | collective-permute-start | bytes 147464 | tf_op jit(solution)/shard_map/ppermute | solution.py:602
  63.1 2.2 %collective-permute-done.11.two_ref = f32[3,4,8,128]{3,2,1,0:T(8,128)S(1)} collective-permute-done((f32[3,4,8,128]{3,2,1,0:T(8,128)S(1)}, f32[3,4,8,128]{3,2,1,0:T(8,128)S(1)}, u32[]{:S(2)}, u32[]{:S(2)}) %collective-permute-start.11) | collective-permute-done | bytes 49184 | tf_op jit(solution)/shard_map/ppermute | solution.py:602
  65.4 0.6 spread.1
  66.0 14.1 %all_to_all.10.got_ref = f32[16,2,4,8,128]{4,3,2,1,0:T(8,128)S(1)} all-to-all(f32[16,2,4,8,128]{4,3,2,1,0:T(8,128)S(1)} %spread.1), channel_id=1, replica_groups={{0,4,8,12,16,20,24,28,32,36,40,44,48,52,56,60},{64,68,72,76,80,84,88,92..., dimensions={0} | all-to-all | bytes 1048576 | tf_op jit(solution)/shard_map/all_to_all | solution.py:604
  80.1 0.9 %field.1 = f32[4,8,2048]{2,1,0:T(8,128)} custom-call(f32[16,4,8,128]{3,2,1,0:T(8,128)S(1)} %get-tuple-element.35.blocks_ref, f32[16,2,4,8,128]{4,3,2,1,0:T(8,128)S(1)} %all_to_all.10.got_ref), custom_call_target="tpu_custom_call" | custom-call | tf_op jit(solution)/shard_map/field/pallas_call | solution.py:556
  (6 shorter events, 0.1 us)
Async XLA Ops:
  0.6 13.8 %copy-start = (bf16[9,128,128]{2,1,0:T(8,128)(2,1)S(1)}, bf16[9,128,128]{2,1,0:T(8,128)(2,1)}, u32[]{:S(2)}) copy-start(bf16[9,128,128]{2,1,0:T(8,128)(2,1)} %first_ref.1) | copy-start | bytes 884740
  0.6 13.8 %copy-start.1 = (bf16[9,128,128]{2,1,0:T(8,128)(2,1)S(1)}, bf16[9,128,128]{2,1,0:T(8,128)(2,1)}, u32[]{:S(2)}) copy-start(bf16[9,128,128]{2,1,0:T(8,128)(2,1)} %second_ref.1) | copy-start | bytes 884740
  0.7 13.8 %copy-start.2 = (bf16[4,128]{1,0:T(4,128)(2,1)S(1)}, bf16[4,128]{1,0:T(4,128)(2,1)}, u32[]{:S(2)}) copy-start(bf16[4,128]{1,0:T(4,128)(2,1)} %head_ref.3) | copy-start | bytes 3076
  4.8 9.9 %collective-permute-start.1 = (bf16[2048,128]{1,0:T(8,128)(2,1)S(1)}, bf16[2048,128]{1,0:T(8,128)(2,1)S(1)}, u32[]{:S(2)}, u32[]{:S(2)}) collective-permute-start(bf16[2048,128]{1,0:T(8,128)(2,1)S(1)} %get-tuple-element.22), channel_id=1, source_target_pairs={{0,1},{1,0},{2,3},{3,2},{4,5},{5,4},{6,7},{7,6},{8,9},{9,8},{10,11... | collective-permute-start | bytes 1572872 | tf_op jit(solution)/shard_map/ppermute | solution.py:567
  8.1 6.5 %collective-permute-start.2 = (f32[8,128]{1,0:T(8,128)S(1)}, f32[8,128]{1,0:T(8,128)S(1)}, u32[]{:S(2)}, u32[]{:S(2)}) collective-permute-start(f32[8,128]{1,0:T(8,128)S(1)} %get-tuple-element.23.s0), channel_id=1, source_target_pairs={{0,1},{1,0},{2,3},{3,2},{4,5},{5,4},{6,7},{7,6},{8,9},{9,8},{10,11... | collective-permute-start | bytes 12296 | tf_op jit(solution)/shard_map/ppermute | solution.py:567
  8.2 6.4 %collective-permute-start.3 = (f32[8,128]{1,0:T(8,128)S(1)}, f32[8,128]{1,0:T(8,128)S(1)}, u32[]{:S(2)}, u32[]{:S(2)}) collective-permute-start(f32[8,128]{1,0:T(8,128)S(1)} %get-tuple-element.23.s0), channel_id=1, source_target_pairs={{0,2},{1,3},{2,0},{3,1},{4,6},{5,7},{6,4},{7,5},{8,10},{9,11},{10,... | collective-permute-start | bytes 12296 | tf_op jit(solution)/shard_map/ppermute | solution.py:567
  9.2 5.4 %collective-permute-start.4 = (f32[8,128]{1,0:T(8,128)S(1)}, f32[8,128]{1,0:T(8,128)S(1)}, u32[]{:S(2)}, u32[]{:S(2)}) collective-permute-start(f32[8,128]{1,0:T(8,128)S(1)} %get-tuple-element.23.s0), channel_id=1, source_target_pairs={{0,3},{1,2},{2,1},{3,0},{4,7},{5,6},{6,5},{7,4},{8,11},{9,10},{10,... | collective-permute-start | bytes 12296 | tf_op jit(solution)/shard_map/ppermute | solution.py:567
  11.8 12.0 %collective-permute-start = (bf16[2048,128]{1,0:T(8,128)(2,1)S(1)}, bf16[2048,128]{1,0:T(8,128)(2,1)S(1)}, u32[]{:S(2)}, u32[]{:S(2)}) collective-permute-start(bf16[2048,128]{1,0:T(8,128)(2,1)S(1)} %get-tuple-element.21), channel_id=1, source_target_pairs={{1,2},{2,1},{5,6},{6,5},{9,10},{10,9},{13,14},{14,13},{17,18},{18,... | collective-permute-start | bytes 1572872 | tf_op jit(solution)/shard_map/ppermute | solution.py:571
  26.1 11.7 %copy-start.4 = (f32[1,4,8,2048]{3,2,1,0:T(8,128)S(1)}, f32[1,4,8,2048]{3,2,1,0:T(8,128)}, u32[]{:S(2)}) copy-start(f32[1,4,8,2048]{3,2,1,0:T(8,128)} %param.10) | copy-start | bytes 786436
  26.1 11.7 %copy-start.5 = (f32[1,4,8,2048]{3,2,1,0:T(8,128)S(1)}, f32[1,4,8,2048]{3,2,1,0:T(8,128)}, u32[]{:S(2)}) copy-start(f32[1,4,8,2048]{3,2,1,0:T(8,128)} %param.11) | copy-start | bytes 786436
  26.1 4.4 %collective-permute-start.5 = (f32[8,128]{1,0:T(8,128)S(1)}, f32[8,128]{1,0:T(8,128)S(1)}, u32[]{:S(2)}, u32[]{:S(2)}) collective-permute-start(f32[8,128]{1,0:T(8,128)S(1)} %get-tuple-element.31.s0), channel_id=1, source_target_pairs={{0,1},{1,0},{2,3},{3,2},{4,5},{5,4},{6,7},{7,6},{8,9},{9,8},{10,11... | collective-permute-start | bytes 12296 | tf_op jit(solution)/shard_map/ppermute | solution.py:567
  26.2 4.3 %collective-permute-start.6 = (f32[8,128]{1,0:T(8,128)S(1)}, f32[8,128]{1,0:T(8,128)S(1)}, u32[]{:S(2)}, u32[]{:S(2)}) collective-permute-start(f32[8,128]{1,0:T(8,128)S(1)} %get-tuple-element.31.s0), channel_id=1, source_target_pairs={{0,2},{1,3},{2,0},{3,1},{4,6},{5,7},{6,4},{7,5},{8,10},{9,11},{10,... | collective-permute-start | bytes 12296 | tf_op jit(solution)/shard_map/ppermute | solution.py:567
  27.1 4.5 %collective-permute-start.7 = (f32[8,128]{1,0:T(8,128)S(1)}, f32[8,128]{1,0:T(8,128)S(1)}, u32[]{:S(2)}, u32[]{:S(2)}) collective-permute-start(f32[8,128]{1,0:T(8,128)S(1)} %get-tuple-element.31.s0), channel_id=1, source_target_pairs={{0,3},{1,2},{2,1},{3,0},{4,7},{5,6},{6,5},{7,4},{8,11},{9,10},{10,... | collective-permute-start | bytes 12296 | tf_op jit(solution)/shard_map/ppermute | solution.py:567
  32.9 8.5 %collective-permute-start.8 = (f32[4,2048]{1,0:T(4,128)S(1)}, f32[4,2048]{1,0:T(4,128)S(1)}, u32[]{:S(2)}, u32[]{:S(2)}) collective-permute-start(f32[4,2048]{1,0:T(4,128)S(1)} %get-tuple-element.33), channel_id=1, source_target_pairs={{0,1},{1,0},{2,3},{3,2},{4,5},{5,4},{6,7},{7,6},{8,9},{9,8},{10,11... | collective-permute-start | bytes 98312 | tf_op jit(solution)/shard_map/ppermute | solution.py:567
  33.3 8.0 %collective-permute-start.9 = (f32[4,2048]{1,0:T(4,128)S(1)}, f32[4,2048]{1,0:T(4,128)S(1)}, u32[]{:S(2)}, u32[]{:S(2)}) collective-permute-start(f32[4,2048]{1,0:T(4,128)S(1)} %get-tuple-element.34), channel_id=1, source_target_pairs={{1,2},{2,1},{5,6},{6,5},{9,10},{10,9},{13,14},{14,13},{17,18},{18,... | collective-permute-start | bytes 98312 | tf_op jit(solution)/shard_map/ppermute | solution.py:571
  37.8 9.4 %copy-start.6 = (f32[4,8,32]{2,1,0:T(8,128)S(1)}, f32[4,8,32]{2,1,0:T(8,128)}, u32[]{:S(2)}) copy-start(f32[4,8,32]{2,1,0:T(8,128)} %param.12) | copy-start | bytes 12292
  37.8 27.5 %copy-start.3 = (f32[4]{0:T(128)S(1)}, f32[4]{0:T(128)}, u32[]{:S(2)}) copy-start(f32[4]{0:T(128)} %target_ref.1) | copy-start | bytes 52
  42.4 11.5 %all-to-all-start = ((f32[16,4,8,128]{3,2,1,0:T(8,128)}), f32[16,4,8,128]{3,2,1,0:T(8,128)S(1)}, u32[]{:S(2)}, u32[]{:S(2)}) async-start(f32[16,4,8,128]{3,2,1,0:T(8,128)} %get-tuple-element.36), calls=%async_computation | async-start | bytes 524288 | tf_op jit(solution)/shard_map/all_to_all | solution.py:598
  54.0 5.1 %collective-permute-start.10 = (f32[3,4,8,128]{3,2,1,0:T(8,128)S(1)}, f32[3,4,8,128]{3,2,1,0:T(8,128)S(1)}, u32[]{:S(2)}, u32[]{:S(2)}) collective-permute-start(f32[3,4,8,128]{3,2,1,0:T(8,128)S(1)} %sums.1), channel_id=1, source_target_pairs={{0,64},{4,68},{8,72},{12,76},{16,80},{20,84},{24,88},{28,92},{32,9... | collective-permute-start | bytes 147464 | tf_op jit(solution)/shard_map/ppermute | solution.py:601
  59.1 6.3 %collective-permute-start.11 = (f32[3,4,8,128]{3,2,1,0:T(8,128)S(1)}, f32[3,4,8,128]{3,2,1,0:T(8,128)S(1)}, u32[]{:S(2)}, u32[]{:S(2)}) collective-permute-start(f32[3,4,8,128]{3,2,1,0:T(8,128)S(1)} %add.3.one_ref), channel_id=1, source_target_pairs={{0,192},{4,196},{8,200},{12,204},{16,208},{20,212},{24,216},{28,22... | collective-permute-start | bytes 147464 | tf_op jit(solution)/shard_map/ppermute | solution.py:602

commit v5 on v4

--- a/solution.py
+++ b/solution.py
@@ -360,17 +360,18 @@
     return lax.dot_general(left, right, (((1,), (1,)), ((), ())), preferred_element_type=F32)
 
 
-def rim_kernel(first_ref, last_ref, s0, s1, s2, s3, fold_ref, core_ref, far_ref, act):
-    width, chans = act.shape[0], act.shape[1] // 2
+def rim_kernel(first_ref, last_ref, s0, s1, s2, s3, fold_ref, core_ref, far_ref, top_ref, bottom_ref):
+    width, chans = top_ref.shape
     scale, shift = norm_factors([s0, s1, s2, s3], TILES * 2 * width)
     value = silu(first_ref[0].astype(F32) * scale + shift)
-    act[:, pl.ds(0, chans)] = value.astype(BF16)
+    top_ref[...] = value.astype(BF16)
     value = silu(last_ref[last_ref.shape[0] - 1].astype(F32) * scale + shift)
-    act[:, pl.ds(chans, chans)] = value.astype(BF16)
+    bottom_ref[...] = value.astype(BF16)
     none = jnp.zeros((24, chans), BF16)
     before = jnp.concatenate([fold_ref[0:24, :chans], none], axis=1)
     after = jnp.concatenate([none, fold_ref[72:96, chans:]], axis=1)
-    ends = product(jnp.concatenate([before, after], axis=0), act[...])
+    both = jnp.concatenate([top_ref[...], bottom_ref[...]], axis=1)
+    ends = product(jnp.concatenate([before, after], axis=0), both)
     far_ref[...] = columns_joined(ends[0:24])
     core_ref[...] = columns_joined(ends[24:48])
 
@@ -378,42 +379,70 @@
 def rim_call(first, last, stats, fold):
     width, chans = first.shape[1:]
     part = jax.ShapeDtypeStruct((4, width), F32)
+    act = jax.ShapeDtypeStruct((width, chans), BF16)
     return pl.pallas_call(
         rim_kernel,
-        out_shape=(part, part),
+        out_shape=(part, part, act, act),
         in_specs=[VM] * 7,
-        out_specs=(VM, VM),
-        scratch_shapes=[pltpu.VMEM((width, 2 * chans), BF16)],
+        out_specs=(VM,) * 4,
         compiler_params=limit(8),
         name="rim",
     )(first, last, *stats, fold)
 
 
-def taps_kernel(
-    x_ref, first_ref, last_ref, s0, s1, s2, s3, fold_ref, head_ref, state_ref, noise_ref, index_ref, out_ref, *rest
-):
-    rows, width, chans = x_ref.shape
+def base_kernel(x_ref, head_ref, state_ref, noise_ref, index_ref, out_ref, net):
+    rows, width, _ = x_ref.shape
     outs = state_ref.shape[0]
-    half = rows // 2
-    acts, taps, net = rest[:half], rest[half], rest[half + 1]
     even = (lax.axis_index("tile") & 1) == 0
-    scale, shift = norm_factors([s0, s1, s2, s3], rows * width)
     head = head_ref[...].astype(F32)
     head = jnp.concatenate([head, jnp.zeros_like(head)], axis=0)
     none = jnp.zeros_like(head)
     head = jnp.concatenate(
         [jnp.concatenate([head, none], axis=1), jnp.concatenate([none, head], axis=1)], axis=0
     ).astype(BF16)
-    direct = []
+    for pair in range(rows // 2):
+        features = jnp.concatenate([x_ref[2 * pair], x_ref[2 * pair + 1]], axis=1)
+        both = product(head, features)
+        for side in range(2):
+            r = 2 * pair + side
+            for o in range(outs):
+                line = both[8 * side + o : 8 * side + o + 1]
+                net[o, pl.ds(jnp.where(even, r, rows - 1 - r), 1), :] = line
+    keep, stir, push = step_factors(index_ref[0])
+    for t in range(width // 128):
+        at = pl.ds(t * 128, 128)
+        for o in range(outs):
+            direct = keep * state_ref[o, :, at] + stir * noise_ref[o, :, at]
+            out_ref[o, :, at] = direct + push * net[o, :, at]
+
+
+def base_call(xt, head, state, noise, index):
+    return pl.pallas_call(
+        base_kernel,
+        out_shape=jax.ShapeDtypeStruct(state.shape, F32),
+        in_specs=[VM] * 4 + [SM],
+        out_specs=VM,
+        scratch_shapes=[pltpu.VMEM(state.shape, F32)],
+        compiler_params=limit(12),
+        cost_estimate=pl.CostEstimate(flops=1 << 24, bytes_accessed=1 << 20, transcendentals=0),
+        name="base",
+    )(xt, head, state, noise, index)
+
+
+def taps_kernel(first_ref, last_ref, top_ref, bottom_ref, s0, s1, s2, s3, fold_ref, base_ref, index_ref, out_ref, *rest):
+    outs, rows, width = base_ref.shape
+    half = rows // 2
+    acts, taps, net = rest[: rows - 2], rest[rows - 2], rest[rows - 1]
+    acts = (top_ref,) + acts + (bottom_ref,)
+    even = (lax.axis_index("tile") & 1) == 0
+    scale, shift = norm_factors([s0, s1, s2, s3], rows * width)
     for pair in range(half):
-        features = jnp.concatenate([x_ref[2 * pair], x_ref[2 * pair + 1]], axis=1)
-        direct.append(product(head, features))
-        for side in range(2):
-            row = 2 * pair + side
-            value = first_ref[row] if row < 2 else last_ref[row - 2]
-            value = silu(value.astype(F32) * scale + shift)
-            acts[pair][:, pl.ds(side * chans, chans)] = value.astype(BF16)
-        taps[pair] = product(fold_ref[...], acts[pair][...])
+        for row in (2 * pair, 2 * pair + 1):
+            if 0 < row < rows - 1:
+                value = first_ref[row] if row < 2 else last_ref[row - 2]
+                acts[row][...] = silu(value.astype(F32) * scale + shift).astype(BF16)
+        both = jnp.concatenate([acts[2 * pair][...], acts[2 * pair + 1][...]], axis=1)
+        taps[pair] = product(fold_ref[...], both)
     for r in range(rows):
         pair, side = r // 2, r % 2
         total = taps[pair, 24 + 24 * side : 48 + 24 * side]
@@ -421,33 +450,32 @@
             total = total + taps[pair - 1, 72:96]
         if side == 1 and pair + 1 < half:
             total = total + taps[pair + 1, 0:24]
-        both = columns_joined(total) + direct[pair][8 * side : 8 * side + 4]
+        both = columns_joined(total)
         for o in range(outs):
             net[o, pl.ds(jnp.where(even, r, rows - 1 - r), 1), :] = both[o : o + 1]
-    keep, stir, push = step_factors(index_ref[0])
+    push = step_factors(index_ref[0])[2]
     for t in range(width // 128):
         at = pl.ds(t * 128, 128)
         for o in range(outs):
-            direct = keep * state_ref[o, :, at] + stir * noise_ref[o, :, at]
-            out_ref[o, :, at] = direct + push * net[o, :, at]
-
-
-def taps_call(xt, first, last, stats, fold, head, state, noise, index):
-    rows, width, chans = xt.shape
-    half = rows // 2
+            out_ref[o, :, at] = base_ref[o, :, at] + push * net[o, :, at]
+
+
+def taps_call(first, last, top, bottom, stats, fold, base, index):
+    outs, rows, width = base.shape
+    chans = top.shape[1]
     return pl.pallas_call(
         taps_kernel,
-        out_shape=jax.ShapeDtypeStruct(state.shape, F32),
-        in_specs=[VM] * 11 + [SM],
+        out_shape=jax.ShapeDtypeStruct(base.shape, F32),
+        in_specs=[VM] * 10 + [SM],
         out_specs=VM,
-        scratch_shapes=[pltpu.VMEM((width, 2 * chans), BF16)] * half
-        + [pltpu.VMEM((half, 96, width), F32), pltpu.VMEM(state.shape, F32)],
+        scratch_shapes=[pltpu.VMEM((width, chans), BF16)] * (rows - 2)
+        + [pltpu.VMEM((rows // 2, 96, width), F32), pltpu.VMEM(base.shape, F32)],
         compiler_params=limit(24),
         cost_estimate=pl.CostEstimate(
-            flops=6144 * width * chans * half, bytes_accessed=1 << 22, transcendentals=2 * xt.size
+            flops=3072 * width * chans * rows, bytes_accessed=1 << 22, transcendentals=1 << 22
         ),
         name="taps",
-    )(xt, first, last, *stats, fold, head, state, noise, index)
+    )(first, last, top, bottom, *stats, fold, base, index)
 
 
 def step_kernel(part_ref, core_ref, far_ref, index_ref, next_ref, blocks_ref, kept_ref):
@@ -586,11 +614,10 @@
     last, sums, acts = inner_call(xt, core, stats, wt, 1024)
     first, stats = outer_call(acts, far, stats, sums, wt, 1024)
     stats = spread_stats(stats)
-    core, far = rim_call(first, last, stats, fold)
+    base = base_call(xt, head_weight, residual_state[0], noise[0], step_index)
+    core, far, top, bottom = rim_call(first, last, stats, fold)
     core, far = swap(core, 1), far_swap(far)
-    part = taps_call(
-        xt, first, last, stats, fold, head_weight, residual_state[0], noise[0], step_index
-    )
+    part = taps_call(first, last, top, bottom, stats, fold, base, step_index)
     advanced, blocks, kept = step_call(part, core, far, step_index)
     members = lax.axis_size("member")
     size = blocks.shape[0]

time: 81.4 us -> 80.3 us (0.986)
  the two profiles are of different devices: /device:TPU:1 before, /device:TPU:4 now
where the time goes in v5:
time: 80.3 us; the launch traced here: 79.9 us
  starting transfers between devices  28.6 us (36%)
  Pallas kernels  21.6 us (27%)
  waiting for transfers between devices  16.3 us (20%)
  blocking collectives  11.8 us (15%)
  between operations  1.54 us (2%)
    all_to_all x1, blocking collectives, shards(): lax.all_to_all(sent, 'member', 0, 0, tiled=True, axis_index_groups=runs)  11.8 us
    all_to_all x1, waiting for transfers between devices, shards(): lax.all_to_all(blocks, 'member', 0, 0, tiled=True, axis_index_groups=runs)  7.73 us
    ppermute x8, starting transfers between devices, swap(): return lax.ppermute(value, 'tile', [(i, i ^ bits) for i in range(TILES)])  7.29 us
    pallas_call x1, Pallas kernels, inner_call(): pl.pallas_call(functools.partial(inner_kernel, block), out_shape=(jax.Sha...  6.91 us
    ppermute x2, starting transfers between devices, far_swap(): return lax.ppermute(value, 'tile', [(1, 2), (2, 1)])  6.64 us
    all_to_all x1, starting transfers between devices, shards(): lax.all_to_all(blocks, 'member', 0, 0, tiled=True, axis_index_groups=runs)  5.72 us
    ppermute x1, starting transfers between devices, shards(): lax.ppermute(sums, 'member', [(i, i ^ 3 * size) for i in range(members)])  5.39 us
    pallas_call x1, Pallas kernels, features_call(): pl.pallas_call(features_kernel, out_shape=(jax.ShapeDtypeStruct((rows, wi...  4.13 us
  transfers between devices with their start and end apart: 13, of which 6 were waited for; matrix products, arithmetic and copies ran while one was open for 0% of the time, Pallas kernels for 14%

profile of v5, /device:TPU:4, one launch (start us, length us, event | category | flops | bytes accessed | tf_op | source)
XLA Modules:
  0.0 79.9 jit_solution(3789447917204208071)
XLA Ops:
  0.6 0.0 copy-start.4
  0.6 0.0 copy-start.1
  0.7 0.0 copy-start
  0.7 4.1 %features.1 = (bf16[8,2048,128]{2,1,0:T(8,128)(2,1)S(1)}, bf16[2048,128]{1,0:T(8,128)(2,1)S(1)}, bf16[2048,128]{1,0:T(8,128)(2,1)S(1)}, f32[8,128]{1,0:T(8,128)S(1)}) custom-call(bf16[128,8,2048]{2,1,0:T(8,128)(2,1)} %bitcast.7), custom_call_target="tpu_custom_call" | custom-call | tf_op jit(solution)/shard_map/features/pallas_call | solution.py:100
  4.8 0.1 collective-permute-start.1
  4.9 2.4 %collective-permute-start.4 = (f32[8,128]{1,0:T(8,128)S(1)}, f32[8,128]{1,0:T(8,128)S(1)}, u32[]{:S(2)}, u32[]{:S(2)}) collective-permute-start(f32[8,128]{1,0:T(8,128)S(1)} %get-tuple-element.25.s0), channel_id=1, source_target_pairs={{0,3},{1,2},{2,1},{3,0},{4,7},{5,6},{6,5},{7,4},{8,11},{9,10},{10,... | collective-permute-start | bytes 12296 | tf_op jit(solution)/shard_map/ppermute | solution.py:595
  7.3 1.3 %collective-permute-start.3 = (f32[8,128]{1,0:T(8,128)S(1)}, f32[8,128]{1,0:T(8,128)S(1)}, u32[]{:S(2)}, u32[]{:S(2)}) collective-permute-start(f32[8,128]{1,0:T(8,128)S(1)} %get-tuple-element.25.s0), channel_id=1, source_target_pairs={{0,2},{1,3},{2,0},{3,1},{4,6},{5,7},{6,4},{7,5},{8,10},{9,11},{10,... | collective-permute-start | bytes 12296 | tf_op jit(solution)/shard_map/ppermute | solution.py:595
  8.6 0.0 collective-permute-start.2
  8.6 4.3 %collective-permute-start = (bf16[2048,128]{1,0:T(8,128)(2,1)S(1)}, bf16[2048,128]{1,0:T(8,128)(2,1)S(1)}, u32[]{:S(2)}, u32[]{:S(2)}) collective-permute-start(bf16[2048,128]{1,0:T(8,128)(2,1)S(1)} %get-tuple-element.22), channel_id=1, source_target_pairs={{1,2},{2,1},{5,6},{6,5},{9,10},{10,9},{13,14},{14,13},{17,18},{18,... | collective-permute-start | bytes 1572872 | tf_op jit(solution)/shard_map/ppermute | solution.py:599
  12.8 0.0 copy-done.4
  12.8 0.0 copy-done.1
  12.8 0.0 copy-done
  12.8 0.2 weights.1
  13.1 0.0 collective-permute-done.4.s3
  13.1 0.0 collective-permute-done.3.s2
  13.1 0.0 collective-permute-done.2.s1
  13.1 0.0 collective-permute-done.1.core_ref
  13.1 6.9 %inner.1 = (bf16[6,2048,128]{2,1,0:T(8,128)(2,1)S(1)}, f32[3,8,128]{2,1,0:T(8,128)S(1)}, bf16[3,2048,128]{2,1,0:T(8,128)(2,1)S(1)}, bf16[3,2048,128]{2,1,0:T(8,128)(2,1)S(1)}, bf16[3,2048,128]{2,1,0:T(8,128)(2,1)S(1)}) custom-call(bf16[8,2048,128]{2,1,0:T(8,128)(2,1)S(1)} %get-tuple-element.23.x_ref, bf16[2048,128]{1,0:T(8,128)(2,1)S(1)} %collective-permute-done.1.core_ref, ...), custom_call_target="tpu_custom_call" | custom-call | flops 6442450944 | bytes 4194304 | tf_op jit(solution)/shard_map/inner/pallas_call | solution.py:279
  20.0 0.0 copy-start.2
  20.0 0.0 copy-start.3
  20.0 0.5 collective-permute-done.far_ref
  20.6 2.3 %outer.1 = (bf16[2,2048,128]{2,1,0:T(8,128)(2,1)S(1)}, f32[8,128]{1,0:T(8,128)S(1)}) custom-call(bf16[2048,128]{1,0:T(8,128)(2,1)S(1)} %collective-permute-done.far_ref, bf16[3,2048,128]{2,1,0:T(8,128)(2,1)S(1)} %get-tuple-element.27.a0, bf16[3,2048,128]{2,1,0:T(8,128)(2,1)S(1)} %get-tuple-element.28.a1, bf16[3,2048,128]{2,1,0:T(8,128)(2,1)S(1)} %get-tuple-element.29.a2, ...), custom_call_target="tpu_custom_call" | custom-call | tf_op jit(solution)/shard_map/outer/pallas_call | solution.py:322
  22.9 2.4 %collective-permute-start.7 = (f32[8,128]{1,0:T(8,128)S(1)}, f32[8,128]{1,0:T(8,128)S(1)}, u32[]{:S(2)}, u32[]{:S(2)}) collective-permute-start(f32[8,128]{1,0:T(8,128)S(1)} %get-tuple-element.33.s0), channel_id=1, source_target_pairs={{0,3},{1,2},{2,1},{3,0},{4,7},{5,6},{6,5},{7,4},{8,11},{9,10},{10,... | collective-permute-start | bytes 12296 | tf_op jit(solution)/shard_map/ppermute | solution.py:595
  25.3 0.0 collective-permute-start.6
  25.3 1.0 %collective-permute-start.5 = (f32[8,128]{1,0:T(8,128)S(1)}, f32[8,128]{1,0:T(8,128)S(1)}, u32[]{:S(2)}, u32[]{:S(2)}) collective-permute-start(f32[8,128]{1,0:T(8,128)S(1)} %get-tuple-element.33.s0), channel_id=1, source_target_pairs={{0,1},{1,0},{2,3},{3,2},{4,5},{5,4},{6,7},{7,6},{8,9},{9,8},{10,11... | collective-permute-start | bytes 12296 | tf_op jit(solution)/shard_map/ppermute | solution.py:595
  27.0 1.2 %base.1.base_ref = f32[4,8,2048]{2,1,0:T(8,128)S(1)} custom-call(bf16[8,2048,128]{2,1,0:T(8,128)(2,1)S(1)} %get-tuple-element.23.x_ref, bf16[4,128]{1,0:T(4,128)(2,1)S(1)} %copy-done.4, f32[4,8,2048]{2,1,0:T(8,128)S(1)} %bitcast.5, f32[4,8,2048]{2,1,0:T(8,128)S(1)} %bitcast.6, s32[1]{0:T(128)S(6)} %copy.11.index_ref), custom_call_target="tpu_custom_call" | custom-call | flops 16777216 | bytes 1048576 | tf_op jit(solution)/shard_map/base/pallas_call | solution.py:420
  28.2 0.0 collective-permute-done.7.s3
  28.3 2.2 %collective-permute-done.6.s2 = f32[8,128]{1,0:T(8,128)S(1)} collective-permute-done((f32[8,128]{1,0:T(8,128)S(1)}, f32[8,128]{1,0:T(8,128)S(1)}, u32[]{:S(2)}, u32[]{:S(2)}) %collective-permute-start.6) | collective-permute-done | bytes 4128 | tf_op jit(solution)/shard_map/ppermute | solution.py:595
  30.4 0.0 collective-permute-done.5.s1
  30.4 1.3 %rim.1 = (f32[4,2048]{1,0:T(4,128)S(1)}, f32[4,2048]{1,0:T(4,128)S(1)}, bf16[2048,128]{1,0:T(8,128)(2,1)S(1)}, bf16[2048,128]{1,0:T(8,128)(2,1)S(1)}) custom-call(bf16[2,2048,128]{2,1,0:T(8,128)(2,1)S(1)} %get-tuple-element.31.first_ref, bf16[6,2048,128]{2,1,0:T(8,128)(2,1)S(1)} %get-tuple-element.32.last_ref, f32[8,128]{1,0:T(8,128)S(1)} %get-tuple-element.33.s0, ...), custom_call_target="tpu_custom_call" | custom-call | tf_op jit(solution)/shard_map/rim/pallas_call | solution.py:383
  31.7 0.1 collective-permute-start.8
  31.8 2.4 %collective-permute-start.9 = (f32[4,2048]{1,0:T(4,128)S(1)}, f32[4,2048]{1,0:T(4,128)S(1)}, u32[]{:S(2)}, u32[]{:S(2)}) collective-permute-start(f32[4,2048]{1,0:T(4,128)S(1)} %get-tuple-element.38), channel_id=1, source_target_pairs={{1,2},{2,1},{5,6},{6,5},{9,10},{10,9},{13,14},{14,13},{17,18},{18,... | collective-permute-start | bytes 98312 | tf_op jit(solution)/shard_map/ppermute | solution.py:599
  34.2 0.0 copy-start.6
  34.2 0.0 copy-start.5
  34.2 2.9 %taps.1.part_ref = f32[4,8,2048]{2,1,0:T(8,128)S(1)} custom-call(bf16[2,2048,128]{2,1,0:T(8,128)(2,1)S(1)} %get-tuple-element.31.first_ref, bf16[6,2048,128]{2,1,0:T(8,128)(2,1)S(1)} %get-tuple-element.32.last_ref, bf16[2048,128]{1,0:T(8,128)(2,1)S(1)} %get-tuple-element.35.top_ref, bf16[2048,128]{1,0:T(8,128)(2,1)S(1)} %get-tuple-element.36.bottom_ref, ...), custom_call_target="tpu_custom_call" | custom-call | flops 6442450944 | bytes 4194304 | tf_op jit(solution)/shard_map/taps/pallas_call | solution.py:466
  37.1 0.0 collective-permute-done.8.core_ref
  37.1 1.4 %collective-permute-done.9.far_ref = f32[4,2048]{1,0:T(4,128)S(1)} collective-permute-done((f32[4,2048]{1,0:T(4,128)S(1)}, f32[4,2048]{1,0:T(4,128)S(1)}, u32[]{:S(2)}, u32[]{:S(2)}) %collective-permute-start.9) | collective-permute-done | bytes 32800 | tf_op jit(solution)/shard_map/ppermute | solution.py:599
  38.5 1.0 %step.1 = (f32[4,8,2048]{2,1,0:T(8,128)}, f32[16,4,8,128]{3,2,1,0:T(8,128)}, f32[16,4,8,128]{3,2,1,0:T(8,128)S(1)}) custom-call(f32[4,8,2048]{2,1,0:T(8,128)S(1)} %taps.1.part_ref, f32[4,2048]{1,0:T(4,128)S(1)} %collective-permute-done.8.core_ref, f32[4,2048]{1,0:T(4,128)S(1)} %collective-permute-done.9.far_ref, s32[1]{0:T(128)S(6)} %copy.11.index_ref), custom_call_target="tpu_custom_call" | custom-call | tf_op jit(solution)/shard_map/step/pallas_call | solution.py:506
  39.6 5.7 %all-to-all-start = ((f32[16,4,8,128]{3,2,1,0:T(8,128)}), f32[16,4,8,128]{3,2,1,0:T(8,128)S(1)}, u32[]{:S(2)}, u32[]{:S(2)}) async-start(f32[16,4,8,128]{3,2,1,0:T(8,128)} %get-tuple-element.40), calls=%async_computation | async-start | bytes 524288 | tf_op jit(solution)/shard_map/all_to_all | solution.py:625
  45.3 0.1 tile.10.reg_ref
  45.4 7.7 %all-to-all-done.got_ref = f32[16,4,8,128]{3,2,1,0:T(8,128)S(1)} async-done(((f32[16,4,8,128]{3,2,1,0:T(8,128)}), f32[16,4,8,128]{3,2,1,0:T(8,128)S(1)}, u32[]{:S(2)}, u32[]{:S(2)}) %all-to-all-start) | async-done | bytes 262176 | tf_op jit(solution)/shard_map/all_to_all | solution.py:625
  53.2 3.6 %collective-permute-start.10 = (f32[3,4,8,128]{3,2,1,0:T(8,128)S(1)}, f32[3,4,8,128]{3,2,1,0:T(8,128)S(1)}, u32[]{:S(2)}, u32[]{:S(2)}) collective-permute-start(f32[3,4,8,128]{3,2,1,0:T(8,128)S(1)} %sums.1), channel_id=1, source_target_pairs={{0,64},{4,68},{8,72},{12,76},{16,80},{20,84},{24,88},{28,92},{32,9... | collective-permute-start | bytes 147464 | tf_op jit(solution)/shard_map/ppermute | solution.py:628
  56.7 2.4 %collective-permute-done.10 = f32[3,4,8,128]{3,2,1,0:T(8,128)S(1)} collective-permute-done((f32[3,4,8,128]{3,2,1,0:T(8,128)S(1)}, f32[3,4,8,128]{3,2,1,0:T(8,128)S(1)}, u32[]{:S(2)}, u32[]{:S(2)}) %collective-permute-start.10) | collective-permute-done | bytes 49184 | tf_op jit(solution)/shard_map/ppermute | solution.py:628
  59.1 5.4 %collective-permute-start.11 = (f32[3,4,8,128]{3,2,1,0:T(8,128)S(1)}, f32[3,4,8,128]{3,2,1,0:T(8,128)S(1)}, u32[]{:S(2)}, u32[]{:S(2)}) collective-permute-start(f32[3,4,8,128]{3,2,1,0:T(8,128)S(1)} %add.3.one_ref), channel_id=1, source_target_pairs={{0,192},{4,196},{8,200},{12,204},{16,208},{20,212},{24,216},{28,22... | collective-permute-start | bytes 147464 | tf_op jit(solution)/shard_map/ppermute | solution.py:629
  64.5 2.1 %collective-permute-done.11.two_ref = f32[3,4,8,128]{3,2,1,0:T(8,128)S(1)} collective-permute-done((f32[3,4,8,128]{3,2,1,0:T(8,128)S(1)}, f32[3,4,8,128]{3,2,1,0:T(8,128)S(1)}, u32[]{:S(2)}, u32[]{:S(2)}) %collective-permute-start.11) | collective-permute-done | bytes 49184 | tf_op jit(solution)/shard_map/ppermute | solution.py:629
  66.6 0.6 spread.1
  67.2 11.8 %all_to_all.10.got_ref = f32[16,2,4,8,128]{4,3,2,1,0:T(8,128)S(1)} all-to-all(f32[16,2,4,8,128]{4,3,2,1,0:T(8,128)S(1)} %spread.1), channel_id=1, replica_groups={{0,4,8,12,16,20,24,28,32,36,40,44,48,52,56,60},{64,68,72,76,80,84,88,92..., dimensions={0} | all-to-all | bytes 1048576 | tf_op jit(solution)/shard_map/all_to_all | solution.py:631
  79.0 0.9 %field.1 = f32[4,8,2048]{2,1,0:T(8,128)} custom-call(f32[16,4,8,128]{3,2,1,0:T(8,128)S(1)} %get-tuple-element.39.blocks_ref, f32[16,2,4,8,128]{4,3,2,1,0:T(8,128)S(1)} %all_to_all.10.got_ref), custom_call_target="tpu_custom_call" | custom-call | tf_op jit(solution)/shard_map/field/pallas_call | solution.py:584
  (7 shorter events, 0.1 us)
Async XLA Ops:
  0.6 12.2 %copy-start.4 = (bf16[4,128]{1,0:T(4,128)(2,1)S(1)}, bf16[4,128]{1,0:T(4,128)(2,1)}, u32[]{:S(2)}) copy-start(bf16[4,128]{1,0:T(4,128)(2,1)} %head_ref.3) | copy-start | bytes 3076
  0.6 12.2 %copy-start.1 = (bf16[9,128,128]{2,1,0:T(8,128)(2,1)S(1)}, bf16[9,128,128]{2,1,0:T(8,128)(2,1)}, u32[]{:S(2)}) copy-start(bf16[9,128,128]{2,1,0:T(8,128)(2,1)} %second_ref.1) | copy-start | bytes 884740
  0.7 12.2 %copy-start = (bf16[9,128,128]{2,1,0:T(8,128)(2,1)S(1)}, bf16[9,128,128]{2,1,0:T(8,128)(2,1)}, u32[]{:S(2)}) copy-start(bf16[9,128,128]{2,1,0:T(8,128)(2,1)} %first_ref.1) | copy-start | bytes 884740
  4.8 8.3 %collective-permute-start.1 = (bf16[2048,128]{1,0:T(8,128)(2,1)S(1)}, bf16[2048,128]{1,0:T(8,128)(2,1)S(1)}, u32[]{:S(2)}, u32[]{:S(2)}) collective-permute-start(bf16[2048,128]{1,0:T(8,128)(2,1)S(1)} %get-tuple-element.24), channel_id=1, source_target_pairs={{0,1},{1,0},{2,3},{3,2},{4,5},{5,4},{6,7},{7,6},{8,9},{9,8},{10,11... | collective-permute-start | bytes 1572872 | tf_op jit(solution)/shard_map/ppermute | solution.py:595
  4.9 8.2 %collective-permute-start.4 = (f32[8,128]{1,0:T(8,128)S(1)}, f32[8,128]{1,0:T(8,128)S(1)}, u32[]{:S(2)}, u32[]{:S(2)}) collective-permute-start(f32[8,128]{1,0:T(8,128)S(1)} %get-tuple-element.25.s0), channel_id=1, source_target_pairs={{0,3},{1,2},{2,1},{3,0},{4,7},{5,6},{6,5},{7,4},{8,11},{9,10},{10,... | collective-permute-start | bytes 12296 | tf_op jit(solution)/shard_map/ppermute | solution.py:595
  7.3 5.8 %collective-permute-start.3 = (f32[8,128]{1,0:T(8,128)S(1)}, f32[8,128]{1,0:T(8,128)S(1)}, u32[]{:S(2)}, u32[]{:S(2)}) collective-permute-start(f32[8,128]{1,0:T(8,128)S(1)} %get-tuple-element.25.s0), channel_id=1, source_target_pairs={{0,2},{1,3},{2,0},{3,1},{4,6},{5,7},{6,4},{7,5},{8,10},{9,11},{10,... | collective-permute-start | bytes 12296 | tf_op jit(solution)/shard_map/ppermute | solution.py:595
  8.6 4.5 %collective-permute-start.2 = (f32[8,128]{1,0:T(8,128)S(1)}, f32[8,128]{1,0:T(8,128)S(1)}, u32[]{:S(2)}, u32[]{:S(2)}) collective-permute-start(f32[8,128]{1,0:T(8,128)S(1)} %get-tuple-element.25.s0), channel_id=1, source_target_pairs={{0,1},{1,0},{2,3},{3,2},{4,5},{5,4},{6,7},{7,6},{8,9},{9,8},{10,11... | collective-permute-start | bytes 12296 | tf_op jit(solution)/shard_map/ppermute | solution.py:595
  8.6 12.0 %collective-permute-start = (bf16[2048,128]{1,0:T(8,128)(2,1)S(1)}, bf16[2048,128]{1,0:T(8,128)(2,1)S(1)}, u32[]{:S(2)}, u32[]{:S(2)}) collective-permute-start(bf16[2048,128]{1,0:T(8,128)(2,1)S(1)} %get-tuple-element.22), channel_id=1, source_target_pairs={{1,2},{2,1},{5,6},{6,5},{9,10},{10,9},{13,14},{14,13},{17,18},{18,... | collective-permute-start | bytes 1572872 | tf_op jit(solution)/shard_map/ppermute | solution.py:599
  20.0 7.0 %copy-start.2 = (f32[1,4,8,2048]{3,2,1,0:T(8,128)S(1)}, f32[1,4,8,2048]{3,2,1,0:T(8,128)}, u32[]{:S(2)}) copy-start(f32[1,4,8,2048]{3,2,1,0:T(8,128)} %param.10) | copy-start | bytes 786436
  20.0 7.0 %copy-start.3 = (f32[1,4,8,2048]{3,2,1,0:T(8,128)S(1)}, f32[1,4,8,2048]{3,2,1,0:T(8,128)}, u32[]{:S(2)}) copy-start(f32[1,4,8,2048]{3,2,1,0:T(8,128)} %param.11) | copy-start | bytes 786436
  22.9 5.4 %collective-permute-start.7 = (f32[8,128]{1,0:T(8,128)S(1)}, f32[8,128]{1,0:T(8,128)S(1)}, u32[]{:S(2)}, u32[]{:S(2)}) collective-permute-start(f32[8,128]{1,0:T(8,128)S(1)} %get-tuple-element.33.s0), channel_id=1, source_target_pairs={{0,3},{1,2},{2,1},{3,0},{4,7},{5,6},{6,5},{7,4},{8,11},{9,10},{10,... | collective-permute-start | bytes 12296 | tf_op jit(solution)/shard_map/ppermute | solution.py:595
  25.3 5.1 %collective-permute-start.6 = (f32[8,128]{1,0:T(8,128)S(1)}, f32[8,128]{1,0:T(8,128)S(1)}, u32[]{:S(2)}, u32[]{:S(2)}) collective-permute-start(f32[8,128]{1,0:T(8,128)S(1)} %get-tuple-element.33.s0), channel_id=1, source_target_pairs={{0,2},{1,3},{2,0},{3,1},{4,6},{5,7},{6,4},{7,5},{8,10},{9,11},{10,... | collective-permute-start | bytes 12296 | tf_op jit(solution)/shard_map/ppermute | solution.py:595
  25.3 5.1 %collective-permute-start.5 = (f32[8,128]{1,0:T(8,128)S(1)}, f32[8,128]{1,0:T(8,128)S(1)}, u32[]{:S(2)}, u32[]{:S(2)}) collective-permute-start(f32[8,128]{1,0:T(8,128)S(1)} %get-tuple-element.33.s0), channel_id=1, source_target_pairs={{0,1},{1,0},{2,3},{3,2},{4,5},{5,4},{6,7},{7,6},{8,9},{9,8},{10,11... | collective-permute-start | bytes 12296 | tf_op jit(solution)/shard_map/ppermute | solution.py:595
  31.7 5.4 %collective-permute-start.8 = (f32[4,2048]{1,0:T(4,128)S(1)}, f32[4,2048]{1,0:T(4,128)S(1)}, u32[]{:S(2)}, u32[]{:S(2)}) collective-permute-start(f32[4,2048]{1,0:T(4,128)S(1)} %get-tuple-element.37), channel_id=1, source_target_pairs={{0,1},{1,0},{2,3},{3,2},{4,5},{5,4},{6,7},{7,6},{8,9},{9,8},{10,11... | collective-permute-start | bytes 98312 | tf_op jit(solution)/shard_map/ppermute | solution.py:595
  31.8 6.7 %collective-permute-start.9 = (f32[4,2048]{1,0:T(4,128)S(1)}, f32[4,2048]{1,0:T(4,128)S(1)}, u32[]{:S(2)}, u32[]{:S(2)}) collective-permute-start(f32[4,2048]{1,0:T(4,128)S(1)} %get-tuple-element.38), channel_id=1, source_target_pairs={{1,2},{2,1},{5,6},{6,5},{9,10},{10,9},{13,14},{14,13},{17,18},{18,... | collective-permute-start | bytes 98312 | tf_op jit(solution)/shard_map/ppermute | solution.py:599
  34.2 11.1 %copy-start.6 = (f32[4,8,32]{2,1,0:T(8,128)S(1)}, f32[4,8,32]{2,1,0:T(8,128)}, u32[]{:S(2)}) copy-start(f32[4,8,32]{2,1,0:T(8,128)} %param.12) | copy-start | bytes 12292
  34.2 32.4 %copy-start.5 = (f32[4]{0:T(128)S(1)}, f32[4]{0:T(128)}, u32[]{:S(2)}) copy-start(f32[4]{0:T(128)} %target_ref.1) | copy-start | bytes 52
  39.6 13.6 %all-to-all-start = ((f32[16,4,8,128]{3,2,1,0:T(8,128)}), f32[16,4,8,128]{3,2,1,0:T(8,128)S(1)}, u32[]{:S(2)}, u32[]{:S(2)}) async-start(f32[16,4,8,128]{3,2,1,0:T(8,128)} %get-tuple-element.40), calls=%async_computation | async-start | bytes 524288 | tf_op jit(solution)/shard_map/all_to_all | solution.py:625
  53.2 6.0 %collective-permute-start.10 = (f32[3,4,8,128]{3,2,1,0:T(8,128)S(1)}, f32[3,4,8,128]{3,2,1,0:T(8,128)S(1)}, u32[]{:S(2)}, u32[]{:S(2)}) collective-permute-start(f32[3,4,8,128]{3,2,1,0:T(8,128)S(1)} %sums.1), channel_id=1, source_target_pairs={{0,64},{4,68},{8,72},{12,76},{16,80},{20,84},{24,88},{28,92},{32,9... | collective-permute-start | bytes 147464 | tf_op jit(solution)/shard_map/ppermute | solution.py:628
  59.1 7.5 %collective-permute-start.11 = (f32[3,4,8,128]{3,2,1,0:T(8,128)S(1)}, f32[3,4,8,128]{3,2,1,0:T(8,128)S(1)}, u32[]{:S(2)}, u32[]{:S(2)}) collective-permute-start(f32[3,4,8,128]{3,2,1,0:T(8,128)S(1)} %add.3.one_ref), channel_id=1, source_target_pairs={{0,192},{4,196},{8,200},{12,204},{16,208},{20,212},{24,216},{28,22... | collective-permute-start | bytes 147464 | tf_op jit(solution)/shard_map/ppermute | solution.py:629

commit v6 on v5

--- a/solution.py
+++ b/solution.py
@@ -544,22 +544,49 @@
     )(got, reg)
 
 
+STEPS = 32000.0
+
+
+def coded(values):
+    top = jnp.max(jnp.max(jnp.abs(values), axis=1, keepdims=True), axis=0, keepdims=True)
+    power = jnp.clip(jnp.ceil(jnp.log2(jnp.maximum(top, 1e-30))), -100.0, 127.0)
+    power = jnp.broadcast_to(power, (1, values.shape[1]))
+    return jnp.round(values / jnp.exp2(power) * STEPS), power
+
+
+def as_words(values):
+    return values.astype(jnp.int32).astype(jnp.int16)
+
+
+def as_floats(words):
+    return words.astype(jnp.int32).astype(F32)
+
+
 def spread_kernel(members, one_ref, two_ref, target_ref, out_ref):
-    copies, _, outs = out_ref.shape[:3]
+    copies, count = out_ref.shape[:2]
+    outs = count - 1
+    words, powers = [], []
     for o in range(outs):
         mean = (one_ref[0, o] + two_ref[0, o]) / members
         var = (one_ref[1, o] + two_ref[1, o]) / members - mean * mean
         scale = jnp.sqrt(1.0 + target_ref[o] / (var + 1.0))
         offset = one_ref[2, o] + two_ref[2, o] + mean - mean * scale
-        for k in range(copies):
-            out_ref[k, 0, o] = scale
-            out_ref[k, 1, o] = offset
+        high, high_power = coded(scale - 1.0)
+        low, low_power = coded(offset)
+        words.append(as_words(jnp.concatenate([high, low], axis=0)))
+        powers += [high_power, low_power]
+    rest = jnp.zeros((16 - len(powers), powers[0].shape[1]), F32)
+    words.append(as_words(jnp.concatenate(powers + [rest], axis=0)))
+    for k in range(copies):
+        for o in range(count):
+            out_ref[k, o] = words[o]
 
 
 def spread_call(one, two, target, copies, members):
+    _, outs, rows, lanes = one.shape
     return pl.pallas_call(
         functools.partial(spread_kernel, members),
-        out_shape=jax.ShapeDtypeStruct((copies, 2) + one.shape[1:], F32),
+        out_shape=jax.ShapeDtypeStruct((copies, outs + 1, 2 * rows, lanes), jnp.int16),
         in_specs=[VM, VM, SM],
         out_specs=VM,
         compiler_params=limit(8),
@@ -572,10 +599,14 @@
     quarter = width // 512
     slot = lax.broadcasted_iota(jnp.int32, (rows, 128), 1) // 32
     for t in range(quarter):
+        units = [jnp.exp2(as_floats(got_ref[4 * t + j, outs])) / STEPS for j in range(4)]
         for o in range(outs):
-            values = [
-                blocks_ref[4 * t + j, o] * got_ref[4 * t + j, 0, o] + got_ref[4 * t + j, 1, o] for j in range(4)
-            ]
+            values = []
+            for j in range(4):
+                words = as_floats(got_ref[4 * t + j, o])
+                scale = 1.0 + words[:rows] * units[j][2 * o : 2 * o + 1]
+                offset = words[rows:] * units[j][2 * o + 1 : 2 * o + 2]
+                values.append(blocks_ref[4 * t + j, o] * scale + offset)
             for k, mixed in enumerate(turn_quarters(values, slot)):
                 out_ref[o, :, pl.ds((quarter * k + t) * 128, 128)] = mixed
 

time: 80.3 us -> 79.5 us (0.990)
  blocking collectives: 11.8 us -> 10.9 us
    all_to_all x1, blocking collectives: 11.8 us -> 10.9 us  [shards(): lax.all_to_all(sent, 'member', 0, 0, tiled=True, axis_index_groups=runs)]
where the time goes in v6:
time: 79.5 us; the launch traced here: 79.2 us
  starting transfers between devices  28.6 us (36%)
  Pallas kernels  21.7 us (27%)
  waiting for transfers between devices  16.3 us (21%)
  blocking collectives  10.9 us (14%)
  between operations  1.54 us (2%)
    all_to_all x1, blocking collectives, shards(): lax.all_to_all(sent, 'member', 0, 0, tiled=True, axis_index_groups=runs)  10.9 us
    all_to_all x1, waiting for transfers between devices, shards(): lax.all_to_all(blocks, 'member', 0, 0, tiled=True, axis_index_groups=runs)  7.73 us
    ppermute x8, starting transfers between devices, swap(): return lax.ppermute(value, 'tile', [(i, i ^ bits) for i in range(TILES)])  7.29 us
    pallas_call x1, Pallas kernels, inner_call(): pl.pallas_call(functools.partial(inner_kernel, block), out_shape=(jax.Sha...  6.91 us
    ppermute x2, starting transfers between devices, far_swap(): return lax.ppermute(value, 'tile', [(1, 2), (2, 1)])  6.64 us
    all_to_all x1, starting transfers between devices, shards(): lax.all_to_all(blocks, 'member', 0, 0, tiled=True, axis_index_groups=runs)  5.72 us
    ppermute x1, starting transfers between devices, shards(): lax.ppermute(sums, 'member', [(i, i ^ 3 * size) for i in range(members)])  5.39 us
    pallas_call x1, Pallas kernels, features_call(): pl.pallas_call(features_kernel, out_shape=(jax.ShapeDtypeStruct((rows, wi...  4.13 us
  transfers between devices with their start and end apart: 13, of which 6 were waited for; matrix products, arithmetic and copies ran while one was open for 0% of the time, Pallas kernels for 14%

profile of v6, /device:TPU:4, one launch (start us, length us, event | category | flops | bytes accessed | tf_op | source)
XLA Modules:
  0.0 79.2 jit_solution(17295038044376508093)
XLA Ops:
  0.6 0.0 copy-start.4
  0.6 0.0 copy-start.1
  0.7 0.0 copy-start
  0.7 4.1 %features.1 = (bf16[8,2048,128]{2,1,0:T(8,128)(2,1)S(1)}, bf16[2048,128]{1,0:T(8,128)(2,1)S(1)}, bf16[2048,128]{1,0:T(8,128)(2,1)S(1)}, f32[8,128]{1,0:T(8,128)S(1)}) custom-call(bf16[128,8,2048]{2,1,0:T(8,128)(2,1)} %bitcast.7), custom_call_target="tpu_custom_call" | custom-call | tf_op jit(solution)/shard_map/features/pallas_call | solution.py:100
  4.8 0.1 collective-permute-start.1
  4.9 2.4 %collective-permute-start.4 = (f32[8,128]{1,0:T(8,128)S(1)}, f32[8,128]{1,0:T(8,128)S(1)}, u32[]{:S(2)}, u32[]{:S(2)}) collective-permute-start(f32[8,128]{1,0:T(8,128)S(1)} %get-tuple-element.25.s0), channel_id=1, source_target_pairs={{0,3},{1,2},{2,1},{3,0},{4,7},{5,6},{6,5},{7,4},{8,11},{9,10},{10,... | collective-permute-start | bytes 12296 | tf_op jit(solution)/shard_map/ppermute | solution.py:626
  7.3 1.3 %collective-permute-start.3 = (f32[8,128]{1,0:T(8,128)S(1)}, f32[8,128]{1,0:T(8,128)S(1)}, u32[]{:S(2)}, u32[]{:S(2)}) collective-permute-start(f32[8,128]{1,0:T(8,128)S(1)} %get-tuple-element.25.s0), channel_id=1, source_target_pairs={{0,2},{1,3},{2,0},{3,1},{4,6},{5,7},{6,4},{7,5},{8,10},{9,11},{10,... | collective-permute-start | bytes 12296 | tf_op jit(solution)/shard_map/ppermute | solution.py:626
  8.6 0.0 collective-permute-start.2
  8.6 4.3 %collective-permute-start = (bf16[2048,128]{1,0:T(8,128)(2,1)S(1)}, bf16[2048,128]{1,0:T(8,128)(2,1)S(1)}, u32[]{:S(2)}, u32[]{:S(2)}) collective-permute-start(bf16[2048,128]{1,0:T(8,128)(2,1)S(1)} %get-tuple-element.22), channel_id=1, source_target_pairs={{1,2},{2,1},{5,6},{6,5},{9,10},{10,9},{13,14},{14,13},{17,18},{18,... | collective-permute-start | bytes 1572872 | tf_op jit(solution)/shard_map/ppermute | solution.py:630
  12.8 0.0 copy-done.4
  12.8 0.0 copy-done.1
  12.8 0.2 weights.1
  13.1 0.0 collective-permute-done.4.s3
  13.1 0.0 collective-permute-done.3.s2
  13.1 0.0 collective-permute-done.2.s1
  13.1 0.0 collective-permute-done.1.core_ref
  13.1 6.9 %inner.1 = (bf16[6,2048,128]{2,1,0:T(8,128)(2,1)S(1)}, f32[3,8,128]{2,1,0:T(8,128)S(1)}, bf16[3,2048,128]{2,1,0:T(8,128)(2,1)S(1)}, bf16[3,2048,128]{2,1,0:T(8,128)(2,1)S(1)}, bf16[3,2048,128]{2,1,0:T(8,128)(2,1)S(1)}) custom-call(bf16[8,2048,128]{2,1,0:T(8,128)(2,1)S(1)} %get-tuple-element.23.x_ref, bf16[2048,128]{1,0:T(8,128)(2,1)S(1)} %collective-permute-done.1.core_ref, ...), custom_call_target="tpu_custom_call" | custom-call | flops 6442450944 | bytes 4194304 | tf_op jit(solution)/shard_map/inner/pallas_call | solution.py:279
  20.0 0.0 copy-start.2
  20.0 0.0 copy-start.3
  20.0 0.5 collective-permute-done.far_ref
  20.6 2.3 %outer.1 = (bf16[2,2048,128]{2,1,0:T(8,128)(2,1)S(1)}, f32[8,128]{1,0:T(8,128)S(1)}) custom-call(bf16[2048,128]{1,0:T(8,128)(2,1)S(1)} %collective-permute-done.far_ref, bf16[3,2048,128]{2,1,0:T(8,128)(2,1)S(1)} %get-tuple-element.27.a0, bf16[3,2048,128]{2,1,0:T(8,128)(2,1)S(1)} %get-tuple-element.28.a1, bf16[3,2048,128]{2,1,0:T(8,128)(2,1)S(1)} %get-tuple-element.29.a2, ...), custom_call_target="tpu_custom_call" | custom-call | tf_op jit(solution)/shard_map/outer/pallas_call | solution.py:322
  22.9 2.4 %collective-permute-start.7 = (f32[8,128]{1,0:T(8,128)S(1)}, f32[8,128]{1,0:T(8,128)S(1)}, u32[]{:S(2)}, u32[]{:S(2)}) collective-permute-start(f32[8,128]{1,0:T(8,128)S(1)} %get-tuple-element.33.s0), channel_id=1, source_target_pairs={{0,3},{1,2},{2,1},{3,0},{4,7},{5,6},{6,5},{7,4},{8,11},{9,10},{10,... | collective-permute-start | bytes 12296 | tf_op jit(solution)/shard_map/ppermute | solution.py:626
  25.3 0.0 collective-permute-start.6
  25.3 1.0 %collective-permute-start.5 = (f32[8,128]{1,0:T(8,128)S(1)}, f32[8,128]{1,0:T(8,128)S(1)}, u32[]{:S(2)}, u32[]{:S(2)}) collective-permute-start(f32[8,128]{1,0:T(8,128)S(1)} %get-tuple-element.33.s0), channel_id=1, source_target_pairs={{0,1},{1,0},{2,3},{3,2},{4,5},{5,4},{6,7},{7,6},{8,9},{9,8},{10,11... | collective-permute-start | bytes 12296 | tf_op jit(solution)/shard_map/ppermute | solution.py:626
  27.0 1.2 %base.1.base_ref = f32[4,8,2048]{2,1,0:T(8,128)S(1)} custom-call(bf16[8,2048,128]{2,1,0:T(8,128)(2,1)S(1)} %get-tuple-element.23.x_ref, bf16[4,128]{1,0:T(4,128)(2,1)S(1)} %copy-done.4, f32[4,8,2048]{2,1,0:T(8,128)S(1)} %bitcast.5, f32[4,8,2048]{2,1,0:T(8,128)S(1)} %bitcast.6, s32[1]{0:T(128)S(6)} %copy.11.index_ref), custom_call_target="tpu_custom_call" | custom-call | flops 16777216 | bytes 1048576 | tf_op jit(solution)/shard_map/base/pallas_call | solution.py:420
  28.2 0.0 collective-permute-done.7.s3
  28.3 2.2 %collective-permute-done.6.s2 = f32[8,128]{1,0:T(8,128)S(1)} collective-permute-done((f32[8,128]{1,0:T(8,128)S(1)}, f32[8,128]{1,0:T(8,128)S(1)}, u32[]{:S(2)}, u32[]{:S(2)}) %collective-permute-start.6) | collective-permute-done | bytes 4128 | tf_op jit(solution)/shard_map/ppermute | solution.py:626
  30.4 0.0 collective-permute-done.5.s1
  30.4 1.3 %rim.1 = (f32[4,2048]{1,0:T(4,128)S(1)}, f32[4,2048]{1,0:T(4,128)S(1)}, bf16[2048,128]{1,0:T(8,128)(2,1)S(1)}, bf16[2048,128]{1,0:T(8,128)(2,1)S(1)}) custom-call(bf16[2,2048,128]{2,1,0:T(8,128)(2,1)S(1)} %get-tuple-element.31.first_ref, bf16[6,2048,128]{2,1,0:T(8,128)(2,1)S(1)} %get-tuple-element.32.last_ref, f32[8,128]{1,0:T(8,128)S(1)} %get-tuple-element.33.s0, ...), custom_call_target="tpu_custom_call" | custom-call | tf_op jit(solution)/shard_map/rim/pallas_call | solution.py:383
  31.7 0.1 collective-permute-start.8
  31.8 2.4 %collective-permute-start.9 = (f32[4,2048]{1,0:T(4,128)S(1)}, f32[4,2048]{1,0:T(4,128)S(1)}, u32[]{:S(2)}, u32[]{:S(2)}) collective-permute-start(f32[4,2048]{1,0:T(4,128)S(1)} %get-tuple-element.38), channel_id=1, source_target_pairs={{1,2},{2,1},{5,6},{6,5},{9,10},{10,9},{13,14},{14,13},{17,18},{18,... | collective-permute-start | bytes 98312 | tf_op jit(solution)/shard_map/ppermute | solution.py:630
  34.2 0.0 copy-start.6
  34.2 0.0 copy-start.5
  34.2 2.9 %taps.1.part_ref = f32[4,8,2048]{2,1,0:T(8,128)S(1)} custom-call(bf16[2,2048,128]{2,1,0:T(8,128)(2,1)S(1)} %get-tuple-element.31.first_ref, bf16[6,2048,128]{2,1,0:T(8,128)(2,1)S(1)} %get-tuple-element.32.last_ref, bf16[2048,128]{1,0:T(8,128)(2,1)S(1)} %get-tuple-element.35.top_ref, bf16[2048,128]{1,0:T(8,128)(2,1)S(1)} %get-tuple-element.36.bottom_ref, ...), custom_call_target="tpu_custom_call" | custom-call | flops 6442450944 | bytes 4194304 | tf_op jit(solution)/shard_map/taps/pallas_call | solution.py:466
  37.1 0.0 collective-permute-done.8.core_ref
  37.1 1.4 %collective-permute-done.9.far_ref = f32[4,2048]{1,0:T(4,128)S(1)} collective-permute-done((f32[4,2048]{1,0:T(4,128)S(1)}, f32[4,2048]{1,0:T(4,128)S(1)}, u32[]{:S(2)}, u32[]{:S(2)}) %collective-permute-start.9) | collective-permute-done | bytes 32800 | tf_op jit(solution)/shard_map/ppermute | solution.py:630
  38.5 1.0 %step.1 = (f32[4,8,2048]{2,1,0:T(8,128)}, f32[16,4,8,128]{3,2,1,0:T(8,128)}, f32[16,4,8,128]{3,2,1,0:T(8,128)S(1)}) custom-call(f32[4,8,2048]{2,1,0:T(8,128)S(1)} %taps.1.part_ref, f32[4,2048]{1,0:T(4,128)S(1)} %collective-permute-done.8.core_ref, f32[4,2048]{1,0:T(4,128)S(1)} %collective-permute-done.9.far_ref, s32[1]{0:T(128)S(6)} %copy.11.index_ref), custom_call_target="tpu_custom_call" | custom-call | tf_op jit(solution)/shard_map/step/pallas_call | solution.py:506
  39.6 5.7 %all-to-all-start = ((f32[16,4,8,128]{3,2,1,0:T(8,128)}), f32[16,4,8,128]{3,2,1,0:T(8,128)S(1)}, u32[]{:S(2)}, u32[]{:S(2)}) async-start(f32[16,4,8,128]{3,2,1,0:T(8,128)} %get-tuple-element.40), calls=%async_computation | async-start | bytes 524288 | tf_op jit(solution)/shard_map/all_to_all | solution.py:656
  45.3 0.0 copy-done.6
  45.3 0.1 tile.10.reg_ref
  45.4 7.7 %all-to-all-done.got_ref = f32[16,4,8,128]{3,2,1,0:T(8,128)S(1)} async-done(((f32[16,4,8,128]{3,2,1,0:T(8,128)}), f32[16,4,8,128]{3,2,1,0:T(8,128)S(1)}, u32[]{:S(2)}, u32[]{:S(2)}) %all-to-all-start) | async-done | bytes 262176 | tf_op jit(solution)/shard_map/all_to_all | solution.py:656
  53.2 3.6 %collective-permute-start.10 = (f32[3,4,8,128]{3,2,1,0:T(8,128)S(1)}, f32[3,4,8,128]{3,2,1,0:T(8,128)S(1)}, u32[]{:S(2)}, u32[]{:S(2)}) collective-permute-start(f32[3,4,8,128]{3,2,1,0:T(8,128)S(1)} %sums.1), channel_id=1, source_target_pairs={{0,64},{4,68},{8,72},{12,76},{16,80},{20,84},{24,88},{28,92},{32,9... | collective-permute-start | bytes 147464 | tf_op jit(solution)/shard_map/ppermute | solution.py:659
  56.7 2.4 %collective-permute-done.10 = f32[3,4,8,128]{3,2,1,0:T(8,128)S(1)} collective-permute-done((f32[3,4,8,128]{3,2,1,0:T(8,128)S(1)}, f32[3,4,8,128]{3,2,1,0:T(8,128)S(1)}, u32[]{:S(2)}, u32[]{:S(2)}) %collective-permute-start.10) | collective-permute-done | bytes 49184 | tf_op jit(solution)/shard_map/ppermute | solution.py:659
  59.1 5.4 %collective-permute-start.11 = (f32[3,4,8,128]{3,2,1,0:T(8,128)S(1)}, f32[3,4,8,128]{3,2,1,0:T(8,128)S(1)}, u32[]{:S(2)}, u32[]{:S(2)}) collective-permute-start(f32[3,4,8,128]{3,2,1,0:T(8,128)S(1)} %add.3.one_ref), channel_id=1, source_target_pairs={{0,192},{4,196},{8,200},{12,204},{16,208},{20,212},{24,216},{28,22... | collective-permute-start | bytes 147464 | tf_op jit(solution)/shard_map/ppermute | solution.py:660
  64.5 2.1 %collective-permute-done.11.two_ref = f32[3,4,8,128]{3,2,1,0:T(8,128)S(1)} collective-permute-done((f32[3,4,8,128]{3,2,1,0:T(8,128)S(1)}, f32[3,4,8,128]{3,2,1,0:T(8,128)S(1)}, u32[]{:S(2)}, u32[]{:S(2)}) %collective-permute-start.11) | collective-permute-done | bytes 49184 | tf_op jit(solution)/shard_map/ppermute | solution.py:660
  66.6 0.7 spread.1
  67.3 10.9 %all_to_all.10.got_ref = s16[16,5,16,128]{3,2,1,0:T(8,128)(2,1)S(1)} all-to-all(s16[16,5,16,128]{3,2,1,0:T(8,128)(2,1)S(1)} %spread.1), channel_id=1, replica_groups={{0,4,8,12,16,20,24,28,32,36,40,44,48,52,56,60},{64,68,72,76,80,84,88,92..., dimensions={0} | all-to-all | bytes 655360 | tf_op jit(solution)/shard_map/all_to_all | solution.py:662
  78.2 1.0 %field.1 = f32[4,8,2048]{2,1,0:T(8,128)} custom-call(f32[16,4,8,128]{3,2,1,0:T(8,128)S(1)} %get-tuple-element.39.blocks_ref, s16[16,5,16,128]{3,2,1,0:T(8,128)(2,1)S(1)} %all_to_all.10.got_ref), custom_call_target="tpu_custom_call" | custom-call | tf_op jit(solution)/shard_map/field/pallas_call | solution.py:615
  (7 shorter events, 0.1 us)
Async XLA Ops:
  0.6 12.2 %copy-start.4 = (bf16[4,128]{1,0:T(4,128)(2,1)S(1)}, bf16[4,128]{1,0:T(4,128)(2,1)}, u32[]{:S(2)}) copy-start(bf16[4,128]{1,0:T(4,128)(2,1)} %head_ref.3) | copy-start | bytes 3076
  0.6 12.2 %copy-start.1 = (bf16[9,128,128]{2,1,0:T(8,128)(2,1)S(1)}, bf16[9,128,128]{2,1,0:T(8,128)(2,1)}, u32[]{:S(2)}) copy-start(bf16[9,128,128]{2,1,0:T(8,128)(2,1)} %second_ref.1) | copy-start | bytes 884740
  0.7 12.2 %copy-start = (bf16[9,128,128]{2,1,0:T(8,128)(2,1)S(1)}, bf16[9,128,128]{2,1,0:T(8,128)(2,1)}, u32[]{:S(2)}) copy-start(bf16[9,128,128]{2,1,0:T(8,128)(2,1)} %first_ref.1) | copy-start | bytes 884740
  4.8 8.3 %collective-permute-start.1 = (bf16[2048,128]{1,0:T(8,128)(2,1)S(1)}, bf16[2048,128]{1,0:T(8,128)(2,1)S(1)}, u32[]{:S(2)}, u32[]{:S(2)}) collective-permute-start(bf16[2048,128]{1,0:T(8,128)(2,1)S(1)} %get-tuple-element.24), channel_id=1, source_target_pairs={{0,1},{1,0},{2,3},{3,2},{4,5},{5,4},{6,7},{7,6},{8,9},{9,8},{10,11... | collective-permute-start | bytes 1572872 | tf_op jit(solution)/shard_map/ppermute | solution.py:626
  4.9 8.2 %collective-permute-start.4 = (f32[8,128]{1,0:T(8,128)S(1)}, f32[8,128]{1,0:T(8,128)S(1)}, u32[]{:S(2)}, u32[]{:S(2)}) collective-permute-start(f32[8,128]{1,0:T(8,128)S(1)} %get-tuple-element.25.s0), channel_id=1, source_target_pairs={{0,3},{1,2},{2,1},{3,0},{4,7},{5,6},{6,5},{7,4},{8,11},{9,10},{10,... | collective-permute-start | bytes 12296 | tf_op jit(solution)/shard_map/ppermute | solution.py:626
  7.3 5.8 %collective-permute-start.3 = (f32[8,128]{1,0:T(8,128)S(1)}, f32[8,128]{1,0:T(8,128)S(1)}, u32[]{:S(2)}, u32[]{:S(2)}) collective-permute-start(f32[8,128]{1,0:T(8,128)S(1)} %get-tuple-element.25.s0), channel_id=1, source_target_pairs={{0,2},{1,3},{2,0},{3,1},{4,6},{5,7},{6,4},{7,5},{8,10},{9,11},{10,... | collective-permute-start | bytes 12296 | tf_op jit(solution)/shard_map/ppermute | solution.py:626
  8.6 4.5 %collective-permute-start.2 = (f32[8,128]{1,0:T(8,128)S(1)}, f32[8,128]{1,0:T(8,128)S(1)}, u32[]{:S(2)}, u32[]{:S(2)}) collective-permute-start(f32[8,128]{1,0:T(8,128)S(1)} %get-tuple-element.25.s0), channel_id=1, source_target_pairs={{0,1},{1,0},{2,3},{3,2},{4,5},{5,4},{6,7},{7,6},{8,9},{9,8},{10,11... | collective-permute-start | bytes 12296 | tf_op jit(solution)/shard_map/ppermute | solution.py:626
  8.6 12.0 %collective-permute-start = (bf16[2048,128]{1,0:T(8,128)(2,1)S(1)}, bf16[2048,128]{1,0:T(8,128)(2,1)S(1)}, u32[]{:S(2)}, u32[]{:S(2)}) collective-permute-start(bf16[2048,128]{1,0:T(8,128)(2,1)S(1)} %get-tuple-element.22), channel_id=1, source_target_pairs={{1,2},{2,1},{5,6},{6,5},{9,10},{10,9},{13,14},{14,13},{17,18},{18,... | collective-permute-start | bytes 1572872 | tf_op jit(solution)/shard_map/ppermute | solution.py:630
  20.0 7.0 %copy-start.2 = (f32[1,4,8,2048]{3,2,1,0:T(8,128)S(1)}, f32[1,4,8,2048]{3,2,1,0:T(8,128)}, u32[]{:S(2)}) copy-start(f32[1,4,8,2048]{3,2,1,0:T(8,128)} %param.10) | copy-start | bytes 786436
  20.0 7.0 %copy-start.3 = (f32[1,4,8,2048]{3,2,1,0:T(8,128)S(1)}, f32[1,4,8,2048]{3,2,1,0:T(8,128)}, u32[]{:S(2)}) copy-start(f32[1,4,8,2048]{3,2,1,0:T(8,128)} %param.11) | copy-start | bytes 786436
  22.9 5.4 %collective-permute-start.7 = (f32[8,128]{1,0:T(8,128)S(1)}, f32[8,128]{1,0:T(8,128)S(1)}, u32[]{:S(2)}, u32[]{:S(2)}) collective-permute-start(f32[8,128]{1,0:T(8,128)S(1)} %get-tuple-element.33.s0), channel_id=1, source_target_pairs={{0,3},{1,2},{2,1},{3,0},{4,7},{5,6},{6,5},{7,4},{8,11},{9,10},{10,... | collective-permute-start | bytes 12296 | tf_op jit(solution)/shard_map/ppermute | solution.py:626
  25.3 5.1 %collective-permute-start.6 = (f32[8,128]{1,0:T(8,128)S(1)}, f32[8,128]{1,0:T(8,128)S(1)}, u32[]{:S(2)}, u32[]{:S(2)}) collective-permute-start(f32[8,128]{1,0:T(8,128)S(1)} %get-tuple-element.33.s0), channel_id=1, source_target_pairs={{0,2},{1,3},{2,0},{3,1},{4,6},{5,7},{6,4},{7,5},{8,10},{9,11},{10,... | collective-permute-start | bytes 12296 | tf_op jit(solution)/shard_map/ppermute | solution.py:626
  25.3 5.1 %collective-permute-start.5 = (f32[8,128]{1,0:T(8,128)S(1)}, f32[8,128]{1,0:T(8,128)S(1)}, u32[]{:S(2)}, u32[]{:S(2)}) collective-permute-start(f32[8,128]{1,0:T(8,128)S(1)} %get-tuple-element.33.s0), channel_id=1, source_target_pairs={{0,1},{1,0},{2,3},{3,2},{4,5},{5,4},{6,7},{7,6},{8,9},{9,8},{10,11... | collective-permute-start | bytes 12296 | tf_op jit(solution)/shard_map/ppermute | solution.py:626
  31.7 5.4 %collective-permute-start.8 = (f32[4,2048]{1,0:T(4,128)S(1)}, f32[4,2048]{1,0:T(4,128)S(1)}, u32[]{:S(2)}, u32[]{:S(2)}) collective-permute-start(f32[4,2048]{1,0:T(4,128)S(1)} %get-tuple-element.37), channel_id=1, source_target_pairs={{0,1},{1,0},{2,3},{3,2},{4,5},{5,4},{6,7},{7,6},{8,9},{9,8},{10,11... | collective-permute-start | bytes 98312 | tf_op jit(solution)/shard_map/ppermute | solution.py:626
  31.8 6.7 %collective-permute-start.9 = (f32[4,2048]{1,0:T(4,128)S(1)}, f32[4,2048]{1,0:T(4,128)S(1)}, u32[]{:S(2)}, u32[]{:S(2)}) collective-permute-start(f32[4,2048]{1,0:T(4,128)S(1)} %get-tuple-element.38), channel_id=1, source_target_pairs={{1,2},{2,1},{5,6},{6,5},{9,10},{10,9},{13,14},{14,13},{17,18},{18,... | collective-permute-start | bytes 98312 | tf_op jit(solution)/shard_map/ppermute | solution.py:630
  34.2 11.1 %copy-start.6 = (f32[4,8,32]{2,1,0:T(8,128)S(1)}, f32[4,8,32]{2,1,0:T(8,128)}, u32[]{:S(2)}) copy-start(f32[4,8,32]{2,1,0:T(8,128)} %param.12) | copy-start | bytes 12292
  34.2 32.4 %copy-start.5 = (f32[4]{0:T(128)S(1)}, f32[4]{0:T(128)}, u32[]{:S(2)}) copy-start(f32[4]{0:T(128)} %target_ref.1) | copy-start | bytes 52
  39.6 13.6 %all-to-all-start = ((f32[16,4,8,128]{3,2,1,0:T(8,128)}), f32[16,4,8,128]{3,2,1,0:T(8,128)S(1)}, u32[]{:S(2)}, u32[]{:S(2)}) async-start(f32[16,4,8,128]{3,2,1,0:T(8,128)} %get-tuple-element.40), calls=%async_computation | async-start | bytes 524288 | tf_op jit(solution)/shard_map/all_to_all | solution.py:656
  53.2 6.0 %collective-permute-start.10 = (f32[3,4,8,128]{3,2,1,0:T(8,128)S(1)}, f32[3,4,8,128]{3,2,1,0:T(8,128)S(1)}, u32[]{:S(2)}, u32[]{:S(2)}) collective-permute-start(f32[3,4,8,128]{3,2,1,0:T(8,128)S(1)} %sums.1), channel_id=1, source_target_pairs={{0,64},{4,68},{8,72},{12,76},{16,80},{20,84},{24,88},{28,92},{32,9... | collective-permute-start | bytes 147464 | tf_op jit(solution)/shard_map/ppermute | solution.py:659
  59.1 7.5 %collective-permute-start.11 = (f32[3,4,8,128]{3,2,1,0:T(8,128)S(1)}, f32[3,4,8,128]{3,2,1,0:T(8,128)S(1)}, u32[]{:S(2)}, u32[]{:S(2)}) collective-permute-start(f32[3,4,8,128]{3,2,1,0:T(8,128)S(1)} %add.3.one_ref), channel_id=1, source_target_pairs={{0,192},{4,196},{8,200},{12,204},{16,208},{20,212},{24,216},{28,22... | collective-permute-start | bytes 147464 | tf_op jit(solution)/shard_map/ppermute | solution.py:660

commit v7 on v6

--- a/solution.py
+++ b/solution.py
@@ -141,7 +141,7 @@
     return jnp.where(even, tap, 3 * (2 - tap // 3) + tap % 3)
 
 
-def weights_kernel(first_ref, second_ref, head_ref, wt_ref, fold_ref):
+def weights_kernel(first_ref, second_ref, head_ref, wt_ref, fold_ref, ends_ref):
     chans = first_ref.shape[1]
     even = (lax.axis_index("tile") & 1) == 0
     wt_ref[...] = jnp.zeros(wt_ref.shape, BF16)
@@ -165,6 +165,9 @@
     left = jnp.concatenate([lines[2], lines[1], lines[0], none], axis=0)
     right = jnp.concatenate([none, lines[2], lines[1], lines[0]], axis=0)
     fold_ref[...] = jnp.concatenate([left, right], axis=1).astype(BF16)
+    left = jnp.concatenate([lines[2], none], axis=0)
+    right = jnp.concatenate([none, lines[0]], axis=0)
+    ends_ref[...] = jnp.concatenate([left, right], axis=1).astype(BF16)
 
 
 def weights_call(first, second, head):
@@ -174,9 +177,10 @@
         out_shape=(
             jax.ShapeDtypeStruct((12 * chans, 2 * chans), BF16),
             jax.ShapeDtypeStruct((96, 2 * chans), BF16),
+            jax.ShapeDtypeStruct((48, 2 * chans), BF16),
         ),
         in_specs=[VM] * 3,
-        out_specs=(VM, VM),
+        out_specs=(VM, VM, VM),
         compiler_params=limit(16),
         cost_estimate=pl.CostEstimate(flops=1 << 22, bytes_accessed=1 << 21, transcendentals=0),
         name="weights",
@@ -360,23 +364,20 @@
     return lax.dot_general(left, right, (((1,), (1,)), ((), ())), preferred_element_type=F32)
 
 
-def rim_kernel(first_ref, last_ref, s0, s1, s2, s3, fold_ref, core_ref, far_ref, top_ref, bottom_ref):
+def rim_kernel(first_ref, last_ref, s0, s1, s2, s3, ends_ref, core_ref, far_ref, top_ref, bottom_ref):
     width, chans = top_ref.shape
     scale, shift = norm_factors([s0, s1, s2, s3], TILES * 2 * width)
     value = silu(first_ref[0].astype(F32) * scale + shift)
     top_ref[...] = value.astype(BF16)
     value = silu(last_ref[last_ref.shape[0] - 1].astype(F32) * scale + shift)
     bottom_ref[...] = value.astype(BF16)
-    none = jnp.zeros((24, chans), BF16)
-    before = jnp.concatenate([fold_ref[0:24, :chans], none], axis=1)
-    after = jnp.concatenate([none, fold_ref[72:96, chans:]], axis=1)
     both = jnp.concatenate([top_ref[...], bottom_ref[...]], axis=1)
-    ends = product(jnp.concatenate([before, after], axis=0), both)
+    ends = product(ends_ref[...], both)
     far_ref[...] = columns_joined(ends[0:24])
     core_ref[...] = columns_joined(ends[24:48])
 
 
-def rim_call(first, last, stats, fold):
+def rim_call(first, last, stats, ends):
     width, chans = first.shape[1:]
     part = jax.ShapeDtypeStruct((4, width), F32)
     act = jax.ShapeDtypeStruct((width, chans), BF16)
@@ -387,7 +388,7 @@
         out_specs=(VM,) * 4,
         compiler_params=limit(8),
         name="rim",
-    )(first, last, *stats, fold)
+    )(first, last, *stats, ends)
 
 
 def base_kernel(x_ref, head_ref, state_ref, noise_ref, index_ref, out_ref, net):
@@ -641,12 +642,12 @@
     xt, core, far, stats = features_call(member, 512)
     stats = spread_stats(stats)
     core, far = swap(core, 1), far_swap(far)
-    wt, fold = weights_call(conv_first, conv_second, head_weight)
+    wt, fold, ends = weights_call(conv_first, conv_second, head_weight)
     last, sums, acts = inner_call(xt, core, stats, wt, 1024)
     first, stats = outer_call(acts, far, stats, sums, wt, 1024)
     stats = spread_stats(stats)
     base = base_call(xt, head_weight, residual_state[0], noise[0], step_index)
-    core, far, top, bottom = rim_call(first, last, stats, fold)
+    core, far, top, bottom = rim_call(first, last, stats, ends)
     core, far = swap(core, 1), far_swap(far)
     part = taps_call(first, last, top, bottom, stats, fold, base, step_index)
     advanced, blocks, kept = step_call(part, core, far, step_index)

time: 79.5 us -> 79.5 us (level)
  no operation moved by 1% of the time
where the time goes in v7:
time: 79.5 us; the launch traced here: 79.2 us
  starting transfers between devices  28.6 us (36%)
  Pallas kernels  21.7 us (27%)
  waiting for transfers between devices  16.3 us (21%)
  blocking collectives  10.9 us (14%)
  between operations  1.54 us (2%)
    all_to_all x1, blocking collectives, shards(): lax.all_to_all(sent, 'member', 0, 0, tiled=True, axis_index_groups=runs)  10.9 us
    all_to_all x1, waiting for transfers between devices, shards(): lax.all_to_all(blocks, 'member', 0, 0, tiled=True, axis_index_groups=runs)  7.73 us
    ppermute x8, starting transfers between devices, swap(): return lax.ppermute(value, 'tile', [(i, i ^ bits) for i in range(TILES)])  7.29 us
    pallas_call x1, Pallas kernels, inner_call(): pl.pallas_call(functools.partial(inner_kernel, block), out_shape=(jax.Sha...  6.89 us
    ppermute x2, starting transfers between devices, far_swap(): return lax.ppermute(value, 'tile', [(1, 2), (2, 1)])  6.64 us
    all_to_all x1, starting transfers between devices, shards(): lax.all_to_all(blocks, 'member', 0, 0, tiled=True, axis_index_groups=runs)  5.72 us
    ppermute x1, starting transfers between devices, shards(): lax.ppermute(sums, 'member', [(i, i ^ 3 * size) for i in range(members)])  5.38 us
    pallas_call x1, Pallas kernels, features_call(): pl.pallas_call(features_kernel, out_shape=(jax.ShapeDtypeStruct((rows, wi...  4.13 us
  transfers between devices with their start and end apart: 13, of which 6 were waited for; matrix products, arithmetic and copies ran while one was open for 0% of the time, Pallas kernels for 14%

profile of v7, /device:TPU:4, one launch (start us, length us, event | category | flops | bytes accessed | tf_op | source)
XLA Modules:
  0.0 79.2 jit_solution(13506980257291855778)
XLA Ops:
  0.6 0.0 copy-start.4
  0.6 0.0 copy-start.1
  0.7 0.0 copy-start
  0.7 4.1 %features.1 = (bf16[8,2048,128]{2,1,0:T(8,128)(2,1)S(1)}, bf16[2048,128]{1,0:T(8,128)(2,1)S(1)}, bf16[2048,128]{1,0:T(8,128)(2,1)S(1)}, f32[8,128]{1,0:T(8,128)S(1)}) custom-call(bf16[128,8,2048]{2,1,0:T(8,128)(2,1)} %bitcast.7), custom_call_target="tpu_custom_call" | custom-call | tf_op jit(solution)/shard_map/features/pallas_call | solution.py:100
  4.8 0.1 collective-permute-start.1
  4.9 2.4 %collective-permute-start.4 = (f32[8,128]{1,0:T(8,128)S(1)}, f32[8,128]{1,0:T(8,128)S(1)}, u32[]{:S(2)}, u32[]{:S(2)}) collective-permute-start(f32[8,128]{1,0:T(8,128)S(1)} %get-tuple-element.26.s0), channel_id=1, source_target_pairs={{0,3},{1,2},{2,1},{3,0},{4,7},{5,6},{6,5},{7,4},{8,11},{9,10},{10,... | collective-permute-start | bytes 12296 | tf_op jit(solution)/shard_map/ppermute | solution.py:627
  7.3 1.3 %collective-permute-start.3 = (f32[8,128]{1,0:T(8,128)S(1)}, f32[8,128]{1,0:T(8,128)S(1)}, u32[]{:S(2)}, u32[]{:S(2)}) collective-permute-start(f32[8,128]{1,0:T(8,128)S(1)} %get-tuple-element.26.s0), channel_id=1, source_target_pairs={{0,2},{1,3},{2,0},{3,1},{4,6},{5,7},{6,4},{7,5},{8,10},{9,11},{10,... | collective-permute-start | bytes 12296 | tf_op jit(solution)/shard_map/ppermute | solution.py:627
  8.6 0.0 collective-permute-start.2
  8.6 4.3 %collective-permute-start = (bf16[2048,128]{1,0:T(8,128)(2,1)S(1)}, bf16[2048,128]{1,0:T(8,128)(2,1)S(1)}, u32[]{:S(2)}, u32[]{:S(2)}) collective-permute-start(bf16[2048,128]{1,0:T(8,128)(2,1)S(1)} %get-tuple-element.23), channel_id=1, source_target_pairs={{1,2},{2,1},{5,6},{6,5},{9,10},{10,9},{13,14},{14,13},{17,18},{18,... | collective-permute-start | bytes 1572872 | tf_op jit(solution)/shard_map/ppermute | solution.py:631
  12.8 0.0 copy-done.4
  12.8 0.0 copy-done.1
  12.8 0.2 weights.1
  13.1 0.0 collective-permute-done.4.s3
  13.1 0.0 collective-permute-done.3.s2
  13.1 0.0 collective-permute-done.2.s1
  13.1 0.0 collective-permute-done.1.core_ref
  13.1 6.9 %inner.1 = (bf16[6,2048,128]{2,1,0:T(8,128)(2,1)S(1)}, f32[3,8,128]{2,1,0:T(8,128)S(1)}, bf16[3,2048,128]{2,1,0:T(8,128)(2,1)S(1)}, bf16[3,2048,128]{2,1,0:T(8,128)(2,1)S(1)}, bf16[3,2048,128]{2,1,0:T(8,128)(2,1)S(1)}) custom-call(bf16[8,2048,128]{2,1,0:T(8,128)(2,1)S(1)} %get-tuple-element.24.x_ref, bf16[2048,128]{1,0:T(8,128)(2,1)S(1)} %collective-permute-done.1.core_ref, ...), custom_call_target="tpu_custom_call" | custom-call | flops 6442450944 | bytes 4194304 | tf_op jit(solution)/shard_map/inner/pallas_call | solution.py:283
  20.0 0.0 copy-start.2
  20.0 0.0 copy-start.3
  20.0 0.5 collective-permute-done.far_ref
  20.6 2.3 %outer.1 = (bf16[2,2048,128]{2,1,0:T(8,128)(2,1)S(1)}, f32[8,128]{1,0:T(8,128)S(1)}) custom-call(bf16[2048,128]{1,0:T(8,128)(2,1)S(1)} %collective-permute-done.far_ref, bf16[3,2048,128]{2,1,0:T(8,128)(2,1)S(1)} %get-tuple-element.28.a0, bf16[3,2048,128]{2,1,0:T(8,128)(2,1)S(1)} %get-tuple-element.29.a1, bf16[3,2048,128]{2,1,0:T(8,128)(2,1)S(1)} %get-tuple-element.30.a2, ...), custom_call_target="tpu_custom_call" | custom-call | tf_op jit(solution)/shard_map/outer/pallas_call | solution.py:326
  22.9 2.4 %collective-permute-start.7 = (f32[8,128]{1,0:T(8,128)S(1)}, f32[8,128]{1,0:T(8,128)S(1)}, u32[]{:S(2)}, u32[]{:S(2)}) collective-permute-start(f32[8,128]{1,0:T(8,128)S(1)} %get-tuple-element.34.s0), channel_id=1, source_target_pairs={{0,3},{1,2},{2,1},{3,0},{4,7},{5,6},{6,5},{7,4},{8,11},{9,10},{10,... | collective-permute-start | bytes 12296 | tf_op jit(solution)/shard_map/ppermute | solution.py:627
  25.3 0.0 collective-permute-start.6
  25.3 1.0 %collective-permute-start.5 = (f32[8,128]{1,0:T(8,128)S(1)}, f32[8,128]{1,0:T(8,128)S(1)}, u32[]{:S(2)}, u32[]{:S(2)}) collective-permute-start(f32[8,128]{1,0:T(8,128)S(1)} %get-tuple-element.34.s0), channel_id=1, source_target_pairs={{0,1},{1,0},{2,3},{3,2},{4,5},{5,4},{6,7},{7,6},{8,9},{9,8},{10,11... | collective-permute-start | bytes 12296 | tf_op jit(solution)/shard_map/ppermute | solution.py:627
  27.0 1.2 %base.1.base_ref = f32[4,8,2048]{2,1,0:T(8,128)S(1)} custom-call(bf16[8,2048,128]{2,1,0:T(8,128)(2,1)S(1)} %get-tuple-element.24.x_ref, bf16[4,128]{1,0:T(4,128)(2,1)S(1)} %copy-done.4, f32[4,8,2048]{2,1,0:T(8,128)S(1)} %bitcast.5, f32[4,8,2048]{2,1,0:T(8,128)S(1)} %bitcast.6, s32[1]{0:T(128)S(6)} %copy.11.index_ref), custom_call_target="tpu_custom_call" | custom-call | flops 16777216 | bytes 1048576 | tf_op jit(solution)/shard_map/base/pallas_call | solution.py:421
  28.2 0.0 collective-permute-done.7.s3
  28.3 2.2 %collective-permute-done.6.s2 = f32[8,128]{1,0:T(8,128)S(1)} collective-permute-done((f32[8,128]{1,0:T(8,128)S(1)}, f32[8,128]{1,0:T(8,128)S(1)}, u32[]{:S(2)}, u32[]{:S(2)}) %collective-permute-start.6) | collective-permute-done | bytes 4128 | tf_op jit(solution)/shard_map/ppermute | solution.py:627
  30.4 0.0 collective-permute-done.5.s1
  30.4 1.3 %rim.1 = (f32[4,2048]{1,0:T(4,128)S(1)}, f32[4,2048]{1,0:T(4,128)S(1)}, bf16[2048,128]{1,0:T(8,128)(2,1)S(1)}, bf16[2048,128]{1,0:T(8,128)(2,1)S(1)}) custom-call(bf16[2,2048,128]{2,1,0:T(8,128)(2,1)S(1)} %get-tuple-element.32.first_ref, bf16[6,2048,128]{2,1,0:T(8,128)(2,1)S(1)} %get-tuple-element.33.last_ref, f32[8,128]{1,0:T(8,128)S(1)} %get-tuple-element.34.s0, ...), custom_call_target="tpu_custom_call" | custom-call | tf_op jit(solution)/shard_map/rim/pallas_call | solution.py:384
  31.7 0.1 collective-permute-start.8
  31.8 2.4 %collective-permute-start.9 = (f32[4,2048]{1,0:T(4,128)S(1)}, f32[4,2048]{1,0:T(4,128)S(1)}, u32[]{:S(2)}, u32[]{:S(2)}) collective-permute-start(f32[4,2048]{1,0:T(4,128)S(1)} %get-tuple-element.40), channel_id=1, source_target_pairs={{1,2},{2,1},{5,6},{6,5},{9,10},{10,9},{13,14},{14,13},{17,18},{18,... | collective-permute-start | bytes 98312 | tf_op jit(solution)/shard_map/ppermute | solution.py:631
  34.2 0.0 copy-start.6
  34.2 0.0 copy-start.5
  34.2 2.9 %taps.1.part_ref = f32[4,8,2048]{2,1,0:T(8,128)S(1)} custom-call(bf16[2,2048,128]{2,1,0:T(8,128)(2,1)S(1)} %get-tuple-element.32.first_ref, bf16[6,2048,128]{2,1,0:T(8,128)(2,1)S(1)} %get-tuple-element.33.last_ref, bf16[2048,128]{1,0:T(8,128)(2,1)S(1)} %get-tuple-element.36.top_ref, bf16[2048,128]{1,0:T(8,128)(2,1)S(1)} %get-tuple-element.37.bottom_ref, ...), custom_call_target="tpu_custom_call" | custom-call | flops 6442450944 | bytes 4194304 | tf_op jit(solution)/shard_map/taps/pallas_call | solution.py:467
  37.1 0.0 collective-permute-done.8.core_ref
  37.1 1.4 %collective-permute-done.9.far_ref = f32[4,2048]{1,0:T(4,128)S(1)} collective-permute-done((f32[4,2048]{1,0:T(4,128)S(1)}, f32[4,2048]{1,0:T(4,128)S(1)}, u32[]{:S(2)}, u32[]{:S(2)}) %collective-permute-start.9) | collective-permute-done | bytes 32800 | tf_op jit(solution)/shard_map/ppermute | solution.py:631
  38.5 1.0 %step.1 = (f32[4,8,2048]{2,1,0:T(8,128)}, f32[16,4,8,128]{3,2,1,0:T(8,128)}, f32[16,4,8,128]{3,2,1,0:T(8,128)S(1)}) custom-call(f32[4,8,2048]{2,1,0:T(8,128)S(1)} %taps.1.part_ref, f32[4,2048]{1,0:T(4,128)S(1)} %collective-permute-done.8.core_ref, f32[4,2048]{1,0:T(4,128)S(1)} %collective-permute-done.9.far_ref, s32[1]{0:T(128)S(6)} %copy.11.index_ref), custom_call_target="tpu_custom_call" | custom-call | tf_op jit(solution)/shard_map/step/pallas_call | solution.py:507
  39.6 5.7 %all-to-all-start = ((f32[16,4,8,128]{3,2,1,0:T(8,128)}), f32[16,4,8,128]{3,2,1,0:T(8,128)S(1)}, u32[]{:S(2)}, u32[]{:S(2)}) async-start(f32[16,4,8,128]{3,2,1,0:T(8,128)} %get-tuple-element.42), calls=%async_computation | async-start | bytes 524288 | tf_op jit(solution)/shard_map/all_to_all | solution.py:657
  45.3 0.1 tile.10.reg_ref
  45.4 7.7 %all-to-all-done.got_ref = f32[16,4,8,128]{3,2,1,0:T(8,128)S(1)} async-done(((f32[16,4,8,128]{3,2,1,0:T(8,128)}), f32[16,4,8,128]{3,2,1,0:T(8,128)S(1)}, u32[]{:S(2)}, u32[]{:S(2)}) %all-to-all-start) | async-done | bytes 262176 | tf_op jit(solution)/shard_map/all_to_all | solution.py:657
  53.2 3.6 %collective-permute-start.10 = (f32[3,4,8,128]{3,2,1,0:T(8,128)S(1)}, f32[3,4,8,128]{3,2,1,0:T(8,128)S(1)}, u32[]{:S(2)}, u32[]{:S(2)}) collective-permute-start(f32[3,4,8,128]{3,2,1,0:T(8,128)S(1)} %sums.1), channel_id=1, source_target_pairs={{0,64},{4,68},{8,72},{12,76},{16,80},{20,84},{24,88},{28,92},{32,9... | collective-permute-start | bytes 147464 | tf_op jit(solution)/shard_map/ppermute | solution.py:660
  56.7 2.4 %collective-permute-done.10 = f32[3,4,8,128]{3,2,1,0:T(8,128)S(1)} collective-permute-done((f32[3,4,8,128]{3,2,1,0:T(8,128)S(1)}, f32[3,4,8,128]{3,2,1,0:T(8,128)S(1)}, u32[]{:S(2)}, u32[]{:S(2)}) %collective-permute-start.10) | collective-permute-done | bytes 49184 | tf_op jit(solution)/shard_map/ppermute | solution.py:660
  59.1 5.4 %collective-permute-start.11 = (f32[3,4,8,128]{3,2,1,0:T(8,128)S(1)}, f32[3,4,8,128]{3,2,1,0:T(8,128)S(1)}, u32[]{:S(2)}, u32[]{:S(2)}) collective-permute-start(f32[3,4,8,128]{3,2,1,0:T(8,128)S(1)} %add.3.one_ref), channel_id=1, source_target_pairs={{0,192},{4,196},{8,200},{12,204},{16,208},{20,212},{24,216},{28,22... | collective-permute-start | bytes 147464 | tf_op jit(solution)/shard_map/ppermute | solution.py:661
  64.5 2.1 %collective-permute-done.11.two_ref = f32[3,4,8,128]{3,2,1,0:T(8,128)S(1)} collective-permute-done((f32[3,4,8,128]{3,2,1,0:T(8,128)S(1)}, f32[3,4,8,128]{3,2,1,0:T(8,128)S(1)}, u32[]{:S(2)}, u32[]{:S(2)}) %collective-permute-start.11) | collective-permute-done | bytes 49184 | tf_op jit(solution)/shard_map/ppermute | solution.py:661
  66.6 0.0 copy-done.5
  66.6 0.7 spread.1
  67.3 10.9 %all_to_all.10.got_ref = s16[16,5,16,128]{3,2,1,0:T(8,128)(2,1)S(1)} all-to-all(s16[16,5,16,128]{3,2,1,0:T(8,128)(2,1)S(1)} %spread.1), channel_id=1, replica_groups={{0,4,8,12,16,20,24,28,32,36,40,44,48,52,56,60},{64,68,72,76,80,84,88,92..., dimensions={0} | all-to-all | bytes 655360 | tf_op jit(solution)/shard_map/all_to_all | solution.py:663
  78.2 1.0 %field.1 = f32[4,8,2048]{2,1,0:T(8,128)} custom-call(f32[16,4,8,128]{3,2,1,0:T(8,128)S(1)} %get-tuple-element.41.blocks_ref, s16[16,5,16,128]{3,2,1,0:T(8,128)(2,1)S(1)} %all_to_all.10.got_ref), custom_call_target="tpu_custom_call" | custom-call | tf_op jit(solution)/shard_map/field/pallas_call | solution.py:616
  (7 shorter events, 0.1 us)
Async XLA Ops:
  0.6 12.2 %copy-start.4 = (bf16[4,128]{1,0:T(4,128)(2,1)S(1)}, bf16[4,128]{1,0:T(4,128)(2,1)}, u32[]{:S(2)}) copy-start(bf16[4,128]{1,0:T(4,128)(2,1)} %head_ref.3) | copy-start | bytes 3076
  0.6 12.2 %copy-start.1 = (bf16[9,128,128]{2,1,0:T(8,128)(2,1)S(1)}, bf16[9,128,128]{2,1,0:T(8,128)(2,1)}, u32[]{:S(2)}) copy-start(bf16[9,128,128]{2,1,0:T(8,128)(2,1)} %second_ref.1) | copy-start | bytes 884740
  0.7 12.2 %copy-start = (bf16[9,128,128]{2,1,0:T(8,128)(2,1)S(1)}, bf16[9,128,128]{2,1,0:T(8,128)(2,1)}, u32[]{:S(2)}) copy-start(bf16[9,128,128]{2,1,0:T(8,128)(2,1)} %first_ref.1) | copy-start | bytes 884740
  4.8 8.3 %collective-permute-start.1 = (bf16[2048,128]{1,0:T(8,128)(2,1)S(1)}, bf16[2048,128]{1,0:T(8,128)(2,1)S(1)}, u32[]{:S(2)}, u32[]{:S(2)}) collective-permute-start(bf16[2048,128]{1,0:T(8,128)(2,1)S(1)} %get-tuple-element.25), channel_id=1, source_target_pairs={{0,1},{1,0},{2,3},{3,2},{4,5},{5,4},{6,7},{7,6},{8,9},{9,8},{10,11... | collective-permute-start | bytes 1572872 | tf_op jit(solution)/shard_map/ppermute | solution.py:627
  4.9 8.2 %collective-permute-start.4 = (f32[8,128]{1,0:T(8,128)S(1)}, f32[8,128]{1,0:T(8,128)S(1)}, u32[]{:S(2)}, u32[]{:S(2)}) collective-permute-start(f32[8,128]{1,0:T(8,128)S(1)} %get-tuple-element.26.s0), channel_id=1, source_target_pairs={{0,3},{1,2},{2,1},{3,0},{4,7},{5,6},{6,5},{7,4},{8,11},{9,10},{10,... | collective-permute-start | bytes 12296 | tf_op jit(solution)/shard_map/ppermute | solution.py:627
  7.3 5.8 %collective-permute-start.3 = (f32[8,128]{1,0:T(8,128)S(1)}, f32[8,128]{1,0:T(8,128)S(1)}, u32[]{:S(2)}, u32[]{:S(2)}) collective-permute-start(f32[8,128]{1,0:T(8,128)S(1)} %get-tuple-element.26.s0), channel_id=1, source_target_pairs={{0,2},{1,3},{2,0},{3,1},{4,6},{5,7},{6,4},{7,5},{8,10},{9,11},{10,... | collective-permute-start | bytes 12296 | tf_op jit(solution)/shard_map/ppermute | solution.py:627
  8.6 4.5 %collective-permute-start.2 = (f32[8,128]{1,0:T(8,128)S(1)}, f32[8,128]{1,0:T(8,128)S(1)}, u32[]{:S(2)}, u32[]{:S(2)}) collective-permute-start(f32[8,128]{1,0:T(8,128)S(1)} %get-tuple-element.26.s0), channel_id=1, source_target_pairs={{0,1},{1,0},{2,3},{3,2},{4,5},{5,4},{6,7},{7,6},{8,9},{9,8},{10,11... | collective-permute-start | bytes 12296 | tf_op jit(solution)/shard_map/ppermute | solution.py:627
  8.6 12.0 %collective-permute-start = (bf16[2048,128]{1,0:T(8,128)(2,1)S(1)}, bf16[2048,128]{1,0:T(8,128)(2,1)S(1)}, u32[]{:S(2)}, u32[]{:S(2)}) collective-permute-start(bf16[2048,128]{1,0:T(8,128)(2,1)S(1)} %get-tuple-element.23), channel_id=1, source_target_pairs={{1,2},{2,1},{5,6},{6,5},{9,10},{10,9},{13,14},{14,13},{17,18},{18,... | collective-permute-start | bytes 1572872 | tf_op jit(solution)/shard_map/ppermute | solution.py:631
  20.0 7.0 %copy-start.2 = (f32[1,4,8,2048]{3,2,1,0:T(8,128)S(1)}, f32[1,4,8,2048]{3,2,1,0:T(8,128)}, u32[]{:S(2)}) copy-start(f32[1,4,8,2048]{3,2,1,0:T(8,128)} %param.10) | copy-start | bytes 786436
  20.0 7.0 %copy-start.3 = (f32[1,4,8,2048]{3,2,1,0:T(8,128)S(1)}, f32[1,4,8,2048]{3,2,1,0:T(8,128)}, u32[]{:S(2)}) copy-start(f32[1,4,8,2048]{3,2,1,0:T(8,128)} %param.11) | copy-start | bytes 786436
  22.9 5.4 %collective-permute-start.7 = (f32[8,128]{1,0:T(8,128)S(1)}, f32[8,128]{1,0:T(8,128)S(1)}, u32[]{:S(2)}, u32[]{:S(2)}) collective-permute-start(f32[8,128]{1,0:T(8,128)S(1)} %get-tuple-element.34.s0), channel_id=1, source_target_pairs={{0,3},{1,2},{2,1},{3,0},{4,7},{5,6},{6,5},{7,4},{8,11},{9,10},{10,... | collective-permute-start | bytes 12296 | tf_op jit(solution)/shard_map/ppermute | solution.py:627
  25.3 5.1 %collective-permute-start.6 = (f32[8,128]{1,0:T(8,128)S(1)}, f32[8,128]{1,0:T(8,128)S(1)}, u32[]{:S(2)}, u32[]{:S(2)}) collective-permute-start(f32[8,128]{1,0:T(8,128)S(1)} %get-tuple-element.34.s0), channel_id=1, source_target_pairs={{0,2},{1,3},{2,0},{3,1},{4,6},{5,7},{6,4},{7,5},{8,10},{9,11},{10,... | collective-permute-start | bytes 12296 | tf_op jit(solution)/shard_map/ppermute | solution.py:627
  25.3 5.1 %collective-permute-start.5 = (f32[8,128]{1,0:T(8,128)S(1)}, f32[8,128]{1,0:T(8,128)S(1)}, u32[]{:S(2)}, u32[]{:S(2)}) collective-permute-start(f32[8,128]{1,0:T(8,128)S(1)} %get-tuple-element.34.s0), channel_id=1, source_target_pairs={{0,1},{1,0},{2,3},{3,2},{4,5},{5,4},{6,7},{7,6},{8,9},{9,8},{10,11... | collective-permute-start | bytes 12296 | tf_op jit(solution)/shard_map/ppermute | solution.py:627
  31.7 5.4 %collective-permute-start.8 = (f32[4,2048]{1,0:T(4,128)S(1)}, f32[4,2048]{1,0:T(4,128)S(1)}, u32[]{:S(2)}, u32[]{:S(2)}) collective-permute-start(f32[4,2048]{1,0:T(4,128)S(1)} %get-tuple-element.39), channel_id=1, source_target_pairs={{0,1},{1,0},{2,3},{3,2},{4,5},{5,4},{6,7},{7,6},{8,9},{9,8},{10,11... | collective-permute-start | bytes 98312 | tf_op jit(solution)/shard_map/ppermute | solution.py:627
  31.8 6.7 %collective-permute-start.9 = (f32[4,2048]{1,0:T(4,128)S(1)}, f32[4,2048]{1,0:T(4,128)S(1)}, u32[]{:S(2)}, u32[]{:S(2)}) collective-permute-start(f32[4,2048]{1,0:T(4,128)S(1)} %get-tuple-element.40), channel_id=1, source_target_pairs={{1,2},{2,1},{5,6},{6,5},{9,10},{10,9},{13,14},{14,13},{17,18},{18,... | collective-permute-start | bytes 98312 | tf_op jit(solution)/shard_map/ppermute | solution.py:631
  34.2 11.1 %copy-start.6 = (f32[4,8,32]{2,1,0:T(8,128)S(1)}, f32[4,8,32]{2,1,0:T(8,128)}, u32[]{:S(2)}) copy-start(f32[4,8,32]{2,1,0:T(8,128)} %param.12) | copy-start | bytes 12292
  34.2 32.4 %copy-start.5 = (f32[4]{0:T(128)S(1)}, f32[4]{0:T(128)}, u32[]{:S(2)}) copy-start(f32[4]{0:T(128)} %target_ref.1) | copy-start | bytes 52
  39.6 13.6 %all-to-all-start = ((f32[16,4,8,128]{3,2,1,0:T(8,128)}), f32[16,4,8,128]{3,2,1,0:T(8,128)S(1)}, u32[]{:S(2)}, u32[]{:S(2)}) async-start(f32[16,4,8,128]{3,2,1,0:T(8,128)} %get-tuple-element.42), calls=%async_computation | async-start | bytes 524288 | tf_op jit(solution)/shard_map/all_to_all | solution.py:657
  53.2 6.0 %collective-permute-start.10 = (f32[3,4,8,128]{3,2,1,0:T(8,128)S(1)}, f32[3,4,8,128]{3,2,1,0:T(8,128)S(1)}, u32[]{:S(2)}, u32[]{:S(2)}) collective-permute-start(f32[3,4,8,128]{3,2,1,0:T(8,128)S(1)} %sums.1), channel_id=1, source_target_pairs={{0,64},{4,68},{8,72},{12,76},{16,80},{20,84},{24,88},{28,92},{32,9... | collective-permute-start | bytes 147464 | tf_op jit(solution)/shard_map/ppermute | solution.py:660
  59.1 7.4 %collective-permute-start.11 = (f32[3,4,8,128]{3,2,1,0:T(8,128)S(1)}, f32[3,4,8,128]{3,2,1,0:T(8,128)S(1)}, u32[]{:S(2)}, u32[]{:S(2)}) collective-permute-start(f32[3,4,8,128]{3,2,1,0:T(8,128)S(1)} %add.3.one_ref), channel_id=1, source_target_pairs={{0,192},{4,196},{8,200},{12,204},{16,208},{20,212},{24,216},{28,22... | collective-permute-start | bytes 147464 | tf_op jit(solution)/shard_map/ppermute | solution.py:661
